TPU v7x, 256 devices: a whole 4x4x8 slice. The times are simulated.
256 devices in a mesh: batch: 16 (over y_lo, x, core), patch: 8 (over z), cfg: 2 (over y_hi).
Axes of the slice: x: 4, y: 4 (y_hi: 2, y_lo: 2; y = y_hi * 2 + y_lo), z: 8, core: 2. Of those that a mesh axis runs over, the one named last changes fastest.
Arguments:
- latent: float32 [128, 128, 640], P(('batch', 'patch')), parts along dimension 0, may hold values from -80 to 80
- stale_conv: bfloat16 [2, 128, 128, 640], P('cfg', ('batch', 'patch')), parts along dimension 1, may hold values from -6 to 6
- stale_attn: bfloat16 [2, 128, 128, 640], P('cfg', ('batch', 'patch')), parts along dimension 1, may hold values from -6 to 6
- cond_embed: float32 [32, 640], P(('batch', 'cfg')), parts along dimension 0, may hold values from -3 to 3
- timesteps: int32 [3], replicated, may hold values from 579 to 699, as said below
- gn_gain: float32 [640], replicated, may hold values from 0.25 to 1.75
- ln_gain: float32 [640], replicated, may hold values from 0.25 to 1.75
- time_scale: float32 [640], replicated, may hold values from -4 to 4
- conv_weight: bfloat16 [3, 3, 640, 640], replicated, may hold values from -0.078125 to 0.078125
- q_weight: bfloat16 [640, 640], replicated, may hold values from -1 to 1
- kv_weight: bfloat16 [640, 1280], replicated, may hold values from -1 to 1
- out_weight: bfloat16 [640, 640], replicated, may hold values from -0.25 to 0.25
Outputs:
- final_latent: float32 [128, 128, 640], P(('batch', 'patch')), parts along dimension 0
- final_guided: float32 [128, 128, 640], P(('batch', 'patch')), parts along dimension 0
There are 16 independent parts, one for each index of `batch`. A program takes and returns all parts, laid end to end along the dimension named above; an argument that names none is the same for every part. Nothing has to cross between parts.
Inputs may be any that keep to these rules, and one draw needn't show every extreme that they name: `timesteps`: strictly falling; the first entry is 699 and the last is 579.
All inputs are finite; a program needn't handle non-finite values.
Results may differ from a plain program's by a relative error of at most 0.033.
Values may be sent and summed in bfloat16 or wider, within the bound.
No kernel may reach another device: no remote copies, remote signals or barrier semaphores. Data moves between devices by JAX's collectives and lax.ppermute only.
A program may use at most 128 MiB of HBM per device.

v0:
```python
import math

import jax
import jax.numpy as jnp
from jax import lax
from jax.sharding import PartitionSpec as P

HEADS = 10
GROUPS = 32
STEPS = 2


def padded_2(block, sides, width):
    for axis, dim in sides:
        count = lax.axis_size(axis)
        forward = [(i, i + 1) for i in range(count - 1)]
        backward = [(target, source) for source, target in forward]
        low = lax.ppermute(
            lax.slice_in_dim(block, block.shape[dim] - width, None, axis=dim), axis, forward
        )
        high = lax.ppermute(lax.slice_in_dim(block, 0, width, axis=dim), axis, backward)
        block = jnp.concatenate([low, block, high], axis=dim)
    return block


def from_partner(x, axis, distance):
    return lax.ppermute(x, axis, [(i, i ^ 1 << distance) for i in range(lax.axis_size(axis))])


def alpha_bars():
    betas = jnp.linspace(0.00085**0.5, 0.012**0.5, 1000, dtype=jnp.float32) ** 2
    return jnp.cumprod(1.0 - betas)


def table_pick(table, index):
    places = jnp.arange(table.shape[0], dtype=jnp.int32)
    return jnp.sum(jnp.where(places == index, table, jnp.zeros_like(table)))


def sinusoid(step_value, width):
    half = width // 2
    freqs = jnp.exp(-math.log(10000.0) * jnp.arange(half, dtype=jnp.float32) / half)
    angles = step_value.astype(jnp.float32) * freqs
    return jnp.concatenate([jnp.cos(angles), jnp.sin(angles)])


def update_coeffs(t_now, t_next):
    table = alpha_bars()
    now = table_pick(table, t_now)
    after = table_pick(table, t_next)
    keep = jnp.sqrt(after / now)
    blend = jnp.sqrt(1.0 - after) - jnp.sqrt(after) * jnp.sqrt(1.0 - now) / jnp.sqrt(now)
    return (keep, blend)


def group_silu(field, gain):
    rows_dev, cols, width = field.shape
    grouped = field.reshape(rows_dev * cols, GROUPS, width // GROUPS)
    count = rows_dev * cols * (width // GROUPS) * lax.axis_size("patch")
    total = lax.psum(jnp.sum(grouped, axis=(0, 2)), "patch")
    mean = total / count
    centered = grouped - mean[None, :, None]
    var = lax.psum(jnp.sum(centered * centered, axis=(0, 2)), "patch") / count
    normed = (centered / jnp.sqrt(var + 1e-05)[None, :, None]).reshape(rows_dev, cols, width) * gain
    return jax.nn.silu(normed).astype(jnp.bfloat16)


def layer_norm(field, gain):
    mean = jnp.mean(field, axis=-1, keepdims=True)
    centered = field - mean
    var = jnp.mean(centered * centered, axis=-1, keepdims=True)
    return (centered / jnp.sqrt(var + 1e-05) * gain).astype(jnp.bfloat16)


def convolve(fresh, stale, weight):
    rows_dev, cols, width = fresh.shape
    rims = padded_2(stale, (("patch", 0),), 1)
    extended = jnp.concatenate([rims[:1], fresh, rims[-1:]], axis=0)
    padded = jnp.pad(extended, ((0, 0), (1, 1), (0, 0)))
    widened = jnp.concatenate(
        [padded[:, 0:cols], padded[:, 1 : cols + 1], padded[:, 2 : cols + 2]], axis=-1
    )
    taps = weight.reshape(3, 3 * width, width)
    total = jnp.zeros((rows_dev * cols, width), jnp.float32)
    for tap_row in range(3):
        window = widened[tap_row : tap_row + rows_dev].reshape(-1, 3 * width)
        total = total + jnp.dot(window, taps[tap_row], preferred_element_type=jnp.float32)
    return total.reshape(rows_dev, cols, width)


def accumulate(carry, query, keys_values, masked):
    running_max, running_sum, running_acc = carry
    heads, head_dim = (query.shape[1], query.shape[2])
    width = heads * head_dim
    keys = keys_values[:, :width].reshape(-1, heads, head_dim)
    values = keys_values[:, width:].reshape(-1, heads, head_dim)
    scores = jnp.einsum(
        "qhd,khd->hqk", query, keys, preferred_element_type=jnp.float32
    ) * head_dim ** (-0.5)
    if masked is not None:
        scores = jnp.where(masked[None, None, :], -1e30, scores)
    new_max = jnp.maximum(running_max, jnp.max(scores, axis=-1))
    factor = jnp.exp(running_max - new_max)
    weights = jnp.exp(scores - new_max[:, :, None])
    new_sum = running_sum * factor + jnp.sum(weights, axis=-1)
    product = jnp.einsum(
        "hqk,khd->qhd", weights.astype(jnp.bfloat16), values, preferred_element_type=jnp.float32
    )
    new_acc = running_acc * jnp.transpose(factor)[:, :, None] + product
    return (new_max, new_sum, new_acc)


def shards(
    latent,
    stale_conv,
    stale_attn,
    cond_embed,
    timesteps,
    gn_gain,
    ln_gain,
    time_scale,
    conv_weight,
    q_weight,
    kv_weight,
    out_weight,
):
    rows_dev, cols, width = latent.shape
    tokens = rows_dev * cols
    branch = lax.axis_index("cfg")
    own_start = lax.axis_index("patch") * rows_dev
    state = latent
    guided = jnp.zeros_like(latent)
    prev_conv = stale_conv[0]
    prev_attn = stale_attn[0]
    prev_keys = (
        jnp.dot(prev_attn.reshape(-1, width), kv_weight, preferred_element_type=jnp.float32)
        .astype(jnp.bfloat16)
        .reshape(rows_dev, cols, 2 * width)
    )
    for step in range(STEPS):
        conv_in = group_silu(state, gn_gain)
        temb = jax.nn.silu(time_scale * sinusoid(timesteps[step], width) + cond_embed[0])
        hidden = state + convolve(conv_in, prev_conv, conv_weight) + temb
        attn_in = layer_norm(hidden, ln_gain)
        flat = attn_in.reshape(-1, width)
        query = (
            jnp.dot(flat, q_weight, preferred_element_type=jnp.float32)
            .astype(jnp.bfloat16)
            .reshape(tokens, HEADS, width // HEADS)
        )
        fresh_kv = jnp.dot(flat, kv_weight, preferred_element_type=jnp.float32).astype(jnp.bfloat16)
        start_carry = (
            jnp.full((HEADS, tokens), -1e30, jnp.float32),
            jnp.zeros((HEADS, tokens), jnp.float32),
            jnp.zeros((tokens, HEADS, width // HEADS), jnp.float32),
        )
        own_carry = accumulate(start_carry, query, fresh_kv, None)
        piece = lax.all_gather(prev_keys, "patch", axis=0, tiled=True)
        piece_rows = piece.shape[0]
        places = jnp.arange(piece_rows, dtype=jnp.int32)
        owned = (places >= own_start) & (places < own_start + rows_dev)
        result = accumulate(
            own_carry,
            query,
            piece.reshape(-1, 2 * width),
            jnp.broadcast_to(owned[:, None], (piece_rows, cols)).reshape(-1),
        )
        final_sum, final_acc = (result[1], result[2])
        mixed = (
            (final_acc / jnp.transpose(final_sum)[:, :, None])
            .astype(jnp.bfloat16)
            .reshape(tokens, width)
        )
        prediction = hidden + jnp.dot(
            mixed, out_weight, preferred_element_type=jnp.float32
        ).reshape(rows_dev, cols, width)
        partner = from_partner(prediction, "cfg", 0)
        uncond = jnp.where(branch == 0, prediction, partner)
        cond = jnp.where(branch == 0, partner, prediction)
        guided = uncond + 3.0 * (cond - uncond)
        keep, blend = update_coeffs(timesteps[step], timesteps[step + 1])
        state = keep * state + blend * guided
        prev_conv = conv_in
        prev_attn = attn_in
        prev_keys = fresh_kv.reshape(rows_dev, cols, 2 * width)
    return (state, guided)


def solution(mesh):
    placed = (
        P(("batch", "patch"), None, None),
        P("cfg", ("batch", "patch"), None, None),
        P("cfg", ("batch", "patch"), None, None),
        P(("batch", "cfg"), None),
        P(),
        P(),
        P(),
        P(),
        P(),
        P(),
        P(),
        P(),
    )
    return jax.shard_map(
        shards,
        mesh=mesh,
        in_specs=placed,
        out_specs=(P(("batch", "patch"), None, None), P(("batch", "patch"), None, None)),
        check_vma=False,
    )
```

profile of v0, /device:TPU:2, one launch (start us, length us, event | category | flops | bytes accessed | tf_op | source)
XLA Modules:
  0.0 183.4 jit_solution(4504894027723827225)
XLA Ops:
  7.3 1.3 copy-done
  8.6 2.1 %convolution_convert_fusion.1 = bf16[128,1280]{1,0:T(8,128)(2,1)} fusion(bf16[640,1280]{1,0:T(8,128)(2,1)S(1)} %copy-done, bf16[1,1,128,640]{3,2,1,0:T(8,128)(2,1)} %param.16), kind=kOutput, calls=%fused_computation.15 | convolution fusion | flops 209879040 | bytes 2129920 | tf_op jit(solution)/shard_map/dot_general | solution.py:136
  10.8 1.3 collective-permute-start.1
  12.1 4.6 %collective-permute-start = (bf16[1,128,640]{2,1,0:T(8,128)(2,1)S(1)}, bf16[1,128,640]{2,1,0:T(8,128)(2,1)S(1)}, u32[]{:S(2)}, u32[]{:S(2)}) collective-permute-start(bf16[1,128,640]{2,1,0:T(8,128)(2,1)S(1)} %bitcast.199), channel_id=1, source_target_pairs={{0,2},{2,4},{4,6},{6,8},{8,10},{10,12},{12,14},{1,3},{3,5},{5,7},{... | collective-permute-start | bytes 491528 | tf_op jit(solution)/shard_map/ppermute | solution.py:18
  16.9 18.8 %psum.28 = f32[32]{0:T(128)S(1)} all-reduce(f32[32]{0:T(128)S(1)} %reduce_sum.180), channel_id=1, replica_groups=mesh['batch'=16,'patch'=8,'cfg'=2] {'patch'}, use_global_device_ids=true, to_apply=%region_7.9 | all-reduce | flops 32 | bytes 256 | tf_op jit(solution)/shard_map/psum | solution.py:60
  36.1 15.3 %psum.29 = f32[32]{0:T(128)S(1)} all-reduce(f32[32]{0:T(128)S(1)} %reduce_sum.183), channel_id=1, replica_groups=mesh['batch'=16,'patch'=8,'cfg'=2] {'patch'}, use_global_device_ids=true, to_apply=%region_10.12 | all-reduce | flops 32 | bytes 256 | tf_op jit(solution)/shard_map/psum | solution.py:63
  51.7 1.3 collective-permute-start.4
  53.0 5.2 %collective-permute-start.3 = (bf16[1,128,640]{2,1,0:T(8,128)(2,1)S(1)}, bf16[1,128,640]{2,1,0:T(8,128)(2,1)}, u32[]{:S(2)}, u32[]{:S(2)}) collective-permute-start(bf16[1,128,640]{2,1,0:T(8,128)(2,1)S(1)} %multiply_convert_fusion.3), channel_id=1, source_target_pairs={{0,2},{2,4},{4,6},{6,8},{8,10},{10,12},{12,14},{1,3},{3,5},{5,7},{... | collective-permute-start | bytes 491528 | tf_op jit(solution)/shard_map/ppermute | solution.py:18
  58.2 0.6 fusion.90
  60.2 3.8 %fusion.83 = (bf16[1,3,640,640]{3,2,1,0:T(8,128)(2,1)S(1)}, bf16[1,3,640,640]{3,2,1,0:T(8,128)(2,1)S(1)}, bf16[1,3,640,640]{3,2,1,0:T(8,128)(2,1)S(1)}) fusion(bf16[3,3,640,640]{3,2,1,0:T(8,128)(2,1)} %param.22), kind=kLoop, calls=%fused_computation.153 | loop fusion | bytes 14745600 | tf_op jit(solution)/shard_map/slice | solution.py:87
  64.6 0.6 fusion.46
  65.5 0.6 fusion.47
  66.2 0.7 fusion.91
  67.2 1.2 convolution_convert_fusion.2
  69.2 1.5 convolution_convert_fusion.4
  71.1 0.8 copy.30
  71.9 1.2 fusion.92
  73.1 3.1 %fusion.85 = (bf16[1024,640]{1,0:T(8,128)(2,1)S(1)}, bf16[1024,640]{1,0:T(8,128)(2,1)}) fusion(bf16[1024,1280]{1,0:T(8,128)(2,1)} %all-gather.5.cloned.1.call-done), kind=kLoop, calls=%fused_computation.155 | loop fusion | bytes 5242880 | tf_op jit(solution)/shard_map/slice | solution.py:95
  76.2 2.5 %copy.33 = bf16[1024,640]{0,1:T(8,128)(2,1)} copy(bf16[1024,640]{1,0:T(8,128)(2,1)} %get-tuple-element.20) | data formatting | bytes 2621440 | tf_op jit(solution)/shard_map/slice | solution.py:96
  78.6 1.5 copy.32
  80.2 2.4 %fusion = (f32[10,128]{1,0:T(8,128)S(1)}, f32[10,128,1024]{2,1,0:T(8,128)S(1)}) fusion(pred[1024]{0:T(1024)(128)(4,1)S(1)} %broadcast_bitcast_fusion, bf16[128,10,64]{0,2,1:T(8,128)(2,1)} %bitcast.187, bf16[1024,10,64]{0,2,1:T(8,128)(2,1)} %bitcast.185), kind=kOutput, calls=%fused_computation.4 | convolution fusion | flops 171703040 | bytes 6723584 | tf_op jit(solution)/shard_map/qhd,khd->hqk/dot_general | solution.py:97
  82.8 1.2 fusion.2
  84.1 1.3 fusion.20
  85.6 1.1 fusion.30
  86.7 3.2 %collective-permute-start.2 = (f32[1,128,640]{2,1,0:T(8,128)}, f32[1,128,640]{2,1,0:T(8,128)}, u32[]{:S(2)}, u32[]{:S(2)}) collective-permute-start(f32[1,128,640]{2,1,0:T(8,128)} %fusion.30), channel_id=1, source_target_pairs={{0,1},{1,0},{2,3},{3,2},{4,5},{5,4},{6,7},{7,6},{8,9},{9,8},{10,11... | collective-permute-start | bytes 983048 | tf_op jit(solution)/shard_map/ppermute | solution.py:27
  89.9 2.4 %select_reduce_fusion.2 = (f32[]{:T(128)}, f32[]{:T(128)}, f32[]{:T(128)}) fusion(f32[1024]{0:T(1024)S(1)} %multiply_bitcast_fusion, s32[]{:T(128)} %bitcast, s32[]{:T(128)} %bitcast.4, s32[]{:T(128)} %bitcast.5), kind=kLoop, calls=%fused_computation.125 | loop fusion | flops 8997 | bytes 4024 | tf_op jit(solution)/shard_map/reduce_sum | solution.py:37
  96.2 13.5 %all-gather.7.cloned.1.call-done = bf16[1024,1280]{1,0:T(8,128)(2,1)} async-done(((bf16[128,1280]{1,0:T(8,128)(2,1)}), bf16[1024,1280]{1,0:T(8,128)(2,1)}) %all-gather.7.cloned.1.call-update) | async-done | bytes 2621456 | tf_op jit(solution)/shard_map/all_gather | solution.py:158
  109.7 3.0 %fusion.84 = (bf16[1024,640]{1,0:T(8,128)(2,1)S(1)}, bf16[1024,640]{1,0:T(8,128)(2,1)}) fusion(bf16[1024,1280]{1,0:T(8,128)(2,1)} %all-gather.7.cloned.1.call-done), kind=kLoop, calls=%fused_computation.154 | loop fusion | bytes 5242880 | tf_op jit(solution)/shard_map/slice | solution.py:95
  112.7 2.5 %copy.39 = bf16[1024,640]{0,1:T(8,128)(2,1)} copy(bf16[1024,640]{1,0:T(8,128)(2,1)} %get-tuple-element.18) | data formatting | bytes 2621440 | tf_op jit(solution)/shard_map/slice | solution.py:96
  115.2 1.6 copy.38
  116.8 1.2 fusion.81
  118.2 16.1 %psum.30 = f32[32]{0:T(128)S(1)} all-reduce(f32[32]{0:T(128)S(1)} %reduce_sum.192), channel_id=1, replica_groups=mesh['batch'=16,'patch'=8,'cfg'=2] {'patch'}, use_global_device_ids=true, to_apply=%region_19.21 | all-reduce | flops 32 | bytes 256 | tf_op jit(solution)/shard_map/psum | solution.py:60
  134.7 14.2 %psum.31 = f32[32]{0:T(128)S(1)} all-reduce(f32[32]{0:T(128)S(1)} %reduce_sum.195), channel_id=1, replica_groups=mesh['batch'=16,'patch'=8,'cfg'=2] {'patch'}, use_global_device_ids=true, to_apply=%region_22.24 | all-reduce | flops 32 | bytes 256 | tf_op jit(solution)/shard_map/psum | solution.py:63
  149.3 1.1 select_maximum_fusion
  150.6 1.3 pad_maximum_fusion.1
  152.3 0.6 fusion.44
  153.1 0.6 fusion.45
  153.7 1.1 copy-done.2
  154.8 0.7 fusion.93
  156.9 2.3 %fusion.1 = (f32[10,128]{1,0:T(8,128)S(1)}, f32[10,128,1024]{2,1,0:T(8,128)S(1)}) fusion(pred[1024]{0:T(1024)(128)(4,1)S(1)} %broadcast_bitcast_fusion, bf16[128,10,64]{0,2,1:T(8,128)(2,1)S(1)} %bitcast.188, bf16[1024,10,64]{0,2,1:T(8,128)(2,1)} %bitcast.184), kind=kOutput, calls=%fused_computation.5 | convolution fusion | flops 171703040 | bytes 6723584 | tf_op jit(solution)/shard_map/qhd,khd->hqk/dot_general | solution.py:97
  159.2 1.2 fusion.94
  160.4 1.2 fusion.4
  161.7 2.0 %fusion.23 = f32[128,10,64]{0,2,1:T(8,128)} fusion(bf16[1024,10,64]{0,2,1:T(8,128)(2,1)S(1)} %bitcast.190, f32[10,128,1024]{2,1,0:T(8,128)S(1)} %get-tuple-element.51, f32[10,128]{1,0:T(8,128)S(1)} %get-tuple-element.31, pred[1024]{0:T(1024)(128)(4,1)S(1)} %broadcast_bitcast_fusion), kind=kOutput, calls=%fused_computation.36 | convolution fusion | flops 173015040 | bytes 6887424 | tf_op jit(solution)/shard_map/hqk,khd->qhd/dot_general | solution.py:106
  163.9 1.3 fusion.41
  165.2 1.4 fusion.36
  167.0 3.2 %collective-permute-start.5 = (f32[1,128,640]{2,1,0:T(8,128)S(1)}, f32[1,128,640]{2,1,0:T(8,128)S(1)}, u32[]{:S(2)}, u32[]{:S(2)}) collective-permute-start(f32[1,128,640]{2,1,0:T(8,128)S(1)} %fusion.31), channel_id=1, source_target_pairs={{0,1},{1,0},{2,3},{3,2},{4,5},{5,4},{6,7},{7,6},{8,9},{9,8},{10,11... | collective-permute-start | bytes 983048 | tf_op jit(solution)/shard_map/ppermute | solution.py:27
  172.9 2.7 %collective-permute-done.5 = f32[1,128,640]{2,1,0:T(8,128)S(1)} collective-permute-done((f32[1,128,640]{2,1,0:T(8,128)S(1)}, f32[1,128,640]{2,1,0:T(8,128)S(1)}, u32[]{:S(2)}, u32[]{:S(2)}) %collective-permute-start.5) | collective-permute-done | bytes 327712 | tf_op jit(solution)/shard_map/ppermute | solution.py:27
  175.6 0.9 multiply_add_fusion
  (123 shorter events, 7.8 us)
Async XLA Ops:
  7.2 1.4 copy-start
  7.2 3.6 %copy-start.23 = (bf16[1,1,128,640]{3,2,1,0:T(8,128)(2,1)S(1)}, bf16[1,1,128,640]{3,2,1,0:T(8,128)(2,1)}, u32[]{:S(2)}) copy-start(bf16[1,1,128,640]{3,2,1,0:T(8,128)(2,1)} %param.15) | copy-start | bytes 491524
  7.2 9.4 %copy-start.7 = (f32[1,128,640]{2,1,0:T(8,128)S(1)}, f32[1,128,640]{2,1,0:T(8,128)}, u32[]{:S(2)}) copy-start(f32[1,128,640]{2,1,0:T(8,128)} %param.14) | copy-start | bytes 983044
  7.2 44.4 %copy-start.18 = (f32[640]{0:T(1024)S(1)}, f32[640]{0:T(1024)}, u32[]{:S(2)}) copy-start(f32[640]{0:T(1024)} %param.19) | copy-start | bytes 7684
  7.2 51.0 %copy-start.19 = (s32[3]{0:T(128)S(1)}, s32[3]{0:T(128)}, u32[]{:S(2)}) copy-start(s32[3]{0:T(128)} %param.18) | copy-start | bytes 40
  7.2 52.8 %copy-start.21 = (f32[1,640]{1,0:T(1,128)S(1)}, f32[1,640]{1,0:T(1,128)}, u32[]{:S(2)}) copy-start(f32[1,640]{1,0:T(1,128)} %param.17) | copy-start | bytes 7684
  7.2 65.9 %all-gather.5.cloned.1.call-start = ((), (), s32[]{:S(2)}) async-start(), calls=%async_computation | async-start | bytes 2949120 | tf_op jit(solution)/shard_map/all_gather | solution.py:158
  10.7 99.0 %all-gather.7.cloned.1.call-start = ((), (), s32[]{:S(2)}) async-start(), calls=%async_computation.1 | async-start | bytes 2949120 | tf_op jit(solution)/shard_map/all_gather | solution.py:158
  10.8 53.4 %collective-permute-start.1 = (bf16[1,128,640]{2,1,0:T(8,128)(2,1)S(1)}, bf16[1,128,640]{2,1,0:T(8,128)(2,1)S(1)}, u32[]{:S(2)}, u32[]{:S(2)}) collective-permute-start(bf16[1,128,640]{2,1,0:T(8,128)(2,1)S(1)} %bitcast.198), channel_id=1, source_target_pairs={{2,0},{4,2},{6,4},{8,6},{10,8},{12,10},{14,12},{3,1},{5,3},{7,5},{... | collective-permute-start | bytes 491528 | tf_op jit(solution)/shard_map/ppermute | solution.py:21
  12.1 52.1 %collective-permute-start = (bf16[1,128,640]{2,1,0:T(8,128)(2,1)S(1)}, bf16[1,128,640]{2,1,0:T(8,128)(2,1)S(1)}, u32[]{:S(2)}, u32[]{:S(2)}) collective-permute-start(bf16[1,128,640]{2,1,0:T(8,128)(2,1)S(1)} %bitcast.199), channel_id=1, source_target_pairs={{0,2},{2,4},{4,6},{6,8},{8,10},{10,12},{12,14},{1,3},{3,5},{5,7},{... | collective-permute-start | bytes 491528 | tf_op jit(solution)/shard_map/ppermute | solution.py:18
  51.7 97.6 %collective-permute-start.4 = (bf16[1,128,640]{2,1,0:T(8,128)(2,1)S(1)}, bf16[1,128,640]{2,1,0:T(8,128)(2,1)}, u32[]{:S(2)}, u32[]{:S(2)}) collective-permute-start(bf16[1,128,640]{2,1,0:T(8,128)(2,1)S(1)} %multiply_convert_fusion.3), channel_id=1, source_target_pairs={{2,0},{4,2},{6,4},{8,6},{10,8},{12,10},{14,12},{3,1},{5,3},{7,5},{... | collective-permute-start | bytes 491528 | tf_op jit(solution)/shard_map/ppermute | solution.py:21
  53.0 96.3 %collective-permute-start.3 = (bf16[1,128,640]{2,1,0:T(8,128)(2,1)S(1)}, bf16[1,128,640]{2,1,0:T(8,128)(2,1)}, u32[]{:S(2)}, u32[]{:S(2)}) collective-permute-start(bf16[1,128,640]{2,1,0:T(8,128)(2,1)S(1)} %multiply_convert_fusion.3), channel_id=1, source_target_pairs={{0,2},{2,4},{4,6},{6,8},{8,10},{10,12},{12,14},{1,3},{3,5},{5,7},{... | collective-permute-start | bytes 491528 | tf_op jit(solution)/shard_map/ppermute | solution.py:18
  60.2 3.9 %copy-start.20 = (f32[640]{0:T(1024)S(1)}, f32[640]{0:T(1024)}, u32[]{:S(2)}) copy-start(f32[640]{0:T(1024)} %param.21) | copy-start | bytes 7684
  64.0 1.5 copy-start.3
  64.0 2.2 %copy-start.1 = (bf16[1,3,640,640]{3,2,1,0:T(8,128)(2,1)}, bf16[1,3,640,640]{3,2,1,0:T(8,128)(2,1)S(1)}, u32[]{:S(2)}) copy-start(bf16[1,3,640,640]{3,2,1,0:T(8,128)(2,1)S(1)} %get-tuple-element.14) | copy-start | bytes 7372804
  64.0 3.0 %copy-start.5 = (bf16[1,3,640,640]{3,2,1,0:T(8,128)(2,1)}, bf16[1,3,640,640]{3,2,1,0:T(8,128)(2,1)S(1)}, u32[]{:S(2)}) copy-start(bf16[1,3,640,640]{3,2,1,0:T(8,128)(2,1)S(1)} %get-tuple-element.15) | copy-start | bytes 7372804
  66.1 1.1 copy-start.24
  67.0 3.7 %copy-start.10 = (f32[1,128,640]{2,1,0:T(8,128)}, f32[1,128,640]{2,1,0:T(8,128)S(1)}, u32[]{:S(2)}) copy-start(f32[1,128,640]{2,1,0:T(8,128)S(1)} %get-tuple-element.41) | copy-start | bytes 983044
  68.4 2.5 %copy-start.16 = (bf16[128,1280]{1,0:T(8,128)(2,1)S(1)}, bf16[128,1280]{1,0:T(8,128)(2,1)}, u32[]{:S(2)}) copy-start(bf16[128,1280]{1,0:T(8,128)(2,1)} %convolution_convert_fusion.2) | copy-start | bytes 983044
  70.9 2.2 %copy-start.13 = (bf16[128,640]{0,1:T(8,128)(2,1)}, bf16[128,640]{0,1:T(8,128)(2,1)S(1)}, u32[]{:S(2)}) copy-start(bf16[128,640]{0,1:T(8,128)(2,1)S(1)} %copy.28) | copy-start | bytes 491524
  80.2 2.5 %copy-start.12 = (f32[10,128,128]{1,2,0:T(8,128)S(1)}, f32[10,128,128]{1,2,0:T(8,128)}, u32[]{:S(2)}) copy-start(f32[10,128,128]{1,2,0:T(8,128)} %get-tuple-element.43) | copy-start | bytes 1966084
  82.7 1.3 copy-start.15
  84.1 1.3 copy-start.17
  84.1 1.5 copy-start.8
  84.1 1.5 copy-start.11
  86.7 30.1 %collective-permute-start.2 = (f32[1,128,640]{2,1,0:T(8,128)}, f32[1,128,640]{2,1,0:T(8,128)}, u32[]{:S(2)}, u32[]{:S(2)}) collective-permute-start(f32[1,128,640]{2,1,0:T(8,128)} %fusion.30), channel_id=1, source_target_pairs={{0,1},{1,0},{2,3},{3,2},{4,5},{5,4},{6,7},{7,6},{8,9},{9,8},{10,11... | collective-permute-start | bytes 983048 | tf_op jit(solution)/shard_map/ppermute | solution.py:27
  150.4 1.9 %copy-start.6 = (bf16[1,3,640,640]{3,2,1,0:T(8,128)(2,1)S(1)}, bf16[1,3,640,640]{3,2,1,0:T(8,128)(2,1)}, u32[]{:S(2)}) copy-start(bf16[1,3,640,640]{3,2,1,0:T(8,128)(2,1)} %copy-done.5) | copy-start | bytes 7372804
  150.6 2.5 %copy-start.4 = (bf16[1,3,640,640]{3,2,1,0:T(8,128)(2,1)S(1)}, bf16[1,3,640,640]{3,2,1,0:T(8,128)(2,1)}, u32[]{:S(2)}) copy-start(bf16[1,3,640,640]{3,2,1,0:T(8,128)(2,1)} %copy-done.3) | copy-start | bytes 7372804
  153.1 1.7 copy-start.2
  153.7 2.0 %copy-start.22 = (bf16[640,640]{1,0:T(8,128)(2,1)S(1)}, bf16[640,640]{1,0:T(8,128)(2,1)}, u32[]{:S(2)}) copy-start(bf16[640,640]{1,0:T(8,128)(2,1)} %param.23) | copy-start | bytes 2457604
  160.4 1.3 copy-start.14
  163.7 2.9 %copy-start.9 = (bf16[640,640]{1,0:T(8,128)(2,1)S(1)}, bf16[640,640]{1,0:T(8,128)(2,1)}, u32[]{:S(2)}) copy-start(bf16[640,640]{1,0:T(8,128)(2,1)} %param.25) | copy-start | bytes 2457604
  167.0 8.7 %collective-permute-start.5 = (f32[1,128,640]{2,1,0:T(8,128)S(1)}, f32[1,128,640]{2,1,0:T(8,128)S(1)}, u32[]{:S(2)}, u32[]{:S(2)}) collective-permute-start(f32[1,128,640]{2,1,0:T(8,128)S(1)} %fusion.31), channel_id=1, source_target_pairs={{0,1},{1,0},{2,3},{3,2},{4,5},{5,4},{6,7},{7,6},{8,9},{9,8},{10,11... | collective-permute-start | bytes 983048 | tf_op jit(solution)/shard_map/ppermute | solution.py:27
Sparse Core Ops, SparseCore 0:
  10.8 46.2 all-gather.4
  68.6 41.0 all-gather.6
where the time goes:
time: 184 us; the launch traced here: 183 us
  blocking collectives  64.4 us (35%)
  local copies, waits for them, and re-layouts  25.7 us (14%)
  matrix products  22.7 us (12%)
  between operations  22.5 us (12%)
  starting transfers between devices  18.8 us (10%)
  waiting for transfers between devices  16.3 us (9%)
  other arithmetic  13 us (7%)
    psum x2, blocking collectives, group_silu(): total = lax.psum(jnp.sum(grouped, axis=(0, 2)), 'patch')  34.9 us
    psum x2, blocking collectives, group_silu(): var = lax.psum(jnp.sum(centered * centered, axis=(0, 2)), 'patch') / count  29.5 us
    all_gather x2, waiting for transfers between devices, shards(): piece = lax.all_gather(prev_keys, 'patch', axis=0, tiled=True)  13.5 us
    ppermute x2, starting transfers between devices, padded_2(): lax.ppermute(lax.slice_in_dim(block, block.shape[dim] - width, None, axis...  9.78 us
    slice x6, local copies, waits for them, and re-layouts, accumulate(): keys = keys_values[:, :width].reshape(-1, heads, head_dim)  9.48 us
    dot_general x4, matrix products, accumulate(): jnp.einsum('qhd,khd->hqk', query, keys, preferred_element_type=jnp.float32)  7.09 us
    ppermute x2, starting transfers between devices, from_partner(): lax.ppermute(x, axis, [(i, i ^ 1 << distance) for i in range(lax.axis_siz...  6.39 us
    slice x6, local copies, waits for them, and re-layouts, accumulate(): values = keys_values[:, width:].reshape(-1, heads, head_dim)  6.04 us
  transfers between devices with their start and end apart: 8, of which 2 were waited for; matrix products, arithmetic and copies ran while one was open for 21% of the time, Pallas kernels for 0%

commit v1 on v0

v1 whole, which is shorter than its diff:
```python
import functools
import math

import jax
import jax.numpy as jnp
import numpy as np
from jax import lax
from jax.experimental import pallas as pl
from jax.experimental.pallas import tpu as pltpu
from jax.sharding import PartitionSpec as P

HEADS = 10
GROUPS = 32
STEPS = 2
PATCHES = 8
COLS = 128
WIDTH = 640
PAIRS = HEADS // 2
PER_GROUP = WIDTH // GROUPS
BF = jnp.bfloat16
F32 = jnp.float32
EXACT = lax.Precision.HIGHEST


def alpha_table():
    start, stop = np.float32(0.00085**0.5), np.float32(0.012**0.5)
    betas = np.linspace(start, stop, 1000, dtype=np.float32) ** 2
    return np.cumprod(1.0 - betas.astype(np.float64)).astype(np.float32)


def table_pick(table, index):
    places = jnp.arange(table.shape[0], dtype=jnp.int32)
    return jnp.sum(jnp.where(places == index, table, jnp.zeros_like(table)))


def sinusoid(step_value, width):
    half = width // 2
    freqs = jnp.exp(-math.log(10000.0) * jnp.arange(half, dtype=F32) / half)
    angles = step_value.astype(F32) * freqs
    return jnp.concatenate([jnp.cos(angles), jnp.sin(angles)])


def update_coeffs(t_now, t_next):
    table = jnp.asarray(alpha_table())
    now = table_pick(table, t_now)
    after = table_pick(table, t_next)
    keep = jnp.sqrt(after / now)
    blend = jnp.sqrt(1.0 - after) - jnp.sqrt(after) * jnp.sqrt(1.0 - now) / jnp.sqrt(now)
    return (keep, blend)


def dot(a, b):
    return jnp.dot(a, b, preferred_element_type=F32)


def dot_exact(a, b):
    return jnp.dot(a, b, preferred_element_type=F32, precision=EXACT)


def call(body, outs, *args, scratch=(), flops=0, traffic=0):
    specs = []
    for arg in args:
        small = arg.ndim == 1 and arg.shape[0] <= 8
        specs.append(pl.BlockSpec(memory_space=pltpu.SMEM if small else pltpu.VMEM))
    return pl.pallas_call(
        body,
        out_shape=outs,
        in_specs=specs,
        out_specs=jax.tree.map(lambda _: pl.BlockSpec(memory_space=pltpu.VMEM), outs),
        scratch_shapes=list(scratch),
        compiler_params=pltpu.CompilerParams(vmem_limit_bytes=28 * 2**20),
        cost_estimate=pl.CostEstimate(flops=flops, bytes_accessed=traffic, transcendentals=0),
    )(*args)


def shape(dims, dtype):
    return jax.ShapeDtypeStruct(dims, dtype)


def group_matrix():
    channel = lax.broadcasted_iota(jnp.int32, (WIDTH, 128), 0)
    group = lax.broadcasted_iota(jnp.int32, (WIDTH, 128), 1)
    inside = (channel >= group * PER_GROUP) & (channel < (group + 1) * PER_GROUP)
    return jnp.where(inside, 1.0, 0.0).astype(F32)


def spread_matrix():
    group = lax.broadcasted_iota(jnp.int32, (128, WIDTH), 0)
    channel = lax.broadcasted_iota(jnp.int32, (128, WIDTH), 1)
    inside = (channel >= group * PER_GROUP) & (channel < (group + 1) * PER_GROUP)
    return jnp.where(inside, 1.0, 0.0).astype(F32)


def local_stats(x, stats_ref):
    gather, spread = group_matrix(), spread_matrix()
    mean_c = jnp.mean(x, axis=0, keepdims=True)
    centered = x - mean_c
    dev_c = jnp.sum(centered * centered, axis=0, keepdims=True)
    wide = lambda row: jnp.broadcast_to(row, (8, row.shape[1]))
    mean_g = dot_exact(wide(mean_c), gather) * (1.0 / PER_GROUP)
    off = wide(mean_c) - dot_exact(mean_g, spread)
    dev_g = dot_exact(wide(dev_c) + COLS * (off * off), gather)
    both = jnp.concatenate([mean_g[:1], dev_g[:1]], axis=0)
    stats_ref[...] = jnp.broadcast_to(both[None], stats_ref.shape)


def first_body(x_ref, attn_ref, conv_ref, stats_ref, out_ref):
    out_ref[0] = attn_ref[0, 0]
    out_ref[1] = conv_ref[0, 0]
    local_stats(x_ref[0], stats_ref)


def shifted(x):
    place = lax.broadcasted_iota(jnp.int32, x.shape, 0)
    before = jnp.where(place == 0, 0.0, pltpu.roll(x, 1, 0))
    after = jnp.where(place == COLS - 1, 0.0, pltpu.roll(x, COLS - 1, 0))
    return before, after


def conv_row(x, weights):
    before, after = shifted(x)
    return (
        dot(before.astype(BF), weights[0])
        + dot(x.astype(BF), weights[1])
        + dot(after.astype(BF), weights[2])
    )


def rims_body(edge_ref, up_ref, down_ref, w_ref, out_ref):
    above = up_ref[1].astype(F32) * edge_ref[0]
    below = down_ref[1].astype(F32) * edge_ref[1]
    out_ref[...] = conv_row(above, w_ref[0]) + conv_row(below, w_ref[2])


def level_body(
    stats_ref, x_ref, rims_ref, temb_ref, gn_ref, ln_ref, w_ref, q_ref, pair_ref, h_ref, query_ref
):
    mean = jnp.zeros((1, 128), F32)
    for p in range(PATCHES):
        mean = mean + stats_ref[p, 0:1]
    mean = mean * (1.0 / PATCHES)
    dev = jnp.zeros((1, 128), F32)
    for p in range(PATCHES):
        off = stats_ref[p, 0:1] - mean
        dev = dev + stats_ref[p, 1:2] + (COLS * PER_GROUP) * (off * off)
    scale = 1.0 / jnp.sqrt(dev * (1.0 / (PATCHES * COLS * PER_GROUP)) + 1e-05)
    rows = jnp.concatenate([jnp.broadcast_to(mean, (8, 128)), jnp.broadcast_to(scale, (8, 128))], axis=0)
    wide = dot_exact(rows, spread_matrix())
    x = x_ref[0]
    normed = (x - wide[0:1]) * (wide[8:9] * gn_ref[...])
    conv_in = normed * jax.nn.sigmoid(normed)
    hidden = x + (conv_row(conv_in, w_ref[0]) + rims_ref[...]) + temb_ref[...]
    pair_ref[1] = conv_in.astype(BF)
    h_ref[...] = hidden
    mid = jnp.mean(hidden, axis=1, keepdims=True)
    centered = hidden - mid
    var = jnp.mean(centered * centered, axis=1, keepdims=True)
    attn_in = (centered * (1.0 / jnp.sqrt(var + 1e-05)) * ln_ref[...]).astype(BF)
    pair_ref[0] = attn_in
    query_ref[...] = dot(attn_in, q_ref[...]).astype(BF)


def keys_body(count, *refs):
    w_ref, out_ref = refs[count], refs[count + 1]
    for i in range(count):
        ref = refs[i]
        rows = ref[0] if len(ref.shape) == 3 else ref[...]
        out_ref[i * COLS : (i + 1) * COLS] = dot(rows, w_ref[...]).astype(BF)


def attend_body(count, query_ref, h_ref, early_ref, *refs):
    kv_ref, out_w_ref, eps_ref, late_ref, mixed_ref = refs[count:]
    for i in range(count):
        ref = refs[i]
        rows = ref[0] if len(ref.shape) == 3 else ref[...]
        late_ref[i * COLS : (i + 1) * COLS] = dot(rows, kv_ref[...]).astype(BF)
    first_half = lax.broadcasted_iota(jnp.int32, (COLS, 128), 1) < WIDTH // HEADS
    for pair in range(PAIRS):
        lanes = slice(pair * 128, (pair + 1) * 128)
        values = slice(WIDTH + pair * 128, WIDTH + (pair + 1) * 128)
        query = query_ref[:, lanes]
        zero = jnp.zeros_like(query)
        stacked = jnp.concatenate(
            [jnp.where(first_half, query, zero), jnp.where(first_half, zero, query)], axis=0
        )
        scores = [
            lax.dot_general(
                stacked, ref[:, lanes], (((1,), (1,)), ((), ())), preferred_element_type=F32
            )
            * (WIDTH // HEADS) ** (-0.5)
            for ref in (early_ref, late_ref)
        ]
        top = jnp.maximum(
            jnp.max(scores[0], axis=1, keepdims=True), jnp.max(scores[1], axis=1, keepdims=True)
        )
        weights = [jnp.exp(s - top) for s in scores]
        total = jnp.sum(weights[0], axis=1, keepdims=True) + jnp.sum(weights[1], axis=1, keepdims=True)
        product = dot(weights[0].astype(BF), early_ref[:, values]) + dot(
            weights[1].astype(BF), late_ref[:, values]
        )
        product = product / total
        mixed_ref[:, lanes] = jnp.where(first_half, product[:COLS], product[COLS:]).astype(BF)
    eps_ref[...] = (h_ref[...] + dot(mixed_ref[...], out_w_ref[...])).astype(eps_ref.dtype)


def guide(branch, own, other):
    uncond = jnp.where(branch == 0, own, other)
    cond = jnp.where(branch == 0, other, own)
    return uncond + 3.0 * (cond - uncond)


def update_body(branch_ref, coeff_ref, x_ref, own_ref, other_ref, state_ref, stats_ref):
    guided = guide(branch_ref[0], own_ref[...].astype(F32), other_ref[...].astype(F32))
    state = coeff_ref[0] * x_ref[0] + coeff_ref[1] * guided
    state_ref[0] = state
    local_stats(state, stats_ref)


def last_body(branch_ref, coeff_ref, x_ref, own_ref, other_ref, state_ref, guided_ref):
    guided = guide(branch_ref[0], own_ref[...].astype(F32), other_ref[...].astype(F32))
    state_ref[0] = coeff_ref[0] * x_ref[0] + coeff_ref[1] * guided
    guided_ref[0] = guided


def shards(
    latent,
    stale_conv,
    stale_attn,
    cond_embed,
    timesteps,
    gn_gain,
    ln_gain,
    time_scale,
    conv_weight,
    q_weight,
    kv_weight,
    out_weight,
):
    branch = lax.axis_index("cfg").astype(jnp.int32).reshape(1)
    patch = lax.axis_index("patch")
    edges = jnp.stack([patch > 0, patch < PATCHES - 1]).astype(F32)
    upward = [(i, (i + 1) % PATCHES) for i in range(PATCHES)]
    downward = [(target, source) for source, target in upward]
    up = lambda x: lax.ppermute(x, "patch", upward)
    down = lambda x: lax.ppermute(x, "patch", downward)
    full = (COLS, WIDTH)
    stats_shape = shape((PATCHES, 2, 128), F32)
    coeffs = [jnp.stack(update_coeffs(timesteps[s], timesteps[s + 1])) for s in range(STEPS)]
    tembs = [
        jax.nn.silu(time_scale * sinusoid(timesteps[s], WIDTH) + cond_embed[0]).reshape(1, WIDTH)
        for s in range(STEPS)
    ]
    gn_gain, ln_gain = gn_gain.reshape(1, WIDTH), ln_gain.reshape(1, WIDTH)
    center = conv_weight[1:2]
    matmul = 2 * COLS * WIDTH * WIDTH

    state = latent
    stats, pair = call(
        first_body, (stats_shape, shape((2,) + full, BF)), state, stale_attn, stale_conv
    )
    for step in range(STEPS):
        ups, downs = [up(pair)], [down(pair)]
        stats = lax.all_to_all(stats, "patch", 0, 0)
        rims = call(
            rims_body, shape(full, F32), edges, ups[0], downs[0], conv_weight, flops=6 * matmul
        )
        ups.append(up(ups[0][0]))
        downs.append(down(downs[0][0]))
        ups.append(up(ups[1]))
        downs.append(down(downs[1]))
        ups.append(up(ups[2]))
        early = call(
            functools.partial(keys_body, 4),
            shape((4 * COLS, 2 * WIDTH), BF),
            ups[0],
            downs[0],
            ups[1],
            downs[1],
            kv_weight,
            flops=8 * matmul,
        )
        pair, hidden, query = call(
            level_body,
            (shape((2,) + full, BF), shape(full, F32), shape(full, BF)),
            stats,
            state,
            rims,
            tembs[step],
            gn_gain,
            ln_gain,
            center,
            q_weight,
            flops=4 * matmul,
        )
        eps = call(
            functools.partial(attend_body, 4),
            shape(full, BF),
            query,
            hidden,
            early,
            pair,
            ups[2],
            downs[2],
            ups[3],
            kv_weight,
            out_weight,
            scratch=(pltpu.VMEM((4 * COLS, 2 * WIDTH), BF), pltpu.VMEM(full, BF)),
            flops=20 * matmul,
        )
        other = lax.ppermute(eps, "cfg", [(0, 1), (1, 0)])
        if step + 1 < STEPS:
            state, stats = call(
                update_body,
                (shape((1,) + full, F32), stats_shape),
                branch,
                coeffs[step],
                state,
                eps,
                other,
            )
    whole = shape((1,) + full, F32)
    return call(last_body, (whole, whole), branch, coeffs[-1], state, eps, other)


def solution(mesh):
    placed = (
        P(("batch", "patch"), None, None),
        P("cfg", ("batch", "patch"), None, None),
        P("cfg", ("batch", "patch"), None, None),
        P(("batch", "cfg"), None),
        P(),
        P(),
        P(),
        P(),
        P(),
        P(),
        P(),
        P(),
    )
    return jax.shard_map(
        shards,
        mesh=mesh,
        in_specs=placed,
        out_specs=(P(("batch", "patch"), None, None), P(("batch", "patch"), None, None)),
        check_vma=False,
    )
```

time: 184 us -> 118 us (0.64)
  blocking collectives: 64.4 us -> 0 us
  Pallas kernels: 0 us -> 27.1 us
  matrix products: 22.7 us -> 0 us
  starting transfers between devices: 18.8 us -> 35.4 us
  between operations: 22.5 us -> 9.53 us
  other arithmetic: 13 us -> 4.33 us
  waiting for transfers between devices: 16.3 us -> 9.42 us
  local copies, waits for them, and re-layouts: 25.7 us -> 31.5 us
    psum x4 -> x0, blocking collectives: 64.4 us -> none  [the longest x2 34.9 us: group_silu(): total = lax.psum(jnp.sum(grouped, axis=(0, 2)), 'patch')]
    pallas_call x0 -> x11, Pallas kernels: none -> 27.1 us  [call(): pl.pallas_call(body, out_shape=outs, in_specs=specs, out_specs=jax.tree.m...]
    dot_general x21 -> x0, matrix products: 22.7 us -> none  [the longest x4 7.09 us: accumulate(): jnp.einsum('qhd,khd->hqk', query, keys, preferred_element_type=jnp.float32)]
    unnamed x50 -> x76, local copies, waits for them, and re-layouts: 3.8 us -> 21.8 us
    slice x17 -> x2, local copies, waits for them, and re-layouts: 20.3 us -> 4.78 us  [the longest x1 3.34 us: shards(): center = conv_weight[1:2]]
    all_gather x2 -> x0, waiting for transfers between devices: 13.5 us -> none  [shards(): piece = lax.all_gather(prev_keys, 'patch', axis=0, tiled=True)]
    all_to_all x0 -> x2, starting transfers between devices: none -> 10.1 us  [shards(): stats = lax.all_to_all(stats, 'patch', 0, 0)]
    ppermute x6 -> x16, starting transfers between devices: 18.8 us -> 25.3 us  [the longest x6 18.1 us: shards(): down = lambda x: lax.ppermute(x, 'patch', downward)]
  transfers between devices with their start and end apart: 8 -> 18, of which waited for: 2 -> 5; matrix products, arithmetic and copies ran while one was open for 21% -> 12% of each run, Pallas kernels for 0% -> 16%
where the time goes in v1:
time: 118 us; the launch traced here: 117 us
  starting transfers between devices  35.4 us (30%)
  local copies, waits for them, and re-layouts  31.5 us (27%)
  Pallas kernels  27.1 us (23%)
  between operations  9.53 us (8%)
  waiting for transfers between devices  9.42 us (8%)
  other arithmetic  4.33 us (4%)
    pallas_call x11, Pallas kernels, call(): pl.pallas_call(body, out_shape=outs, in_specs=specs, out_specs=jax.tree.m...  27.1 us
    unnamed x76, local copies, waits for them, and re-layouts  21.8 us
    ppermute x6, starting transfers between devices, shards(): down = lambda x: lax.ppermute(x, 'patch', downward)  18.1 us
    all_to_all x2, starting transfers between devices, shards(): stats = lax.all_to_all(stats, 'patch', 0, 0)  10.1 us
    ppermute x8, waiting for transfers between devices, shards(): up = lambda x: lax.ppermute(x, 'patch', upward)  5.9 us
    ppermute x2, starting transfers between devices, shards(): other = lax.ppermute(eps, 'cfg', [(0, 1), (1, 0)])  5.17 us
    slice x1, local copies, waits for them, and re-layouts, shards(): center = conv_weight[1:2]  3.34 us
    reduce_sum x1, other arithmetic, table_pick(): return jnp.sum(jnp.where(places == index, table, jnp.zeros_like(table)))  2.53 us
  transfers between devices with their start and end apart: 18, of which 5 were waited for; matrix products, arithmetic and copies ran while one was open for 12% of the time, Pallas kernels for 16%

profile of v1, /device:TPU:2, one launch (start us, length us, event | category | flops | bytes accessed | tf_op | source)
XLA Modules:
  0.0 117.3 jit_solution(10306602686518255175)
XLA Ops:
  0.6 1.0 copy-done.9
  1.6 0.9 copy-done.25
  2.5 0.9 copy-done.26
  3.4 1.5 %shard_map.149 = (f32[8,2,128]{2,1,0:T(2,128)}, bf16[2,128,640]{2,1,0:T(8,128)(2,1)S(1)}) custom-call(f32[1,128,640]{2,1,0:T(8,128)S(1)} %copy-done.9, bf16[1,1,128,640]{3,2,1,0:T(8,128)(2,1)S(1)} %copy-done.25, bf16[1,1,128,640]{3,2,1,0:T(8,128)(2,1)S(1)} %copy-done.26), custom_call_target="tpu_custom_call" | custom-call | tf_op jit(solution)/shard_map/pallas_call | solution.py:65
  5.0 5.9 %collective-permute-start.1 = (bf16[2,128,640]{2,1,0:T(8,128)(2,1)S(1)}, bf16[2,128,640]{2,1,0:T(8,128)(2,1)S(1)}, u32[]{:S(2)}, u32[]{:S(2)}) collective-permute-start(bf16[2,128,640]{2,1,0:T(8,128)(2,1)S(1)} %get-tuple-element.13), channel_id=1, source_target_pairs={{2,0},{4,2},{6,4},{8,6},{10,8},{12,10},{14,12},{0,14},{3,1},{5,3},... | collective-permute-start | bytes 983048 | tf_op jit(solution)/shard_map/ppermute | solution.py:245
  10.8 4.6 %all-to-all-start = ((f32[8,2,128]{2,1,0:T(2,128)}), f32[8,2,128]{2,1,0:T(2,128)S(1)}, u32[]{:S(2)}, u32[]{:S(2)}) async-start(f32[8,2,128]{2,1,0:T(2,128)} %get-tuple-element.12), calls=%async_computation | async-start | bytes 16384 | tf_op jit(solution)/shard_map/all_to_all | solution.py:263
  15.4 1.4 %fusion.8 = (s32[1]{0:T(128)}, s32[1]{0:T(128)}, s32[1]{0:T(128)}) fusion(s32[3]{0:T(128)} %param.18), kind=kLoop, calls=%fused_computation.26 | loop fusion | bytes 24 | tf_op jit(solution)/shard_map/slice | solution.py:248
  20.4 0.8 divide_multiply_fusion
  21.2 3.3 %slice.30.w_ref = bf16[1,3,640,640]{3,2,1,0:T(8,128)(2,1)} slice(bf16[3,3,640,640]{3,2,1,0:T(8,128)(2,1)} %w_ref.3), slice={[1:2], [0:3], [0:640], [0:640]} | slice | bytes 4915200 | tf_op jit(solution)/shard_map/slice | solution.py:254
  25.3 3.2 %collective-permute-start.3 = (bf16[128,640]{1,0:T(8,128)(2,1)}, bf16[128,640]{1,0:T(8,128)(2,1)}, u32[]{:S(2)}, u32[]{:S(2)}) collective-permute-start(bf16[128,640]{1,0:T(8,128)(2,1)} %slice_bitcast_fusion.2), channel_id=1, source_target_pairs={{2,0},{4,2},{6,4},{8,6},{10,8},{12,10},{14,12},{0,14},{3,1},{5,3},... | collective-permute-start | bytes 491528 | tf_op jit(solution)/shard_map/ppermute | solution.py:245
  28.5 3.1 %copy-done = bf16[3,3,640,640]{3,2,1,0:T(8,128)(2,1)S(1)} copy-done((bf16[3,3,640,640]{3,2,1,0:T(8,128)(2,1)S(1)}, bf16[3,3,640,640]{3,2,1,0:T(8,128)(2,1)}, u32[]{:S(2)}) %copy-start) | copy-done | bytes 7372824
  31.6 1.7 %shard_map.150.rims_ref = f32[128,640]{1,0:T(8,128)S(1)} custom-call(f32[2]{0:T(128)S(1)} %add_convert_fusion.edge_ref, bf16[2,128,640]{2,1,0:T(8,128)(2,1)S(1)} %collective-permute-done.up_ref.refs_0_, bf16[2,128,640]{2,1,0:T(8,128)(2,1)S(1)} %collective-permute-done.1.down_ref.refs_1_, bf16[3,3,640,640]{3,2,1,0:T(8,128)(2,1)S(1)} %copy-done), custom_call_target="tpu_custom_call" | custom-call | flops 629145600 | tf_op jit(solution)/shard_map/pallas_call | solution.py:65
  34.1 1.7 %copy-done.1 = bf16[1,3,640,640]{3,2,1,0:T(8,128)(2,1)S(1)} copy-done((bf16[1,3,640,640]{3,2,1,0:T(8,128)(2,1)S(1)}, bf16[1,3,640,640]{3,2,1,0:T(8,128)(2,1)}, u32[]{:S(2)}) %copy-start.1) | copy-done | bytes 2457624
  35.8 1.1 copy-done.7
  36.9 1.0 copy-done.19
  37.9 2.0 %shard_map.151 = (bf16[2,128,640]{2,1,0:T(8,128)(2,1)}, f32[128,640]{1,0:T(8,128)S(1)}, bf16[128,640]{1,0:T(8,128)(2,1)S(1)}) custom-call(f32[8,2,128]{2,1,0:T(2,128)S(1)} %all-to-all-done.stats_ref, f32[1,128,640]{2,1,0:T(8,128)S(1)} %copy-done.10, f32[128,640]{1,0:T(8,128)S(1)} %copy-done.19, f32[1,640]{1,0:T(1,128)S(1)} %reshape.20.temb_ref, ...), custom_call_target="tpu_custom_call" | custom-call | flops 419430400 | tf_op jit(solution)/shard_map/pallas_call | solution.py:65
  40.6 0.8 slice_bitcast_fusion.3
  42.1 2.5 %collective-permute-start.9 = (bf16[2,128,640]{2,1,0:T(8,128)(2,1)}, bf16[2,128,640]{2,1,0:T(8,128)(2,1)}, u32[]{:S(2)}, u32[]{:S(2)}) collective-permute-start(bf16[2,128,640]{2,1,0:T(8,128)(2,1)} %get-tuple-element.16.refs_0_), channel_id=1, source_target_pairs={{2,0},{4,2},{6,4},{8,6},{10,8},{12,10},{14,12},{0,14},{3,1},{5,3},... | collective-permute-start | bytes 983048 | tf_op jit(solution)/shard_map/ppermute | solution.py:245
  44.6 2.5 %select_reduce_fusion = (f32[]{:T(128)}, f32[]{:T(128)}, f32[]{:T(128)}) fusion(f32[1000]{0:T(1024)S(1)} %copy-done.35, s32[]{:T(128)} %bitcast.5, s32[]{:T(128)} %bitcast.1, s32[]{:T(128)} %bitcast.2), kind=kLoop, calls=%fused_computation.10 | loop fusion | flops 8997 | bytes 4024 | tf_op jit(solution)/shard_map/reduce_sum | solution.py:33
  51.1 2.0 %collective-permute-start.5 = (bf16[128,640]{1,0:T(8,128)(2,1)}, bf16[128,640]{1,0:T(8,128)(2,1)S(1)}, u32[]{:S(2)}, u32[]{:S(2)}) collective-permute-start(bf16[128,640]{1,0:T(8,128)(2,1)} %collective-permute-done.3.refs_3_), channel_id=1, source_target_pairs={{2,0},{4,2},{6,4},{8,6},{10,8},{12,10},{14,12},{0,14},{3,1},{5,3},... | collective-permute-start | bytes 491528 | tf_op jit(solution)/shard_map/ppermute | solution.py:245
  53.7 1.4 %copy-done.3 = bf16[640,1280]{1,0:T(8,128)(2,1)S(1)} copy-done((bf16[640,1280]{1,0:T(8,128)(2,1)S(1)}, bf16[640,1280]{1,0:T(8,128)(2,1)}, u32[]{:S(2)}) %copy-start.3) | copy-done | bytes 1638424
  55.1 1.0 copy-done.12
  56.1 1.0 copy-done.15
  57.1 2.3 %shard_map.152.early_ref = bf16[512,1280]{1,0:T(8,128)(2,1)S(1)} custom-call(bf16[2,128,640]{2,1,0:T(8,128)(2,1)S(1)} %copy-done.15, bf16[2,128,640]{2,1,0:T(8,128)(2,1)S(1)} %copy-done.12, bf16[128,640]{1,0:T(8,128)(2,1)} %collective-permute-done.2.refs_2_, bf16[128,640]{1,0:T(8,128)(2,1)} %collective-permute-done.3.refs_3_, bf16[640,1280]{1,0:T(8,128)(2,1)S(1)} %copy-done.3), custom_call_target="tpu_custom_call" | custom-call | flops 838860800 | tf_op jit(solution)/shard_map/pallas_call | solution.py:65
  59.5 1.1 slice_bitcast_fusion.1
  60.6 1.3 %collective-permute-start.6 = (bf16[128,640]{1,0:T(8,128)(2,1)S(1)}, bf16[128,640]{1,0:T(8,128)(2,1)S(1)}, u32[]{:S(2)}, u32[]{:S(2)}) collective-permute-start(bf16[128,640]{1,0:T(8,128)(2,1)S(1)} %collective-permute-done.4.refs_1_), channel_id=1, source_target_pairs={{0,2},{2,4},{4,6},{6,8},{8,10},{10,12},{12,14},{14,0},{1,3},{3,5},... | collective-permute-start | bytes 491528 | tf_op jit(solution)/shard_map/ppermute | solution.py:244
  61.9 0.9 slice_bitcast_fusion
  62.8 2.3 %collective-permute-start.11 = (bf16[128,640]{1,0:T(8,128)(2,1)S(1)}, bf16[128,640]{1,0:T(8,128)(2,1)}, u32[]{:S(2)}, u32[]{:S(2)}) collective-permute-start(bf16[128,640]{1,0:T(8,128)(2,1)S(1)} %slice_bitcast_fusion), channel_id=1, source_target_pairs={{2,0},{4,2},{6,4},{8,6},{10,8},{12,10},{14,12},{0,14},{3,1},{5,3},... | collective-permute-start | bytes 491528 | tf_op jit(solution)/shard_map/ppermute | solution.py:245
  65.2 2.0 %collective-permute-done.10.refs_2_ = bf16[128,640]{1,0:T(8,128)(2,1)S(1)} collective-permute-done((bf16[128,640]{1,0:T(8,128)(2,1)S(1)}, bf16[128,640]{1,0:T(8,128)(2,1)S(1)}, u32[]{:S(2)}, u32[]{:S(2)}) %collective-permute-start.10) | collective-permute-done | bytes 163872 | tf_op jit(solution)/shard_map/ppermute | solution.py:244
  67.2 3.3 %collective-permute-done.6.refs_3_ = bf16[128,640]{1,0:T(8,128)(2,1)S(1)} collective-permute-done((bf16[128,640]{1,0:T(8,128)(2,1)S(1)}, bf16[128,640]{1,0:T(8,128)(2,1)S(1)}, u32[]{:S(2)}, u32[]{:S(2)}) %collective-permute-start.6) | collective-permute-done | bytes 163872 | tf_op jit(solution)/shard_map/ppermute | solution.py:244
  70.6 4.8 %shard_map.153.own_ref = bf16[128,640]{1,0:T(8,128)(2,1)S(1)} custom-call(bf16[128,640]{1,0:T(8,128)(2,1)S(1)} %copy-done.34, f32[128,640]{1,0:T(8,128)S(1)} %copy-done.32, bf16[512,1280]{1,0:T(8,128)(2,1)S(1)} %shard_map.152.early_ref, bf16[2,128,640]{2,1,0:T(8,128)(2,1)} %get-tuple-element.16.refs_0_, bf16[128,640]{1,0:T(8,128)(2,1)S(1)} %collective-permute-done.4.refs_1_, ...), custom_call_target="tpu_custom_call" | custom-call | flops 2097152000 | tf_op jit(solution)/shard_map/pallas_call | solution.py:65
  75.4 3.3 %collective-permute-start.7 = (bf16[128,640]{1,0:T(8,128)(2,1)S(1)}, bf16[128,640]{1,0:T(8,128)(2,1)S(1)}, u32[]{:S(2)}, u32[]{:S(2)}) collective-permute-start(bf16[128,640]{1,0:T(8,128)(2,1)S(1)} %shard_map.153.own_ref), channel_id=1, source_target_pairs={{0,1},{1,0},{2,3},{3,2},{4,5},{5,4},{6,7},{7,6},{8,9},{9,8},{10,11... | collective-permute-start | bytes 491528 | tf_op jit(solution)/shard_map/ppermute | solution.py:310
  78.8 2.2 %collective-permute-start.13 = (bf16[128,640]{1,0:T(8,128)(2,1)}, bf16[128,640]{1,0:T(8,128)(2,1)}, u32[]{:S(2)}, u32[]{:S(2)}) collective-permute-start(bf16[128,640]{1,0:T(8,128)(2,1)} %collective-permute-done.11.refs_3_), channel_id=1, source_target_pairs={{2,0},{4,2},{6,4},{8,6},{10,8},{12,10},{14,12},{0,14},{3,1},{5,3},... | collective-permute-start | bytes 491528 | tf_op jit(solution)/shard_map/ppermute | solution.py:245
  80.9 2.2 %shard_map.155.rims_ref = f32[128,640]{1,0:T(8,128)S(1)} custom-call(f32[2]{0:T(128)S(1)} %add_convert_fusion.edge_ref, bf16[2,128,640]{2,1,0:T(8,128)(2,1)} %collective-permute-done.8.up_ref.refs_0_, bf16[2,128,640]{2,1,0:T(8,128)(2,1)} %collective-permute-done.9.down_ref.refs_1_, bf16[3,3,640,640]{3,2,1,0:T(8,128)(2,1)S(1)} %bitcast.19), custom_call_target="tpu_custom_call" | custom-call | flops 629145600 | tf_op jit(solution)/shard_map/pallas_call | solution.py:65
  83.8 2.1 %shard_map.154 = (f32[1,128,640]{2,1,0:T(8,128)S(1)}, f32[8,2,128]{2,1,0:T(2,128)}) custom-call(s32[1]{0:T(128)} %bitcast.branch_ref, f32[2]{0:T(128)S(1)} %pad_maximum_fusion.1.coeff_ref, f32[1,128,640]{2,1,0:T(8,128)S(1)} %copy-done.10, bf16[128,640]{1,0:T(8,128)(2,1)S(1)} %shard_map.153.own_ref, bf16[128,640]{1,0:T(8,128)(2,1)S(1)} %collective-permute-done.7.other_ref), custom_call_target="tpu_custom_call" | custom-call | tf_op jit(solution)/shard_map/pallas_call | solution.py:65
  86.7 5.4 %all-to-all-start.1 = ((f32[8,2,128]{2,1,0:T(2,128)}), f32[8,2,128]{2,1,0:T(2,128)S(1)}, u32[]{:S(2)}, u32[]{:S(2)}) async-start(f32[8,2,128]{2,1,0:T(2,128)} %get-tuple-element.18), calls=%async_computation.1 | async-start | bytes 16384 | tf_op jit(solution)/shard_map/all_to_all | solution.py:263
  92.2 1.4 %copy-done.5 = bf16[640,1280]{1,0:T(8,128)(2,1)S(1)} copy-done((bf16[640,1280]{1,0:T(8,128)(2,1)S(1)}, bf16[640,1280]{1,0:T(8,128)(2,1)}, u32[]{:S(2)}) %copy-start.5) | copy-done | bytes 1638424
  93.6 0.9 copy-done.28
  94.5 2.5 %shard_map.157.early_ref = bf16[512,1280]{1,0:T(8,128)(2,1)S(1)} custom-call(bf16[2,128,640]{2,1,0:T(8,128)(2,1)} %collective-permute-done.8.up_ref.refs_0_, bf16[2,128,640]{2,1,0:T(8,128)(2,1)} %collective-permute-done.9.down_ref.refs_1_, bf16[128,640]{1,0:T(8,128)(2,1)S(1)} %copy-done.28, bf16[128,640]{1,0:T(8,128)(2,1)} %collective-permute-done.11.refs_3_, ...), custom_call_target="tpu_custom_call" | custom-call | flops 838860800 | tf_op jit(solution)/shard_map/pallas_call | solution.py:65
  97.0 1.0 copy-done.23
  98.0 1.9 %all-to-all-done.1.stats_ref = f32[8,2,128]{2,1,0:T(2,128)S(1)} async-done(((f32[8,2,128]{2,1,0:T(2,128)}), f32[8,2,128]{2,1,0:T(2,128)S(1)}, u32[]{:S(2)}, u32[]{:S(2)}) %all-to-all-start.1) | async-done | bytes 8224 | tf_op jit(solution)/shard_map/all_to_all | solution.py:263
  99.9 1.0 copy-done.17
  100.9 1.0 copy-done.21
  101.8 1.5 %shard_map.156 = (bf16[2,128,640]{2,1,0:T(8,128)(2,1)S(1)}, f32[128,640]{1,0:T(8,128)S(1)}, bf16[128,640]{1,0:T(8,128)(2,1)S(1)}) custom-call(f32[8,2,128]{2,1,0:T(2,128)S(1)} %all-to-all-done.1.stats_ref, f32[1,128,640]{2,1,0:T(8,128)S(1)} %copy-done.21, f32[128,640]{1,0:T(8,128)S(1)} %copy-done.17, f32[1,640]{1,0:T(1,128)S(1)} %reshape.23.temb_ref, ...), custom_call_target="tpu_custom_call" | custom-call | flops 419430400 | tf_op jit(solution)/shard_map/pallas_call | solution.py:65
  103.9 5.0 %shard_map.158.own_ref = bf16[128,640]{1,0:T(8,128)(2,1)S(1)} custom-call(bf16[128,640]{1,0:T(8,128)(2,1)S(1)} %get-tuple-element.19.query_ref, f32[128,640]{1,0:T(8,128)S(1)} %get-tuple-element.20.h_ref, bf16[512,1280]{1,0:T(8,128)(2,1)S(1)} %copy-done.24, bf16[2,128,640]{2,1,0:T(8,128)(2,1)S(1)} %get-tuple-element.21.refs_0_, ...), custom_call_target="tpu_custom_call" | custom-call | flops 2097152000 | tf_op jit(solution)/shard_map/pallas_call | solution.py:65
  108.9 1.9 %collective-permute-start.15 = (bf16[128,640]{1,0:T(8,128)(2,1)S(1)}, bf16[128,640]{1,0:T(8,128)(2,1)S(1)}, u32[]{:S(2)}, u32[]{:S(2)}) collective-permute-start(bf16[128,640]{1,0:T(8,128)(2,1)S(1)} %shard_map.158.own_ref), channel_id=1, source_target_pairs={{0,1},{1,0},{2,3},{3,2},{4,5},{5,4},{6,7},{7,6},{8,9},{9,8},{10,11... | collective-permute-start | bytes 491528 | tf_op jit(solution)/shard_map/ppermute | solution.py:310
  114.2 1.6 %collective-permute-done.15.other_ref = bf16[128,640]{1,0:T(8,128)(2,1)S(1)} collective-permute-done((bf16[128,640]{1,0:T(8,128)(2,1)S(1)}, bf16[128,640]{1,0:T(8,128)(2,1)S(1)}, u32[]{:S(2)}, u32[]{:S(2)}) %collective-permute-start.15) | collective-permute-done | bytes 163872 | tf_op jit(solution)/shard_map/ppermute | solution.py:310
  115.8 1.5 %shard_map.159 = (f32[1,128,640]{2,1,0:T(8,128)}, f32[1,128,640]{2,1,0:T(8,128)}) custom-call(s32[1]{0:T(128)} %bitcast.branch_ref, f32[2]{0:T(128)S(1)} %pad_maximum_fusion.coeff_ref, f32[1,128,640]{2,1,0:T(8,128)S(1)} %copy-done.22, bf16[128,640]{1,0:T(8,128)(2,1)S(1)} %shard_map.158.own_ref, bf16[128,640]{1,0:T(8,128)(2,1)S(1)} %collective-permute-done.15.other_ref), custom_call_target="tpu_custom_call" | custom-call | tf_op jit(solution)/shard_map/pallas_call | solution.py:65
  (94 shorter events, 7.9 us)
Async XLA Ops:
  0.6 1.0 copy-start.9
  5.0 19.7 %collective-permute-start.1 = (bf16[2,128,640]{2,1,0:T(8,128)(2,1)S(1)}, bf16[2,128,640]{2,1,0:T(8,128)(2,1)S(1)}, u32[]{:S(2)}, u32[]{:S(2)}) collective-permute-start(bf16[2,128,640]{2,1,0:T(8,128)(2,1)S(1)} %get-tuple-element.13), channel_id=1, source_target_pairs={{2,0},{4,2},{6,4},{8,6},{10,8},{12,10},{14,12},{0,14},{3,1},{5,3},... | collective-permute-start | bytes 983048 | tf_op jit(solution)/shard_map/ppermute | solution.py:245
  10.8 17.7 %collective-permute-start = (bf16[2,128,640]{2,1,0:T(8,128)(2,1)S(1)}, bf16[2,128,640]{2,1,0:T(8,128)(2,1)S(1)}, u32[]{:S(2)}, u32[]{:S(2)}) collective-permute-start(bf16[2,128,640]{2,1,0:T(8,128)(2,1)S(1)} %get-tuple-element.13), channel_id=1, source_target_pairs={{0,2},{2,4},{4,6},{6,8},{8,10},{10,12},{12,14},{14,0},{1,3},{3,5},... | collective-permute-start | bytes 983048 | tf_op jit(solution)/shard_map/ppermute | solution.py:244
  10.8 23.3 %all-to-all-start = ((f32[8,2,128]{2,1,0:T(2,128)}), f32[8,2,128]{2,1,0:T(2,128)S(1)}, u32[]{:S(2)}, u32[]{:S(2)}) async-start(f32[8,2,128]{2,1,0:T(2,128)} %get-tuple-element.12), calls=%async_computation | async-start | bytes 16384 | tf_op jit(solution)/shard_map/all_to_all | solution.py:263
  24.6 8.7 %copy-start.11 = (bf16[2,128,640]{2,1,0:T(8,128)(2,1)}, bf16[2,128,640]{2,1,0:T(8,128)(2,1)S(1)}, u32[]{:S(2)}) copy-start(bf16[2,128,640]{2,1,0:T(8,128)(2,1)S(1)} %collective-permute-done.1.down_ref.refs_1_) | copy-start | bytes 983044
  24.6 9.5 %copy-start.10 = (f32[1,128,640]{2,1,0:T(8,128)S(1)}, f32[1,128,640]{2,1,0:T(8,128)}, u32[]{:S(2)}) copy-start(f32[1,128,640]{2,1,0:T(8,128)} %x_ref.5) | copy-start | bytes 983044
  25.3 25.8 %collective-permute-start.3 = (bf16[128,640]{1,0:T(8,128)(2,1)}, bf16[128,640]{1,0:T(8,128)(2,1)}, u32[]{:S(2)}, u32[]{:S(2)}) collective-permute-start(bf16[128,640]{1,0:T(8,128)(2,1)} %slice_bitcast_fusion.2), channel_id=1, source_target_pairs={{2,0},{4,2},{6,4},{8,6},{10,8},{12,10},{14,12},{0,14},{3,1},{5,3},... | collective-permute-start | bytes 491528 | tf_op jit(solution)/shard_map/ppermute | solution.py:245
  28.5 3.1 %copy-start = (bf16[3,3,640,640]{3,2,1,0:T(8,128)(2,1)S(1)}, bf16[3,3,640,640]{3,2,1,0:T(8,128)(2,1)}, u32[]{:S(2)}) copy-start(bf16[3,3,640,640]{3,2,1,0:T(8,128)(2,1)} %w_ref.3) | copy-start | bytes 22118404
  31.6 1.7 %copy-start.13 = (bf16[2,128,640]{2,1,0:T(8,128)(2,1)}, bf16[2,128,640]{2,1,0:T(8,128)(2,1)S(1)}, u32[]{:S(2)}) copy-start(bf16[2,128,640]{2,1,0:T(8,128)(2,1)S(1)} %collective-permute-done.up_ref.refs_0_) | copy-start | bytes 983044
  34.1 1.7 %copy-start.1 = (bf16[1,3,640,640]{3,2,1,0:T(8,128)(2,1)S(1)}, bf16[1,3,640,640]{3,2,1,0:T(8,128)(2,1)}, u32[]{:S(2)}) copy-start(bf16[1,3,640,640]{3,2,1,0:T(8,128)(2,1)} %slice.30.w_ref) | copy-start | bytes 7372804
  35.8 1.1 copy-start.7
  36.9 1.0 copy-start.19
  37.9 2.7 %copy-start.14 = (bf16[2,128,640]{2,1,0:T(8,128)(2,1)S(1)}, bf16[2,128,640]{2,1,0:T(8,128)(2,1)}, u32[]{:S(2)}) copy-start(bf16[2,128,640]{2,1,0:T(8,128)(2,1)} %copy-done.13) | copy-start | bytes 983044
  37.9 6.7 %copy-start.35 = (f32[1000]{0:T(1024)S(1)}, f32[1000]{0:T(1024)}, u32[]{:S(2)}) copy-start(f32[1000]{0:T(1024)} %constant.27.clone) | copy-start | bytes 12004
  37.9 43.0 %slice-start = ((s8[7372800]{0:T(1024)(128)(4,1)}), s8[3178496]{0:T(1024)(128)(4,1)S(1)}, s32[]{:S(2)}) async-start(s8[7372800]{0:T(1024)(128)(4,1)} %bitcast.18), calls=%async_computation.2 | async-start | bytes 6356992
  40.6 18.8 %collective-permute-start.8 = (bf16[2,128,640]{2,1,0:T(8,128)(2,1)}, bf16[2,128,640]{2,1,0:T(8,128)(2,1)}, u32[]{:S(2)}, u32[]{:S(2)}) collective-permute-start(bf16[2,128,640]{2,1,0:T(8,128)(2,1)} %get-tuple-element.16.refs_0_), channel_id=1, source_target_pairs={{0,2},{2,4},{4,6},{6,8},{8,10},{10,12},{12,14},{14,0},{1,3},{3,5},... | collective-permute-start | bytes 983048 | tf_op jit(solution)/shard_map/ppermute | solution.py:244
  41.4 12.3 %collective-permute-start.2 = (bf16[128,640]{1,0:T(8,128)(2,1)}, bf16[128,640]{1,0:T(8,128)(2,1)}, u32[]{:S(2)}, u32[]{:S(2)}) collective-permute-start(bf16[128,640]{1,0:T(8,128)(2,1)} %slice_bitcast_fusion.3), channel_id=1, source_target_pairs={{0,2},{2,4},{4,6},{6,8},{8,10},{10,12},{12,14},{14,0},{1,3},{3,5},... | collective-permute-start | bytes 491528 | tf_op jit(solution)/shard_map/ppermute | solution.py:244
  42.1 19.8 %collective-permute-start.9 = (bf16[2,128,640]{2,1,0:T(8,128)(2,1)}, bf16[2,128,640]{2,1,0:T(8,128)(2,1)}, u32[]{:S(2)}, u32[]{:S(2)}) collective-permute-start(bf16[2,128,640]{2,1,0:T(8,128)(2,1)} %get-tuple-element.16.refs_0_), channel_id=1, source_target_pairs={{2,0},{4,2},{6,4},{8,6},{10,8},{12,10},{14,12},{0,14},{3,1},{5,3},... | collective-permute-start | bytes 983048 | tf_op jit(solution)/shard_map/ppermute | solution.py:245
  51.1 16.1 %collective-permute-start.5 = (bf16[128,640]{1,0:T(8,128)(2,1)}, bf16[128,640]{1,0:T(8,128)(2,1)S(1)}, u32[]{:S(2)}, u32[]{:S(2)}) collective-permute-start(bf16[128,640]{1,0:T(8,128)(2,1)} %collective-permute-done.3.refs_3_), channel_id=1, source_target_pairs={{2,0},{4,2},{6,4},{8,6},{10,8},{12,10},{14,12},{0,14},{3,1},{5,3},... | collective-permute-start | bytes 491528 | tf_op jit(solution)/shard_map/ppermute | solution.py:245
  53.7 6.9 %collective-permute-start.4 = (bf16[128,640]{1,0:T(8,128)(2,1)}, bf16[128,640]{1,0:T(8,128)(2,1)S(1)}, u32[]{:S(2)}, u32[]{:S(2)}) collective-permute-start(bf16[128,640]{1,0:T(8,128)(2,1)} %collective-permute-done.2.refs_2_), channel_id=1, source_target_pairs={{0,2},{2,4},{4,6},{6,8},{8,10},{10,12},{12,14},{14,0},{1,3},{3,5},... | collective-permute-start | bytes 491528 | tf_op jit(solution)/shard_map/ppermute | solution.py:244
  53.7 1.4 %copy-start.3 = (bf16[640,1280]{1,0:T(8,128)(2,1)S(1)}, bf16[640,1280]{1,0:T(8,128)(2,1)}, u32[]{:S(2)}) copy-start(bf16[640,1280]{1,0:T(8,128)(2,1)} %refs_4_.7) | copy-start | bytes 4915204
  55.1 1.0 copy-start.12
  56.1 1.0 copy-start.15
  57.1 13.5 %copy-start.4 = (bf16[640,1280]{1,0:T(8,128)(2,1)S(1)}, bf16[640,1280]{1,0:T(8,128)(2,1)}, u32[]{:S(2)}) copy-start(bf16[640,1280]{1,0:T(8,128)(2,1)} %refs_4_.7) | copy-start | bytes 4915204
  57.1 13.5 %copy-start.29 = (bf16[640,640]{1,0:T(8,128)(2,1)S(1)}, bf16[640,640]{1,0:T(8,128)(2,1)}, u32[]{:S(2)}) copy-start(bf16[640,640]{1,0:T(8,128)(2,1)} %refs_5_.3) | copy-start | bytes 2457604
  57.1 13.5 %copy-start.32 = (f32[128,640]{1,0:T(8,128)S(1)}, f32[128,640]{1,0:T(8,128)}, u32[]{:S(2)}) copy-start(f32[128,640]{1,0:T(8,128)} %copy-done.31) | copy-start | bytes 983044
  57.1 13.5 %copy-start.34 = (bf16[128,640]{1,0:T(8,128)(2,1)S(1)}, bf16[128,640]{1,0:T(8,128)(2,1)}, u32[]{:S(2)}) copy-start(bf16[128,640]{1,0:T(8,128)(2,1)} %copy-done.33) | copy-start | bytes 491524
  59.4 21.5 %slice-start.1 = ((s8[7372800]{0:T(1024)(128)(4,1)}), s8[4194304]{0:T(1024)(128)(4,1)S(1)}, s32[]{:S(2)}) async-start(s8[7372800]{0:T(1024)(128)(4,1)} %bitcast.18), calls=%async_computation.3 | async-start | bytes 8388608
  60.5 6.7 %collective-permute-start.10 = (bf16[128,640]{1,0:T(8,128)(2,1)S(1)}, bf16[128,640]{1,0:T(8,128)(2,1)S(1)}, u32[]{:S(2)}, u32[]{:S(2)}) collective-permute-start(bf16[128,640]{1,0:T(8,128)(2,1)S(1)} %slice_bitcast_fusion.1), channel_id=1, source_target_pairs={{0,2},{2,4},{4,6},{6,8},{8,10},{10,12},{12,14},{14,0},{1,3},{3,5},... | collective-permute-start | bytes 491528 | tf_op jit(solution)/shard_map/ppermute | solution.py:244
  60.6 9.9 %collective-permute-start.6 = (bf16[128,640]{1,0:T(8,128)(2,1)S(1)}, bf16[128,640]{1,0:T(8,128)(2,1)S(1)}, u32[]{:S(2)}, u32[]{:S(2)}) collective-permute-start(bf16[128,640]{1,0:T(8,128)(2,1)S(1)} %collective-permute-done.4.refs_1_), channel_id=1, source_target_pairs={{0,2},{2,4},{4,6},{6,8},{8,10},{10,12},{12,14},{14,0},{1,3},{3,5},... | collective-permute-start | bytes 491528 | tf_op jit(solution)/shard_map/ppermute | solution.py:244
  62.8 15.9 %collective-permute-start.11 = (bf16[128,640]{1,0:T(8,128)(2,1)S(1)}, bf16[128,640]{1,0:T(8,128)(2,1)}, u32[]{:S(2)}, u32[]{:S(2)}) collective-permute-start(bf16[128,640]{1,0:T(8,128)(2,1)S(1)} %slice_bitcast_fusion), channel_id=1, source_target_pairs={{2,0},{4,2},{6,4},{8,6},{10,8},{12,10},{14,12},{0,14},{3,1},{5,3},... | collective-permute-start | bytes 491528 | tf_op jit(solution)/shard_map/ppermute | solution.py:245
  67.2 8.2 %copy-start.27 = (bf16[128,640]{1,0:T(8,128)(2,1)}, bf16[128,640]{1,0:T(8,128)(2,1)S(1)}, u32[]{:S(2)}) copy-start(bf16[128,640]{1,0:T(8,128)(2,1)S(1)} %collective-permute-done.10.refs_2_) | copy-start | bytes 491524
  67.2 13.7 %collective-permute-start.12 = (bf16[128,640]{1,0:T(8,128)(2,1)S(1)}, bf16[128,640]{1,0:T(8,128)(2,1)}, u32[]{:S(2)}, u32[]{:S(2)}) collective-permute-start(bf16[128,640]{1,0:T(8,128)(2,1)S(1)} %collective-permute-done.10.refs_2_), channel_id=1, source_target_pairs={{0,2},{2,4},{4,6},{6,8},{8,10},{10,12},{12,14},{14,0},{1,3},{3,5},... | collective-permute-start | bytes 491528 | tf_op jit(solution)/shard_map/ppermute | solution.py:244
  75.4 8.4 %collective-permute-start.7 = (bf16[128,640]{1,0:T(8,128)(2,1)S(1)}, bf16[128,640]{1,0:T(8,128)(2,1)S(1)}, u32[]{:S(2)}, u32[]{:S(2)}) collective-permute-start(bf16[128,640]{1,0:T(8,128)(2,1)S(1)} %shard_map.153.own_ref), channel_id=1, source_target_pairs={{0,1},{1,0},{2,3},{3,2},{4,5},{5,4},{6,7},{7,6},{8,9},{9,8},{10,11... | collective-permute-start | bytes 491528 | tf_op jit(solution)/shard_map/ppermute | solution.py:310
  78.8 24.6 %collective-permute-start.13 = (bf16[128,640]{1,0:T(8,128)(2,1)}, bf16[128,640]{1,0:T(8,128)(2,1)}, u32[]{:S(2)}, u32[]{:S(2)}) collective-permute-start(bf16[128,640]{1,0:T(8,128)(2,1)} %collective-permute-done.11.refs_3_), channel_id=1, source_target_pairs={{2,0},{4,2},{6,4},{8,6},{10,8},{12,10},{14,12},{0,14},{3,1},{5,3},... | collective-permute-start | bytes 491528 | tf_op jit(solution)/shard_map/ppermute | solution.py:245
  80.9 22.4 %collective-permute-start.14 = (bf16[128,640]{1,0:T(8,128)(2,1)}, bf16[128,640]{1,0:T(8,128)(2,1)}, u32[]{:S(2)}, u32[]{:S(2)}) collective-permute-start(bf16[128,640]{1,0:T(8,128)(2,1)} %collective-permute-done.12.refs_1_), channel_id=1, source_target_pairs={{0,2},{2,4},{4,6},{6,8},{8,10},{10,12},{12,14},{14,0},{1,3},{3,5},... | collective-permute-start | bytes 491528 | tf_op jit(solution)/shard_map/ppermute | solution.py:244
  86.7 13.2 %all-to-all-start.1 = ((f32[8,2,128]{2,1,0:T(2,128)}), f32[8,2,128]{2,1,0:T(2,128)S(1)}, u32[]{:S(2)}, u32[]{:S(2)}) async-start(f32[8,2,128]{2,1,0:T(2,128)} %get-tuple-element.18), calls=%async_computation.1 | async-start | bytes 16384 | tf_op jit(solution)/shard_map/all_to_all | solution.py:263
  92.2 1.4 %copy-start.5 = (bf16[640,1280]{1,0:T(8,128)(2,1)S(1)}, bf16[640,1280]{1,0:T(8,128)(2,1)}, u32[]{:S(2)}) copy-start(bf16[640,1280]{1,0:T(8,128)(2,1)} %refs_4_.7) | copy-start | bytes 4915204
  94.5 5.4 %copy-start.2 = (bf16[1,3,640,640]{3,2,1,0:T(8,128)(2,1)S(1)}, bf16[1,3,640,640]{3,2,1,0:T(8,128)(2,1)}, u32[]{:S(2)}) copy-start(bf16[1,3,640,640]{3,2,1,0:T(8,128)(2,1)} %slice.30.w_ref) | copy-start | bytes 7372804
  94.5 5.4 %copy-start.8 = (bf16[640,640]{1,0:T(8,128)(2,1)S(1)}, bf16[640,640]{1,0:T(8,128)(2,1)}, u32[]{:S(2)}) copy-start(bf16[640,640]{1,0:T(8,128)(2,1)} %q_ref.3) | copy-start | bytes 2457604
  97.0 1.1 copy-start.23
  99.9 1.0 copy-start.17
  100.9 1.0 copy-start.21
  101.8 1.5 %copy-start.6 = (bf16[640,1280]{1,0:T(8,128)(2,1)S(1)}, bf16[640,1280]{1,0:T(8,128)(2,1)}, u32[]{:S(2)}) copy-start(bf16[640,1280]{1,0:T(8,128)(2,1)} %refs_4_.7) | copy-start | bytes 4915204
  101.8 1.8 %copy-start.24 = (bf16[512,1280]{1,0:T(8,128)(2,1)S(1)}, bf16[512,1280]{1,0:T(8,128)(2,1)}, u32[]{:S(2)}) copy-start(bf16[512,1280]{1,0:T(8,128)(2,1)} %copy-done.23) | copy-start | bytes 3932164
  101.8 2.0 %copy-start.30 = (bf16[640,640]{1,0:T(8,128)(2,1)S(1)}, bf16[640,640]{1,0:T(8,128)(2,1)}, u32[]{:S(2)}) copy-start(bf16[640,640]{1,0:T(8,128)(2,1)} %refs_5_.3) | copy-start | bytes 2457604
  103.9 12.0 %copy-start.22 = (f32[1,128,640]{2,1,0:T(8,128)S(1)}, f32[1,128,640]{2,1,0:T(8,128)}, u32[]{:S(2)}) copy-start(f32[1,128,640]{2,1,0:T(8,128)} %copy-done.20) | copy-start | bytes 983044
  108.9 6.9 %collective-permute-start.15 = (bf16[128,640]{1,0:T(8,128)(2,1)S(1)}, bf16[128,640]{1,0:T(8,128)(2,1)S(1)}, u32[]{:S(2)}, u32[]{:S(2)}) collective-permute-start(bf16[128,640]{1,0:T(8,128)(2,1)S(1)} %shard_map.158.own_ref), channel_id=1, source_target_pairs={{0,1},{1,0},{2,3},{3,2},{4,5},{5,4},{6,7},{7,6},{8,9},{9,8},{10,11... | collective-permute-start | bytes 491528 | tf_op jit(solution)/shard_map/ppermute | solution.py:310
  (8 other events, 6.4 us)

commit v2 on v1

v2 whole, which is shorter than its diff:
```python
import functools
import math

import jax
import jax.numpy as jnp
import numpy as np
from jax import lax
from jax.experimental import pallas as pl
from jax.experimental.pallas import tpu as pltpu
from jax.sharding import PartitionSpec as P

HEADS = 10
GROUPS = 32
STEPS = 2
PATCHES = 8
COLS = 128
WIDTH = 640
PAIRS = HEADS // 2
PER_GROUP = WIDTH // GROUPS
BYTES_PER_MICRO = 3.4e6
BF = jnp.bfloat16
F32 = jnp.float32


def alpha_table():
    start, stop = np.float32(0.00085**0.5), np.float32(0.012**0.5)
    betas = np.linspace(start, stop, 1000, dtype=np.float32) ** 2
    return np.cumprod(1.0 - betas.astype(np.float64)).astype(np.float32)


def dot(a, b):
    return jnp.dot(a, b, preferred_element_type=F32)


def dot_exact(a, b):
    high = a.astype(BF)
    rest = a - high.astype(F32)
    mid = rest.astype(BF)
    low = (rest - mid.astype(F32)).astype(BF)
    return dot(high, b) + (dot(mid, b) + dot(low, b))


HBM, FAR, NEAR, VMEM, SCALARS = "hbm", "far", "near", "vmem", "scalars"


class Arriving:
    def __init__(self, source, target, sem):
        self.copy = pltpu.make_async_copy(source, target, sem)
        self.target, self.waiting, self.shape = target, True, target.shape
        self.copy.start()

    def wait(self):
        if self.waiting:
            self.copy.wait()
            self.waiting = False

    def __getitem__(self, index):
        self.wait()
        return self.target[index]


def call(body, outs, *args, scratch=(), after=(), micros=0.1, limit=12):
    args += tuple((one, "token") for one in after)
    count, far = len(args), [i for i, (_, where) in enumerate(args) if where in (HBM, NEAR)]
    leaves, tree = jax.tree.flatten(outs)
    specs = {
        HBM: pl.BlockSpec(memory_space=pl.ANY),
        FAR: pl.BlockSpec(memory_space=pl.ANY),
        NEAR: pl.BlockSpec(memory_space=pl.ANY),
        "token": pl.BlockSpec(memory_space=pl.ANY),
        VMEM: pl.BlockSpec(memory_space=pltpu.VMEM),
        SCALARS: pl.BlockSpec(memory_space=pltpu.SMEM),
    }
    buffers = [pltpu.VMEM(args[i][0].shape, args[i][0].dtype) for i in far]
    if far:
        buffers.append(pltpu.SemaphoreType.DMA((len(far),)))

    def wrapped(*refs):
        ins, rest = list(refs[:count]), list(refs[count:])
        if far:
            held, sem = rest[-len(buffers) : -1], rest[-1]
            rest = rest[: -len(buffers)]
            for k, i in enumerate(far):
                ins[i] = Arriving(ins[i], held[k], sem.at[k])
        body(*ins[: count - len(after)], *rest)
        for i in far:
            ins[i].wait()

    def put(arg, where):
        if where not in (VMEM, HBM, FAR):
            return arg
        return pltpu.with_memory_space_constraint(arg, pltpu.VMEM if where == VMEM else pltpu.HBM)

    return pl.pallas_call(
        wrapped,
        out_shape=jax.tree.unflatten(tree, leaves),
        in_specs=[specs[where] for _, where in args],
        out_specs=jax.tree.unflatten(tree, [specs[VMEM] for _ in leaves]),
        scratch_shapes=list(scratch) + buffers,
        compiler_params=pltpu.CompilerParams(vmem_limit_bytes=limit * 2**20),
        cost_estimate=pl.CostEstimate(
            flops=0, bytes_accessed=int(micros * BYTES_PER_MICRO), transcendentals=0
        ),
    )(*[put(arg, where) for arg, where in args])


def fast(dims, dtype):
    return pltpu.VMEM(dims, dtype)


def later(arrays, after):
    count = len(arrays)
    spec = pl.BlockSpec(memory_space=pl.ANY)
    return list(pl.pallas_call(
        lambda *refs: None,
        out_shape=[shape(one.shape, one.dtype) for one in arrays],
        in_specs=[spec] * (count + len(after)),
        out_specs=[spec] * count,
        input_output_aliases={i: i for i in range(count)},
        cost_estimate=pl.CostEstimate(flops=0, bytes_accessed=0, transcendentals=0),
        compiler_params=pltpu.CompilerParams(vmem_limit_bytes=2**20),
    )(*arrays, *after))


def shape(dims, dtype):
    return jax.ShapeDtypeStruct(dims, dtype)


def group_matrix():
    channel = lax.broadcasted_iota(jnp.int32, (WIDTH, 128), 0)
    group = lax.broadcasted_iota(jnp.int32, (WIDTH, 128), 1)
    inside = (channel >= group * PER_GROUP) & (channel < (group + 1) * PER_GROUP)
    return jnp.where(inside, 1.0, 0.0).astype(BF)


def spread_matrix():
    group = lax.broadcasted_iota(jnp.int32, (128, WIDTH), 0)
    channel = lax.broadcasted_iota(jnp.int32, (128, WIDTH), 1)
    inside = (channel >= group * PER_GROUP) & (channel < (group + 1) * PER_GROUP)
    return jnp.where(inside, 1.0, 0.0).astype(BF)


def local_stats(x):
    gather, spread = group_matrix(), spread_matrix()
    mean_c = jnp.mean(x, axis=0, keepdims=True)
    centered = x - mean_c
    dev_c = jnp.sum(centered * centered, axis=0, keepdims=True)
    wide = lambda row: jnp.broadcast_to(row, (8, row.shape[1]))
    mean_g = dot_exact(wide(mean_c), gather) * (1.0 / PER_GROUP)
    off = wide(mean_c) - dot_exact(mean_g, spread)
    dev_g = dot_exact(wide(dev_c) + COLS * (off * off), gather)
    return jnp.concatenate([mean_g[:1], dev_g[:1]], axis=0)


def load_body(*refs):
    count = (len(refs) - 8) // 2
    sources, small, out_ref = refs[:count], refs[count : count + 6], refs[count + 6]
    targets, sem = refs[count + 7 : -1], refs[-1]
    copies = [
        pltpu.make_async_copy(source, target, sem.at[k])
        for k, (source, target) in enumerate(zip(sources, targets))
    ]
    for copy in copies:
        copy.start()
    prep_body(*small, out_ref)
    for copy in copies:
        copy.wait()


def prep_body(steps_ref, table_ref, scale_ref, embed_ref, gn_ref, ln_ref, out_ref):
    half = WIDTH // 2
    lane = lax.broadcasted_iota(jnp.int32, (1, WIDTH), 1)
    low = lane < half
    index = jnp.where(low, lane, lane - half).astype(F32)
    freqs = jnp.exp(index * (-math.log(10000.0) / half))
    table = table_ref[...]
    places = lax.broadcasted_iota(jnp.int32, table.shape, 0) * 128 + lax.broadcasted_iota(
        jnp.int32, table.shape, 1
    )
    pick = lambda t: jnp.sum(jnp.where(places == t, table, 0.0), keepdims=True)
    steps = [steps_ref[0:1, s : s + 1] for s in range(STEPS + 1)]
    levels = [pick(t) for t in steps]
    row = lambda value: jnp.broadcast_to(value, (1, WIDTH))
    rows = []
    for s in range(STEPS):
        angles = steps[s].astype(F32) * freqs
        wave = jnp.where(low, jnp.cos(angles), jnp.sin(angles))
        rows.append(scale_ref[...].reshape(1, WIDTH) * wave + embed_ref[...])
    rows = [r * jax.nn.sigmoid(r) for r in rows]
    for s in range(STEPS):
        now, after = levels[s], levels[s + 1]
        rows.append(row(jnp.sqrt(after / now)))
        rows.append(
            row(jnp.sqrt(1.0 - after) - jnp.sqrt(after) * jnp.sqrt(1.0 - now) / jnp.sqrt(now))
        )
    rows.append(gn_ref[...].reshape(1, WIDTH))
    rows.append(ln_ref[...].reshape(1, WIDTH))
    for r, value in enumerate(rows):
        out_ref[r : r + 1] = value


GN_ROW, LN_ROW = 3 * STEPS, 3 * STEPS + 1


def first_body(x_ref, attn_ref, conv_ref, pair_ref, state_ref, stats_ref, sem):
    copies = [
        pltpu.make_async_copy(source, pair_ref.at[pl.ds(k * COLS, COLS)], sem.at[k])
        for k, source in enumerate((attn_ref, conv_ref))
    ]
    for copy in copies:
        copy.start()
    x = x_ref[...]
    state_ref[...] = x
    stats_ref[...] = jnp.broadcast_to(local_stats(x[0])[None], stats_ref.shape)
    for copy in copies:
        copy.wait()


def trim_body(*refs):
    count = len(refs) // 2
    for source, target in zip(refs[:count], refs[count:]):
        target[...] = source[:COLS]


def shifted(x):
    place = lax.broadcasted_iota(jnp.int32, x.shape, 0)
    before = jnp.where(place == 0, 0.0, pltpu.roll(x, 1, 0))
    after = jnp.where(place == COLS - 1, 0.0, pltpu.roll(x, COLS - 1, 0))
    return before, after


def conv_row(x, taps):
    before, after = shifted(x)
    return (
        dot(x.astype(BF), taps[1][...])
        + dot(before.astype(BF), taps[0][...])
        + dot(after.astype(BF), taps[2][...])
    )


def rims_body(place_ref, up_ref, down_ref, w_ref, out_ref):
    above = up_ref[COLS:].astype(F32) * place_ref[0]
    below = down_ref[COLS:].astype(F32) * place_ref[1]
    out_ref[...] = conv_row(above, [w_ref[0, t] for t in range(3)]) + conv_row(
        below, [w_ref[2, t] for t in range(3)]
    )


def level(step, moments, x, rims, prep_ref, taps, q_w):
    mean, dev = moments
    scale = 1.0 / jnp.sqrt(dev * (1.0 / (PATCHES * COLS * PER_GROUP)) + 1e-05)
    rows = jnp.concatenate([jnp.broadcast_to(mean, (8, 128)), jnp.broadcast_to(scale, (8, 128))], axis=0)
    wide = dot_exact(rows, spread_matrix())
    x = x[0]
    normed = (x - wide[0:1]) * (wide[8:9] * prep_ref[GN_ROW : GN_ROW + 1])
    conv_in = normed * jax.nn.sigmoid(normed)
    hidden = x + (conv_row(conv_in, taps) + rims[...]) + prep_ref[step : step + 1]
    mid = jnp.mean(hidden, axis=1, keepdims=True)
    centered = hidden - mid
    var = jnp.mean(centered * centered, axis=1, keepdims=True)
    attn_in = (centered * (1.0 / jnp.sqrt(var + 1e-05)) * prep_ref[LN_ROW : LN_ROW + 1]).astype(BF)
    scale = (WIDTH // HEADS) ** (-0.5) * math.log2(math.e)
    query = (dot(attn_in, q_w[...]) * scale).astype(BF)
    return conv_in.astype(BF), hidden, attn_in, query


def combined(stats):
    mean = sum(stats[p, 0:1] for p in range(PATCHES)) * (1.0 / PATCHES)
    dev = sum(stats[p, 1:2] for p in range(PATCHES))
    for p in range(PATCHES):
        off = stats[p, 0:1] - mean
        dev = dev + (COLS * PER_GROUP) * (off * off)
    return mean, dev


def level_body(stats_ref, x_ref, rims_ref, prep_ref, w_ref, q_ref, pair_ref, h_ref, query_ref):
    taps = [w_ref.at[1, t] for t in range(3)]
    pair_ref[COLS:], h_ref[...], pair_ref[:COLS], query_ref[...] = level(
        0, combined(stats_ref[...]), x_ref[...], rims_ref, prep_ref, taps, q_ref
    )


def keys_of(rows, kv_ref, out_ref):
    out_ref[...] = dot(jnp.concatenate([ref[:COLS] for ref in rows], axis=0), kv_ref[...]).astype(BF)


def keys_body(*refs):
    keys_of(refs[:-2], *refs[-2:])


def attend(query_ref, parts, mixed_ref):
    first_half = lax.broadcasted_iota(jnp.int32, (COLS, 128), 1) < WIDTH // HEADS
    for pair in range(PAIRS):
        lanes = slice(pair * 128, (pair + 1) * 128)
        values = slice(WIDTH + pair * 128, WIDTH + (pair + 1) * 128)
        query = query_ref[:, lanes]
        zero = jnp.zeros_like(query)
        stacked = jnp.concatenate(
            [jnp.where(first_half, query, zero), jnp.where(first_half, zero, query)], axis=0
        )
        scores = [
            lax.dot_general(
                stacked, ref[:, lanes], (((1,), (1,)), ((), ())), preferred_element_type=F32
            )
            for ref in parts
        ]
        top = functools.reduce(jnp.maximum, [jnp.max(s, axis=1, keepdims=True) for s in scores])
        weights = [jnp.exp2(s - top) for s in scores]
        total = sum(jnp.sum(w, axis=1, keepdims=True) for w in weights)
        product = sum(dot(w.astype(BF), ref[:, values]) for w, ref in zip(weights, parts))
        product = product * (1.0 / total)
        mixed_ref[:, lanes] = jnp.where(first_half, product[:COLS], product[COLS:]).astype(BF)


def attend_body(early, late, query_ref, h_ref, *refs):
    parts, rows = refs[:early], refs[early : early + 1 + late]
    kv_ref, out_w_ref, eps_ref, late_ref, mixed_ref = refs[early + 1 + late :]
    keys_of(rows, kv_ref, late_ref)
    attend(query_ref, (*parts, late_ref), mixed_ref)
    eps_ref[...] = (h_ref[...] + dot(mixed_ref[...], out_w_ref[...])).astype(eps_ref.dtype)


def second_body(stats_ref, x_ref, w_ref, rims_ref, prep_ref, q_ref, kv_ref, o_ref, *refs):
    attn_in_ref, h_ref, query_ref, kv_w, out_w, held_ref, sem, more_sem = refs
    taps = {t: Arriving(w_ref.at[1, t], held_ref.at[t], sem.at[t]) for t in (1, 0, 2)}
    copies = [
        pltpu.make_async_copy(source, target, more_sem.at[k])
        for k, (source, target) in enumerate(((kv_ref, kv_w), (o_ref, out_w)))
    ]
    for copy in copies:
        copy.start()
    _, h_ref[...], attn_in_ref[...], query_ref[...] = level(
        1, combined(stats_ref[...]), x_ref[...], rims_ref, prep_ref, taps, q_ref
    )
    for copy in copies:
        copy.wait()


def guide(place_ref, own_ref, other_ref):
    own, other = own_ref[...].astype(F32), other_ref[...].astype(F32)
    first = place_ref[2] == 0.0
    uncond = jnp.where(first, own, other)
    cond = jnp.where(first, other, own)
    return uncond + 3.0 * (cond - uncond)


def update_body(step, place_ref, prep_ref, x_ref, own_ref, other_ref, state_ref, *refs):
    guided = guide(place_ref, own_ref, other_ref)
    prep, row = prep_ref[...], STEPS + 2 * step
    state = prep[row : row + 1] * x_ref[0] + prep[row + 1 : row + 2] * guided
    state_ref[0] = state
    if step + 1 < STEPS:
        refs[0][...] = jnp.broadcast_to(local_stats(state)[None], refs[0].shape)
    else:
        refs[0][0] = guided


def shards(
    latent,
    stale_conv,
    stale_attn,
    cond_embed,
    timesteps,
    gn_gain,
    ln_gain,
    time_scale,
    conv_weight,
    q_weight,
    kv_weight,
    out_weight,
):
    patch, branch = lax.axis_index("patch"), lax.axis_index("cfg")
    place = jnp.stack([patch > 0, patch < PATCHES - 1, branch > 0]).astype(F32)
    upward = [(i, (i + 1) % PATCHES) for i in range(PATCHES)]
    downward = [(target, source) for source, target in upward]
    up = lambda x: lax.ppermute(x, "patch", upward)
    down = lambda x: lax.ppermute(x, "patch", downward)
    full = (COLS, WIDTH)
    whole = (1,) + full
    stats_shape = shape((PATCHES, 2, 128), F32)
    near = lambda arrays: [(one, NEAR) for one in arrays]
    gather_stats = lambda x: lax.all_to_all(x, "patch", 0, 0)

    pair, state, stats = call(
        first_body,
        (fast((2 * COLS, WIDTH), BF), fast(whole, F32), stats_shape),
        (latent, HBM),
        (stale_attn.reshape(full), FAR),
        (stale_conv.reshape(full), FAR),
        scratch=(pltpu.SemaphoreType.DMA((2,)),),
        after=(place,),
    )
    table = np.ones((8, 128), np.float32)
    table.reshape(-1)[:1000] = alpha_table()
    weights = (conv_weight, q_weight, kv_weight, out_weight)
    trim = lambda blocks, after=(): call(
        trim_body,
        tuple(fast(full, BF) for _ in blocks),
        *[(one, VMEM) for one in blocks],
        after=after,
    )

    ring1 = [up(pair), down(pair)]
    stats = gather_stats(stats)
    passing = trim(ring1, (stats,))
    ring2 = [up(passing[0]), down(passing[1])]
    prep, conv_w, q_w, kv_w, out_w = call(
        load_body,
        (fast((8, WIDTH), F32),) + tuple(fast(w.shape, w.dtype) for w in weights),
        *[(w, FAR) for w in weights],
        (timesteps.reshape(1, -1), HBM),
        (jnp.asarray(table), HBM),
        (time_scale, HBM),
        (cond_embed, HBM),
        (gn_gain, HBM),
        (ln_gain, HBM),
        scratch=(pltpu.SemaphoreType.DMA((4,)),),
        after=(stats,),
        limit=2,
    )
    keys = lambda blocks, after=(), micros=0.1: call(
        keys_body,
        fast((len(blocks) * COLS, 2 * WIDTH), BF),
        *near(blocks),
        (kv_w, VMEM),
        after=after,
        micros=micros,
    )
    conv_rims = lambda after=(), micros=0.1: call(
        rims_body,
        fast(full, F32),
        (place, SCALARS),
        *[(one, VMEM) for one in ring1],
        (conv_w, VMEM),
        after=after,
        micros=micros,
    )
    rims = conv_rims()
    ring2 = later(ring2, (prep,))
    ring3 = [up(ring2[0]), down(ring2[1])]
    pair, hidden, query = call(
        level_body,
        (fast((2 * COLS, WIDTH), BF), fast(full, F32), fast(full, BF)),
        (stats, VMEM),
        (state, VMEM),
        (rims, VMEM),
        (prep, VMEM),
        (conv_w, VMEM),
        (q_w, VMEM),
    )
    near_keys = keys(ring1, (rims,))
    ring3 = later(ring3, (near_keys,))
    ring4 = [up(ring3[0])]
    mid_keys = keys(ring2, (ring3[0],))
    far_keys = keys(ring3, (mid_keys,))
    ring1 = [up(pair), down(pair)]
    attend_to = lambda weights, early, late: call(
        functools.partial(attend_body, len(early), len(late)),
        fast(full, BF),
        (query, VMEM),
        (hidden, VMEM),
        *early,
        (pair, VMEM),
        *near(late),
        *[(w, VMEM) for w in weights],
        scratch=(pltpu.VMEM(((1 + len(late)) * COLS, 2 * WIDTH), BF), pltpu.VMEM(full, BF)),
        micros=4.0,
    )
    early = [(one, VMEM) for one in (near_keys, mid_keys, far_keys)]
    eps = attend_to((kv_w, out_w), early, ring4)
    exchange = lambda x: lax.ppermute(x, "cfg", [(0, 1), (1, 0)])
    other = exchange(eps)
    passing = trim(ring1, (eps,))
    ring2 = [up(passing[0]), down(passing[1])]
    near_keys = keys(ring1, (passing[0],), 6.0)
    rims = conv_rims((near_keys,), 6.0)
    state, stats = call(
        functools.partial(update_body, 0),
        (fast(whole, F32), stats_shape),
        (place, SCALARS),
        (prep, VMEM),
        (state, VMEM),
        (eps, VMEM),
        (other, VMEM),
        after=(rims,),
    )
    ring2 = later(ring2, (state,))
    ring3 = [up(ring2[0]), down(ring2[1])]
    stats = gather_stats(stats)
    ring3 = later(ring3, (stats,))
    ring4 = [up(ring3[0])]
    pair, hidden, query, kv_w, out_w = call(
        second_body,
        (fast(full, BF), fast(full, F32), fast(full, BF))
        + tuple(fast(w.shape, w.dtype) for w in weights[2:]),
        (stats, NEAR),
        (state, NEAR),
        (conv_weight, FAR),
        (rims, NEAR),
        (prep, NEAR),
        (q_weight, HBM),
        (kv_weight, FAR),
        (out_weight, FAR),
        scratch=(
            pltpu.VMEM((3, WIDTH, WIDTH), BF),
            pltpu.SemaphoreType.DMA((3,)),
            pltpu.SemaphoreType.DMA((2,)),
        ),
        after=(ring3[0],),
    )
    mid_keys = keys(ring2)
    eps = attend_to((kv_w, out_w), [(near_keys, NEAR), (mid_keys, VMEM)], ring3 + ring4)
    other = exchange(eps)
    return call(
        functools.partial(update_body, 1),
        (shape(whole, F32), shape(whole, F32)),
        (place, SCALARS),
        (prep, VMEM),
        (state, VMEM),
        (eps, VMEM),
        (other, VMEM),
    )


def solution(mesh):
    placed = (
        P(("batch", "patch"), None, None),
        P("cfg", ("batch", "patch"), None, None),
        P("cfg", ("batch", "patch"), None, None),
        P(("batch", "cfg"), None),
        P(),
        P(),
        P(),
        P(),
        P(),
        P(),
        P(),
        P(),
    )
    return jax.shard_map(
        shards,
        mesh=mesh,
        in_specs=placed,
        out_specs=(P(("batch", "patch"), None, None), P(("batch", "patch"), None, None)),
        check_vma=False,
    )
```

time: 118 us -> 95.5 us (0.81)
  local copies, waits for them, and re-layouts: 31.5 us -> 0 us
  blocking collectives: 0 us -> 23.5 us
  between operations: 9.53 us -> 0.87 us
  starting transfers between devices: 35.4 us -> 27.8 us
  other arithmetic: 4.33 us -> 0.08 us
  Pallas kernels: 27.1 us -> 31.1 us
  waiting for transfers between devices: 9.42 us -> 12 us
    all_to_all x0 -> x2, blocking collectives: none -> 23.5 us  [shards(): gather_stats = lambda x: lax.all_to_all(x, 'patch', 0, 0)]
    unnamed x76 -> x0, local copies, waits for them, and re-layouts: 21.8 us -> none
    all_to_all x2 -> x0, starting transfers between devices: 10.1 us -> none  [shards(): stats = lax.all_to_all(stats, 'patch', 0, 0)]
    slice x2 -> x0, local copies, waits for them, and re-layouts: 4.78 us -> none  [the longest x1 3.34 us: shards(): center = conv_weight[1:2]]
    ppermute x2, waiting for transfers between devices: 1.63 us -> 6.1 us  [shards(): exchange = lambda x: lax.ppermute(x, 'cfg', [(0, 1), (1, 0)])]
    pallas_call x11 -> x21, Pallas kernels: 27.1 us -> 31.1 us  [the longest x17 31.1 us: call(): pl.pallas_call(wrapped, out_shape=jax.tree.unflatten(tree, leaves), in_sp...]
    squeeze x4 -> x0, local copies, waits for them, and re-layouts: 3.47 us -> none  [the longest x2 1.85 us: shards(): ups.append(up(ups[0][0]))]
    reduce_sum x1 -> x0, other arithmetic: 2.53 us -> none  [table_pick(): return jnp.sum(jnp.where(places == index, table, jnp.zeros_like(table)))]
  transfers between devices with their start and end apart: 18 -> 16, of which waited for: 5 -> 3; matrix products, arithmetic and copies ran while one was open for 12% -> 0% of each run, Pallas kernels for 16% -> 24%
where the time goes in v2:
time: 95.5 us; the launch traced here: 95.3 us
  Pallas kernels  31.1 us (33%)
  starting transfers between devices  27.8 us (29%)
  blocking collectives  23.5 us (25%)
  waiting for transfers between devices  12 us (13%)
    pallas_call x17, Pallas kernels, call(): pl.pallas_call(wrapped, out_shape=jax.tree.unflatten(tree, leaves), in_sp...  31.1 us
    all_to_all x2, blocking collectives, shards(): gather_stats = lambda x: lax.all_to_all(x, 'patch', 0, 0)  23.5 us
    ppermute x6, starting transfers between devices, shards(): down = lambda x: lax.ppermute(x, 'patch', downward)  19.6 us
    ppermute x2, waiting for transfers between devices, shards(): exchange = lambda x: lax.ppermute(x, 'cfg', [(0, 1), (1, 0)])  6.1 us
    ppermute x8, waiting for transfers between devices, shards(): up = lambda x: lax.ppermute(x, 'patch', upward)  5.88 us
    ppermute x8, starting transfers between devices, shards(): up = lambda x: lax.ppermute(x, 'patch', upward)  4.12 us
    ppermute x2, starting transfers between devices, shards(): exchange = lambda x: lax.ppermute(x, 'cfg', [(0, 1), (1, 0)])  4.1 us
  transfers between devices with their start and end apart: 16, of which 3 were waited for; matrix products, arithmetic and copies ran while one was open for 0% of the time, Pallas kernels for 24%

profile of v2, /device:TPU:2, one launch (start us, length us, event | category | flops | bytes accessed | tf_op | source)
XLA Modules:
  0.0 95.3 jit_solution(4024660621520986575)
XLA Ops:
  0.6 0.1 add_convert_fusion.refs_3_.refs_0_
  0.7 1.8 %shard_map.140 = (bf16[256,640]{1,0:T(8,128)(2,1)S(1)}, f32[1,128,640]{2,1,0:T(8,128)S(1)}, f32[8,2,128]{2,1,0:T(2,128)S(1)}) custom-call(f32[1,128,640]{2,1,0:T(8,128)} %refs_0_.2, bf16[128,640]{1,0:T(8,128)(2,1)} %bitcast.6, bf16[128,640]{1,0:T(8,128)(2,1)} %bitcast.7, f32[3]{0:T(128)S(1)} %add_convert_fusion.refs_3_.refs_0_), custom_call_target="tpu_custom_call" | custom-call | bytes 340000 | tf_op jit(solution)/shard_map/pallas_call | solution.py:94
  2.5 2.0 %collective-permute-start = (bf16[256,640]{1,0:T(8,128)(2,1)S(1)}, bf16[256,640]{1,0:T(8,128)(2,1)S(1)}, u32[]{:S(2)}, u32[]{:S(2)}) collective-permute-start(bf16[256,640]{1,0:T(8,128)(2,1)S(1)} %get-tuple-element.35), channel_id=1, source_target_pairs={{0,2},{2,4},{4,6},{6,8},{8,10},{10,12},{12,14},{14,0},{1,3},{3,5},... | collective-permute-start | bytes 983048 | tf_op jit(solution)/shard_map/ppermute | solution.py:376
  4.5 4.0 %collective-permute-start.1 = (bf16[256,640]{1,0:T(8,128)(2,1)S(1)}, bf16[256,640]{1,0:T(8,128)(2,1)S(1)}, u32[]{:S(2)}, u32[]{:S(2)}) collective-permute-start(bf16[256,640]{1,0:T(8,128)(2,1)S(1)} %get-tuple-element.35), channel_id=1, source_target_pairs={{2,0},{4,2},{6,4},{8,6},{10,8},{12,10},{14,12},{0,14},{3,1},{5,3},... | collective-permute-start | bytes 983048 | tf_op jit(solution)/shard_map/ppermute | solution.py:377
  8.5 13.3 %all_to_all.10.refs_10_.refs_0_.refs_2_ = f32[8,2,128]{2,1,0:T(2,128)S(1)} all-to-all(f32[8,2,128]{2,1,0:T(2,128)S(1)} %get-tuple-element.32), channel_id=1, replica_groups=mesh['batch'=16,'patch'=8,'cfg'=2] {'patch'}, dimensions={0} | all-to-all | bytes 16384 | tf_op jit(solution)/shard_map/all_to_all | solution.py:382
  21.8 0.0 collective-permute-done.refs_1_.refs_0_
  21.8 0.0 collective-permute-done.1.refs_2_.refs_1_
  21.8 0.7 collective-permute-start.2
  22.5 2.7 %collective-permute-start.3 = (bf16[128,640]{1,0:T(8,128)(2,1)S(1)}, bf16[128,640]{1,0:T(8,128)(2,1)S(1)}, u32[]{:S(2)}, u32[]{:S(2)}) collective-permute-start(bf16[128,640]{1,0:T(8,128)(2,1)S(1)} %get-tuple-element.42), channel_id=1, source_target_pairs={{2,0},{4,2},{6,4},{8,6},{10,8},{12,10},{14,12},{0,14},{3,1},{5,3},... | collective-permute-start | bytes 491528 | tf_op jit(solution)/shard_map/ppermute | solution.py:377
  25.1 4.1 %shard_map.141 = (f32[8,640]{1,0:T(8,128)S(1)}, bf16[3,3,640,640]{3,2,1,0:T(8,128)(2,1)S(1)}, bf16[640,640]{1,0:T(8,128)(2,1)S(1)}, bf16[640,1280]{1,0:T(8,128)(2,1)S(1)}, bf16[640,640]{1,0:T(8,128)(2,1)S(1)}) custom-call(bf16[3,3,640,640]{3,2,1,0:T(8,128)(2,1)} %refs_2_.3, bf16[640,640]{1,0:T(8,128)(2,1)} %refs_5_.2, bf16[640,1280]{1,0:T(8,128)(2,1)} %refs_6_.3, ...), custom_call_target="tpu_custom_call" | custom-call | bytes 340000 | tf_op jit(solution)/shard_map/pallas_call | solution.py:94
  29.3 0.0 collective-permute-done.2.refs_0_
  29.3 0.0 collective-permute-done.3.refs_1_
  29.3 0.1 collective-permute-start.4
  29.4 3.2 %collective-permute-start.5 = (bf16[128,640]{1,0:T(8,128)(2,1)S(1)}, bf16[128,640]{1,0:T(8,128)(2,1)S(1)}, u32[]{:S(2)}, u32[]{:S(2)}) collective-permute-start(bf16[128,640]{1,0:T(8,128)(2,1)S(1)} %get-tuple-element.44.refs_1_), channel_id=1, source_target_pairs={{2,0},{4,2},{6,4},{8,6},{10,8},{12,10},{14,12},{0,14},{3,1},{5,3},... | collective-permute-start | bytes 491528 | tf_op jit(solution)/shard_map/ppermute | solution.py:377
  32.6 1.7 %shard_map.142.refs_2_.refs_3_ = f32[128,640]{1,0:T(8,128)S(1)} custom-call(f32[3]{0:T(128)S(1)} %add_convert_fusion.refs_3_.refs_0_, bf16[256,640]{1,0:T(8,128)(2,1)S(1)} %collective-permute-done.refs_1_.refs_0_, bf16[256,640]{1,0:T(8,128)(2,1)S(1)} %collective-permute-done.1.refs_2_.refs_1_, bf16[3,3,640,640]{3,2,1,0:T(8,128)(2,1)S(1)} %get-tuple-element.36.refs_3_.refs_4_), custom_call_target="tpu_custom_call" | custom-call | bytes 340000 | tf_op jit(solution)/shard_map/pallas_call | solution.py:94
  34.3 1.4 %shard_map.143 = (bf16[256,640]{1,0:T(8,128)(2,1)S(1)}, f32[128,640]{1,0:T(8,128)S(1)}, bf16[128,640]{1,0:T(8,128)(2,1)S(1)}) custom-call(f32[8,2,128]{2,1,0:T(2,128)S(1)} %all_to_all.10.refs_10_.refs_0_.refs_2_, f32[1,128,640]{2,1,0:T(8,128)S(1)} %get-tuple-element.34.refs_1_.refs_2_, f32[128,640]{1,0:T(8,128)S(1)} %shard_map.142.refs_2_.refs_3_, ...), custom_call_target="tpu_custom_call" | custom-call | bytes 340000 | tf_op jit(solution)/shard_map/pallas_call | solution.py:94
  35.7 0.1 collective-permute-start.8
  35.8 3.2 %collective-permute-start.9 = (bf16[256,640]{1,0:T(8,128)(2,1)S(1)}, bf16[256,640]{1,0:T(8,128)(2,1)S(1)}, u32[]{:S(2)}, u32[]{:S(2)}) collective-permute-start(bf16[256,640]{1,0:T(8,128)(2,1)S(1)} %get-tuple-element.47.refs_5_), channel_id=1, source_target_pairs={{2,0},{4,2},{6,4},{8,6},{10,8},{12,10},{14,12},{0,14},{3,1},{5,3},... | collective-permute-start | bytes 983048 | tf_op jit(solution)/shard_map/ppermute | solution.py:377
  39.0 0.9 shard_map.144.refs_2_
  39.9 0.0 collective-permute-done.4.refs_0_
  39.9 0.3 collective-permute-start.6
  40.2 1.1 %shard_map.148.refs_3_ = bf16[256,1280]{1,0:T(8,128)(2,1)S(1)} custom-call(bf16[128,640]{1,0:T(8,128)(2,1)S(1)} %get-tuple-element.43.refs_0_, bf16[128,640]{1,0:T(8,128)(2,1)S(1)} %get-tuple-element.44.refs_1_, bf16[640,1280]{1,0:T(8,128)(2,1)S(1)} %get-tuple-element.40.refs_2_.refs_7_, bf16[128,640]{1,0:T(8,128)(2,1)S(1)} %get-tuple-element.45.refs_3_.refs_0_), custom_call_target="tpu_custom_call" | custom-call | bytes 340000 | tf_op jit(solution)/shard_map/pallas_call | solution.py:94
  41.4 1.1 %shard_map.149.refs_4_ = bf16[256,1280]{1,0:T(8,128)(2,1)S(1)} custom-call(bf16[128,640]{1,0:T(8,128)(2,1)S(1)} %get-tuple-element.45.refs_3_.refs_0_, bf16[128,640]{1,0:T(8,128)(2,1)S(1)} %get-tuple-element.46.refs_1_, bf16[640,1280]{1,0:T(8,128)(2,1)S(1)} %get-tuple-element.40.refs_2_.refs_7_, bf16[256,1280]{1,0:T(8,128)(2,1)S(1)} %shard_map.148.refs_3_), custom_call_target="tpu_custom_call" | custom-call | bytes 340000 | tf_op jit(solution)/shard_map/pallas_call | solution.py:94
  42.5 4.7 %collective-permute-done.6.refs_6_ = bf16[128,640]{1,0:T(8,128)(2,1)S(1)} collective-permute-done((bf16[128,640]{1,0:T(8,128)(2,1)S(1)}, bf16[128,640]{1,0:T(8,128)(2,1)S(1)}, u32[]{:S(2)}, u32[]{:S(2)}) %collective-permute-start.6) | collective-permute-done | bytes 163872 | tf_op jit(solution)/shard_map/ppermute | solution.py:376
  47.2 3.5 %shard_map.150.refs_2_.refs_3_ = bf16[128,640]{1,0:T(8,128)(2,1)S(1)} custom-call(bf16[128,640]{1,0:T(8,128)(2,1)S(1)} %get-tuple-element.38.refs_0_, f32[128,640]{1,0:T(8,128)S(1)} %get-tuple-element.39.refs_1_, bf16[256,1280]{1,0:T(8,128)(2,1)S(1)} %shard_map.144.refs_2_, bf16[256,1280]{1,0:T(8,128)(2,1)S(1)} %shard_map.148.refs_3_, ...), custom_call_target="tpu_custom_call" | custom-call | bytes 13600000 | tf_op jit(solution)/shard_map/pallas_call | solution.py:94
  50.7 3.3 %collective-permute-start.7 = (bf16[128,640]{1,0:T(8,128)(2,1)S(1)}, bf16[128,640]{1,0:T(8,128)(2,1)S(1)}, u32[]{:S(2)}, u32[]{:S(2)}) collective-permute-start(bf16[128,640]{1,0:T(8,128)(2,1)S(1)} %shard_map.150.refs_2_.refs_3_), channel_id=1, source_target_pairs={{0,1},{1,0},{2,3},{3,2},{4,5},{5,4},{6,7},{7,6},{8,9},{9,8},{10,11... | collective-permute-start | bytes 491528 | tf_op jit(solution)/shard_map/ppermute | solution.py:471
  54.0 0.0 collective-permute-done.8.refs_0_.refs_1_
  54.0 0.0 collective-permute-done.9.refs_1_.refs_2_
  54.1 0.1 collective-permute-start.10
  54.1 3.2 %collective-permute-start.11 = (bf16[128,640]{1,0:T(8,128)(2,1)S(1)}, bf16[128,640]{1,0:T(8,128)(2,1)S(1)}, u32[]{:S(2)}, u32[]{:S(2)}) collective-permute-start(bf16[128,640]{1,0:T(8,128)(2,1)S(1)} %get-tuple-element.52), channel_id=1, source_target_pairs={{2,0},{4,2},{6,4},{8,6},{10,8},{12,10},{14,12},{0,14},{3,1},{5,3},... | collective-permute-start | bytes 491528 | tf_op jit(solution)/shard_map/ppermute | solution.py:377
  57.4 0.9 shard_map.152.refs_4_.refs_2_
  58.3 1.7 %shard_map.153.refs_5_.refs_3_ = f32[128,640]{1,0:T(8,128)S(1)} custom-call(f32[3]{0:T(128)S(1)} %add_convert_fusion.refs_3_.refs_0_, bf16[256,640]{1,0:T(8,128)(2,1)S(1)} %collective-permute-done.8.refs_0_.refs_1_, bf16[256,640]{1,0:T(8,128)(2,1)S(1)} %collective-permute-done.9.refs_1_.refs_2_, ...), custom_call_target="tpu_custom_call" | custom-call | bytes 20400000 | tf_op jit(solution)/shard_map/pallas_call | solution.py:94
  60.0 1.3 %shard_map.154 = (f32[1,128,640]{2,1,0:T(8,128)S(1)}, f32[8,2,128]{2,1,0:T(2,128)S(1)}) custom-call(f32[3]{0:T(128)S(1)} %add_convert_fusion.refs_3_.refs_0_, f32[8,640]{1,0:T(8,128)S(1)} %get-tuple-element.33.refs_3_.refs_2_.refs_1_.refs_4_, f32[1,128,640]{2,1,0:T(8,128)S(1)} %get-tuple-element.34.refs_1_.refs_2_, ...), custom_call_target="tpu_custom_call" | custom-call | bytes 340000 | tf_op jit(solution)/shard_map/pallas_call | solution.py:94
  61.3 0.0 collective-permute-done.10.refs_0_
  61.3 0.0 collective-permute-done.11.refs_1_
  61.4 0.1 collective-permute-start.12
  61.4 3.2 %collective-permute-start.13 = (bf16[128,640]{1,0:T(8,128)(2,1)S(1)}, bf16[128,640]{1,0:T(8,128)(2,1)S(1)}, u32[]{:S(2)}, u32[]{:S(2)}) collective-permute-start(bf16[128,640]{1,0:T(8,128)(2,1)S(1)} %get-tuple-element.54.refs_1_), channel_id=1, source_target_pairs={{2,0},{4,2},{6,4},{8,6},{10,8},{12,10},{14,12},{0,14},{3,1},{5,3},... | collective-permute-start | bytes 491528 | tf_op jit(solution)/shard_map/ppermute | solution.py:377
  64.7 10.2 %all_to_all.11.refs_2_.refs_0_ = f32[8,2,128]{2,1,0:T(2,128)S(1)} all-to-all(f32[8,2,128]{2,1,0:T(2,128)S(1)} %get-tuple-element.51), channel_id=1, replica_groups=mesh['batch'=16,'patch'=8,'cfg'=2] {'patch'}, dimensions={0} | all-to-all | bytes 16384 | tf_op jit(solution)/shard_map/all_to_all | solution.py:382
  74.9 0.0 collective-permute-done.12.refs_0_
  74.9 0.0 collective-permute-done.13.refs_1_
  74.9 0.9 collective-permute-start.14
  75.7 3.6 %shard_map.157 = (bf16[128,640]{1,0:T(8,128)(2,1)S(1)}, f32[128,640]{1,0:T(8,128)S(1)}, bf16[128,640]{1,0:T(8,128)(2,1)S(1)}, bf16[640,1280]{1,0:T(8,128)(2,1)S(1)}, bf16[640,640]{1,0:T(8,128)(2,1)S(1)}) custom-call(f32[8,2,128]{2,1,0:T(2,128)S(1)} %all_to_all.11.refs_2_.refs_0_, f32[1,128,640]{2,1,0:T(8,128)S(1)} %get-tuple-element.50.refs_2_.refs_1_, ...), custom_call_target="tpu_custom_call" | custom-call | bytes 340000 | tf_op jit(solution)/shard_map/pallas_call | solution.py:94
  79.4 1.1 %shard_map.158.refs_3_ = bf16[256,1280]{1,0:T(8,128)(2,1)S(1)} custom-call(bf16[128,640]{1,0:T(8,128)(2,1)S(1)} %get-tuple-element.53.refs_0_, bf16[128,640]{1,0:T(8,128)(2,1)S(1)} %get-tuple-element.54.refs_1_, bf16[640,1280]{1,0:T(8,128)(2,1)S(1)} %get-tuple-element.58.refs_2_.refs_8_), custom_call_target="tpu_custom_call" | custom-call | bytes 340000 | tf_op jit(solution)/shard_map/pallas_call | solution.py:94
  80.5 1.2 %collective-permute-done.14.refs_7_ = bf16[128,640]{1,0:T(8,128)(2,1)S(1)} collective-permute-done((bf16[128,640]{1,0:T(8,128)(2,1)S(1)}, bf16[128,640]{1,0:T(8,128)(2,1)S(1)}, u32[]{:S(2)}, u32[]{:S(2)}) %collective-permute-start.14) | collective-permute-done | bytes 163872 | tf_op jit(solution)/shard_map/ppermute | solution.py:376
  81.7 5.2 %shard_map.159.refs_3_ = bf16[128,640]{1,0:T(8,128)(2,1)S(1)} custom-call(bf16[128,640]{1,0:T(8,128)(2,1)S(1)} %get-tuple-element.56.refs_0_, f32[128,640]{1,0:T(8,128)S(1)} %get-tuple-element.57.refs_1_, bf16[256,1280]{1,0:T(8,128)(2,1)S(1)} %shard_map.152.refs_4_.refs_2_, bf16[256,1280]{1,0:T(8,128)(2,1)S(1)} %shard_map.158.refs_3_, ...), custom_call_target="tpu_custom_call" | custom-call | bytes 13600000 | tf_op jit(solution)/shard_map/pallas_call | solution.py:94
  86.9 0.8 collective-permute-start.15
  87.7 6.1 %collective-permute-done.15.refs_4_ = bf16[128,640]{1,0:T(8,128)(2,1)S(1)} collective-permute-done((bf16[128,640]{1,0:T(8,128)(2,1)S(1)}, bf16[128,640]{1,0:T(8,128)(2,1)S(1)}, u32[]{:S(2)}, u32[]{:S(2)}) %collective-permute-start.15) | collective-permute-done | bytes 163872 | tf_op jit(solution)/shard_map/ppermute | solution.py:471
  93.8 1.5 %shard_map.160 = (f32[1,128,640]{2,1,0:T(8,128)}, f32[1,128,640]{2,1,0:T(8,128)}) custom-call(f32[3]{0:T(128)S(1)} %add_convert_fusion.refs_3_.refs_0_, f32[8,640]{1,0:T(8,128)S(1)} %get-tuple-element.33.refs_3_.refs_2_.refs_1_.refs_4_, f32[1,128,640]{2,1,0:T(8,128)S(1)} %get-tuple-element.50.refs_2_.refs_1_, bf16[128,640]{1,0:T(8,128)(2,1)S(1)} %shard_map.159.refs_3_, ...), custom_call_target="tpu_custom_call" | custom-call | bytes 340000 | tf_op jit(solution)/shard_map/pallas_call | solution.py:94
  (8 shorter events, 0.1 us)
Async XLA Ops:
  2.5 19.3 %collective-permute-start = (bf16[256,640]{1,0:T(8,128)(2,1)S(1)}, bf16[256,640]{1,0:T(8,128)(2,1)S(1)}, u32[]{:S(2)}, u32[]{:S(2)}) collective-permute-start(bf16[256,640]{1,0:T(8,128)(2,1)S(1)} %get-tuple-element.35), channel_id=1, source_target_pairs={{0,2},{2,4},{4,6},{6,8},{8,10},{10,12},{12,14},{14,0},{1,3},{3,5},... | collective-permute-start | bytes 983048 | tf_op jit(solution)/shard_map/ppermute | solution.py:376
  4.5 17.3 %collective-permute-start.1 = (bf16[256,640]{1,0:T(8,128)(2,1)S(1)}, bf16[256,640]{1,0:T(8,128)(2,1)S(1)}, u32[]{:S(2)}, u32[]{:S(2)}) collective-permute-start(bf16[256,640]{1,0:T(8,128)(2,1)S(1)} %get-tuple-element.35), channel_id=1, source_target_pairs={{2,0},{4,2},{6,4},{8,6},{10,8},{12,10},{14,12},{0,14},{3,1},{5,3},... | collective-permute-start | bytes 983048 | tf_op jit(solution)/shard_map/ppermute | solution.py:377
  21.8 7.4 %collective-permute-start.2 = (bf16[128,640]{1,0:T(8,128)(2,1)S(1)}, bf16[128,640]{1,0:T(8,128)(2,1)S(1)}, u32[]{:S(2)}, u32[]{:S(2)}) collective-permute-start(bf16[128,640]{1,0:T(8,128)(2,1)S(1)} %get-tuple-element.41), channel_id=1, source_target_pairs={{0,2},{2,4},{4,6},{6,8},{8,10},{10,12},{12,14},{14,0},{1,3},{3,5},... | collective-permute-start | bytes 491528 | tf_op jit(solution)/shard_map/ppermute | solution.py:376
  22.5 6.8 %collective-permute-start.3 = (bf16[128,640]{1,0:T(8,128)(2,1)S(1)}, bf16[128,640]{1,0:T(8,128)(2,1)S(1)}, u32[]{:S(2)}, u32[]{:S(2)}) collective-permute-start(bf16[128,640]{1,0:T(8,128)(2,1)S(1)} %get-tuple-element.42), channel_id=1, source_target_pairs={{2,0},{4,2},{6,4},{8,6},{10,8},{12,10},{14,12},{0,14},{3,1},{5,3},... | collective-permute-start | bytes 491528 | tf_op jit(solution)/shard_map/ppermute | solution.py:377
  29.3 10.6 %collective-permute-start.4 = (bf16[128,640]{1,0:T(8,128)(2,1)S(1)}, bf16[128,640]{1,0:T(8,128)(2,1)S(1)}, u32[]{:S(2)}, u32[]{:S(2)}) collective-permute-start(bf16[128,640]{1,0:T(8,128)(2,1)S(1)} %get-tuple-element.43.refs_0_), channel_id=1, source_target_pairs={{0,2},{2,4},{4,6},{6,8},{8,10},{10,12},{12,14},{14,0},{1,3},{3,5},... | collective-permute-start | bytes 491528 | tf_op jit(solution)/shard_map/ppermute | solution.py:376
  29.4 10.5 %collective-permute-start.5 = (bf16[128,640]{1,0:T(8,128)(2,1)S(1)}, bf16[128,640]{1,0:T(8,128)(2,1)S(1)}, u32[]{:S(2)}, u32[]{:S(2)}) collective-permute-start(bf16[128,640]{1,0:T(8,128)(2,1)S(1)} %get-tuple-element.44.refs_1_), channel_id=1, source_target_pairs={{2,0},{4,2},{6,4},{8,6},{10,8},{12,10},{14,12},{0,14},{3,1},{5,3},... | collective-permute-start | bytes 491528 | tf_op jit(solution)/shard_map/ppermute | solution.py:377
  35.7 18.3 %collective-permute-start.8 = (bf16[256,640]{1,0:T(8,128)(2,1)S(1)}, bf16[256,640]{1,0:T(8,128)(2,1)S(1)}, u32[]{:S(2)}, u32[]{:S(2)}) collective-permute-start(bf16[256,640]{1,0:T(8,128)(2,1)S(1)} %get-tuple-element.47.refs_5_), channel_id=1, source_target_pairs={{0,2},{2,4},{4,6},{6,8},{8,10},{10,12},{12,14},{14,0},{1,3},{3,5},... | collective-permute-start | bytes 983048 | tf_op jit(solution)/shard_map/ppermute | solution.py:376
  35.8 18.3 %collective-permute-start.9 = (bf16[256,640]{1,0:T(8,128)(2,1)S(1)}, bf16[256,640]{1,0:T(8,128)(2,1)S(1)}, u32[]{:S(2)}, u32[]{:S(2)}) collective-permute-start(bf16[256,640]{1,0:T(8,128)(2,1)S(1)} %get-tuple-element.47.refs_5_), channel_id=1, source_target_pairs={{2,0},{4,2},{6,4},{8,6},{10,8},{12,10},{14,12},{0,14},{3,1},{5,3},... | collective-permute-start | bytes 983048 | tf_op jit(solution)/shard_map/ppermute | solution.py:377
  39.9 7.2 %collective-permute-start.6 = (bf16[128,640]{1,0:T(8,128)(2,1)S(1)}, bf16[128,640]{1,0:T(8,128)(2,1)S(1)}, u32[]{:S(2)}, u32[]{:S(2)}) collective-permute-start(bf16[128,640]{1,0:T(8,128)(2,1)S(1)} %get-tuple-element.45.refs_3_.refs_0_), channel_id=1, source_target_pairs={{0,2},{2,4},{4,6},{6,8},{8,10},{10,12},{12,14},{14,0},{1,3},{3,5},... | collective-permute-start | bytes 491528 | tf_op jit(solution)/shard_map/ppermute | solution.py:376
  50.7 9.2 %collective-permute-start.7 = (bf16[128,640]{1,0:T(8,128)(2,1)S(1)}, bf16[128,640]{1,0:T(8,128)(2,1)S(1)}, u32[]{:S(2)}, u32[]{:S(2)}) collective-permute-start(bf16[128,640]{1,0:T(8,128)(2,1)S(1)} %shard_map.150.refs_2_.refs_3_), channel_id=1, source_target_pairs={{0,1},{1,0},{2,3},{3,2},{4,5},{5,4},{6,7},{7,6},{8,9},{9,8},{10,11... | collective-permute-start | bytes 491528 | tf_op jit(solution)/shard_map/ppermute | solution.py:471
  54.1 7.3 %collective-permute-start.10 = (bf16[128,640]{1,0:T(8,128)(2,1)S(1)}, bf16[128,640]{1,0:T(8,128)(2,1)S(1)}, u32[]{:S(2)}, u32[]{:S(2)}) collective-permute-start(bf16[128,640]{1,0:T(8,128)(2,1)S(1)} %get-tuple-element.49.refs_3_), channel_id=1, source_target_pairs={{0,2},{2,4},{4,6},{6,8},{8,10},{10,12},{12,14},{14,0},{1,3},{3,5},... | collective-permute-start | bytes 491528 | tf_op jit(solution)/shard_map/ppermute | solution.py:376
  54.1 7.2 %collective-permute-start.11 = (bf16[128,640]{1,0:T(8,128)(2,1)S(1)}, bf16[128,640]{1,0:T(8,128)(2,1)S(1)}, u32[]{:S(2)}, u32[]{:S(2)}) collective-permute-start(bf16[128,640]{1,0:T(8,128)(2,1)S(1)} %get-tuple-element.52), channel_id=1, source_target_pairs={{2,0},{4,2},{6,4},{8,6},{10,8},{12,10},{14,12},{0,14},{3,1},{5,3},... | collective-permute-start | bytes 491528 | tf_op jit(solution)/shard_map/ppermute | solution.py:377
  61.4 13.5 %collective-permute-start.12 = (bf16[128,640]{1,0:T(8,128)(2,1)S(1)}, bf16[128,640]{1,0:T(8,128)(2,1)S(1)}, u32[]{:S(2)}, u32[]{:S(2)}) collective-permute-start(bf16[128,640]{1,0:T(8,128)(2,1)S(1)} %get-tuple-element.53.refs_0_), channel_id=1, source_target_pairs={{0,2},{2,4},{4,6},{6,8},{8,10},{10,12},{12,14},{14,0},{1,3},{3,5},... | collective-permute-start | bytes 491528 | tf_op jit(solution)/shard_map/ppermute | solution.py:376
  61.4 13.4 %collective-permute-start.13 = (bf16[128,640]{1,0:T(8,128)(2,1)S(1)}, bf16[128,640]{1,0:T(8,128)(2,1)S(1)}, u32[]{:S(2)}, u32[]{:S(2)}) collective-permute-start(bf16[128,640]{1,0:T(8,128)(2,1)S(1)} %get-tuple-element.54.refs_1_), channel_id=1, source_target_pairs={{2,0},{4,2},{6,4},{8,6},{10,8},{12,10},{14,12},{0,14},{3,1},{5,3},... | collective-permute-start | bytes 491528 | tf_op jit(solution)/shard_map/ppermute | solution.py:377
  74.9 6.8 %collective-permute-start.14 = (bf16[128,640]{1,0:T(8,128)(2,1)S(1)}, bf16[128,640]{1,0:T(8,128)(2,1)S(1)}, u32[]{:S(2)}, u32[]{:S(2)}) collective-permute-start(bf16[128,640]{1,0:T(8,128)(2,1)S(1)} %get-tuple-element.55.refs_8_.refs_5_), channel_id=1, source_target_pairs={{0,2},{2,4},{4,6},{6,8},{8,10},{10,12},{12,14},{14,0},{1,3},{3,5},... | collective-permute-start | bytes 491528 | tf_op jit(solution)/shard_map/ppermute | solution.py:376
  86.9 6.9 %collective-permute-start.15 = (bf16[128,640]{1,0:T(8,128)(2,1)S(1)}, bf16[128,640]{1,0:T(8,128)(2,1)S(1)}, u32[]{:S(2)}, u32[]{:S(2)}) collective-permute-start(bf16[128,640]{1,0:T(8,128)(2,1)S(1)} %shard_map.159.refs_3_), channel_id=1, source_target_pairs={{0,1},{1,0},{2,3},{3,2},{4,5},{5,4},{6,7},{7,6},{8,9},{9,8},{10,11... | collective-permute-start | bytes 491528 | tf_op jit(solution)/shard_map/ppermute | solution.py:471

commit v3 on v2

--- a/solution.py
+++ b/solution.py
@@ -200,26 +200,77 @@
 
 
 GN_ROW, LN_ROW = 3 * STEPS, 3 * STEPS + 1
-
-
-def first_body(x_ref, attn_ref, conv_ref, pair_ref, state_ref, stats_ref, sem):
+EXTRA = 16
+HEAD = COLS + EXTRA
+
+
+def stats_rows(stats):
+    parts = []
+    for _ in range(3):
+        part = stats.astype(BF).astype(F32)
+        parts.append(part)
+        stats = stats - part
+    rows = jnp.concatenate(parts + [jnp.zeros((EXTRA - 6, 128), F32)], axis=0)
+    return jnp.concatenate([rows, jnp.zeros((EXTRA, WIDTH - 128), F32)], axis=1).astype(BF)
+
+
+def stats_of(block_ref):
+    rows = block_ref[COLS:HEAD, :128].astype(F32)
+    return rows[0:2] + rows[2:4] + rows[4:6]
+
+
+def merge(one, other):
+    (count_a, mean_a, dev_a), (count_b, mean_b, dev_b) = one, other
+    count, off = count_a + count_b, mean_b - mean_a
+    scale = COLS * PER_GROUP * count_a * count_b / count
+    return count, mean_a + off * (count_b / count), dev_a + dev_b + scale * (off * off)
+
+
+def patches(count, stats):
+    return count, stats[0:1], stats[1:2]
+
+
+def first_body(x_ref, attn_ref, conv_ref, block_ref, state_ref, stats_ref, sem):
+    places = ((attn_ref, 0), (conv_ref, HEAD))
     copies = [
-        pltpu.make_async_copy(source, pair_ref.at[pl.ds(k * COLS, COLS)], sem.at[k])
-        for k, source in enumerate((attn_ref, conv_ref))
+        pltpu.make_async_copy(source, block_ref.at[pl.ds(start, COLS)], sem.at[k])
+        for k, (source, start) in enumerate(places)
     ]
     for copy in copies:
         copy.start()
     x = x_ref[...]
     state_ref[...] = x
-    stats_ref[...] = jnp.broadcast_to(local_stats(x[0])[None], stats_ref.shape)
+    stats = local_stats(x[0])
+    stats_ref[0:2] = stats
+    block_ref[COLS:HEAD] = stats_rows(stats)
     for copy in copies:
         copy.wait()
 
 
-def trim_body(*refs):
+def join_body(low_ref, up_ref, down_ref, up_block_ref, down_block_ref):
+    for source, target in ((up_ref, up_block_ref), (down_ref, down_block_ref)):
+        target[:COLS] = source[...]
+        target[COLS:] = low_ref[...]
+
+
+def pack_body(stats_ref, up_ref, down_ref, up_block_ref, down_block_ref):
+    rows = stats_rows(stats_ref[0:2])
+    for source, target in ((up_ref, up_block_ref), (down_ref, down_block_ref)):
+        target[:COLS] = source[:COLS]
+        target[COLS:] = rows
+
+
+def partial_body(mine_ref, up_ref, down_ref, three_ref, two_ref):
+    two = merge(patches(1, stats_of(up_ref)), patches(1, mine_ref[0:2]))
+    three = merge(two, patches(1, stats_of(down_ref)))
+    for (_, mean, dev), target in ((three, three_ref), (two, two_ref)):
+        target[0:1], target[1:2] = mean, dev
+
+
+def trim_body(rows, *refs):
     count = len(refs) // 2
     for source, target in zip(refs[:count], refs[count:]):
-        target[...] = source[:COLS]
+        target[...] = source[:rows]
 
 
 def shifted(x):
@@ -238,16 +289,16 @@
     )
 
 
-def rims_body(place_ref, up_ref, down_ref, w_ref, out_ref):
-    above = up_ref[COLS:].astype(F32) * place_ref[0]
-    below = down_ref[COLS:].astype(F32) * place_ref[1]
+def rims_body(start, place_ref, up_ref, down_ref, w_ref, out_ref):
+    above = up_ref[start : start + COLS].astype(F32) * place_ref[0]
+    below = down_ref[start : start + COLS].astype(F32) * place_ref[1]
     out_ref[...] = conv_row(above, [w_ref[0, t] for t in range(3)]) + conv_row(
         below, [w_ref[2, t] for t in range(3)]
     )
 
 
 def level(step, moments, x, rims, prep_ref, taps, q_w):
-    mean, dev = moments
+    _, mean, dev = moments
     scale = 1.0 / jnp.sqrt(dev * (1.0 / (PATCHES * COLS * PER_GROUP)) + 1e-05)
     rows = jnp.concatenate([jnp.broadcast_to(mean, (8, 128)), jnp.broadcast_to(scale, (8, 128))], axis=0)
     wide = dot_exact(rows, spread_matrix())
@@ -264,19 +315,14 @@
     return conv_in.astype(BF), hidden, attn_in, query
 
 
-def combined(stats):
-    mean = sum(stats[p, 0:1] for p in range(PATCHES)) * (1.0 / PATCHES)
-    dev = sum(stats[p, 1:2] for p in range(PATCHES))
-    for p in range(PATCHES):
-        off = stats[p, 0:1] - mean
-        dev = dev + (COLS * PER_GROUP) * (off * off)
-    return mean, dev
-
-
-def level_body(stats_ref, x_ref, rims_ref, prep_ref, w_ref, q_ref, pair_ref, h_ref, query_ref):
+def level_body(x_ref, rims_ref, prep_ref, w_ref, q_ref, *refs):
+    opposite_ref, conv_in_ref, h_ref, attn_in_ref, query_ref = refs[PATCHES - 1 :]
+    total = patches(1, opposite_ref[0:2])
+    for ref in refs[: PATCHES - 1]:
+        total = merge(total, patches(1, stats_of(ref)))
     taps = [w_ref.at[1, t] for t in range(3)]
-    pair_ref[COLS:], h_ref[...], pair_ref[:COLS], query_ref[...] = level(
-        0, combined(stats_ref[...]), x_ref[...], rims_ref, prep_ref, taps, q_ref
+    conv_in_ref[...], h_ref[...], attn_in_ref[...], query_ref[...] = level(
+        0, total, x_ref[...], rims_ref, prep_ref, taps, q_ref
     )
 
 
@@ -320,20 +366,16 @@
     eps_ref[...] = (h_ref[...] + dot(mixed_ref[...], out_w_ref[...])).astype(eps_ref.dtype)
 
 
-def second_body(stats_ref, x_ref, w_ref, rims_ref, prep_ref, q_ref, kv_ref, o_ref, *refs):
-    attn_in_ref, h_ref, query_ref, kv_w, out_w, held_ref, sem, more_sem = refs
-    taps = {t: Arriving(w_ref.at[1, t], held_ref.at[t], sem.at[t]) for t in (1, 0, 2)}
-    copies = [
-        pltpu.make_async_copy(source, target, more_sem.at[k])
-        for k, (source, target) in enumerate(((kv_ref, kv_w), (o_ref, out_w)))
-    ]
-    for copy in copies:
-        copy.start()
+def second_body(
+    three_ref, before_ref, after_ref, x_ref, rims_ref, prep_ref, w_ref, q_ref, *refs
+):
+    attn_in_ref, h_ref, query_ref = refs
+    total = merge(patches(3, three_ref[0:2]), patches(2, after_ref[0:2]))
+    total = merge(total, patches(3, before_ref[0:2]))
+    taps = [w_ref.at[1, t] for t in range(3)]
     _, h_ref[...], attn_in_ref[...], query_ref[...] = level(
-        1, combined(stats_ref[...]), x_ref[...], rims_ref, prep_ref, taps, q_ref
-    )
-    for copy in copies:
-        copy.wait()
+        1, total, x_ref[...], rims_ref, prep_ref, taps, q_ref
+    )
 
 
 def guide(place_ref, own_ref, other_ref):
@@ -350,7 +392,7 @@
     state = prep[row : row + 1] * x_ref[0] + prep[row + 1 : row + 2] * guided
     state_ref[0] = state
     if step + 1 < STEPS:
-        refs[0][...] = jnp.broadcast_to(local_stats(state)[None], refs[0].shape)
+        refs[0][0:2] = local_stats(state)
     else:
         refs[0][0] = guided
 
@@ -377,13 +419,15 @@
     down = lambda x: lax.ppermute(x, "patch", downward)
     full = (COLS, WIDTH)
     whole = (1,) + full
-    stats_shape = shape((PATCHES, 2, 128), F32)
+    stats_shape = fast((8, 128), F32)
     near = lambda arrays: [(one, NEAR) for one in arrays]
-    gather_stats = lambda x: lax.all_to_all(x, "patch", 0, 0)
-
-    pair, state, stats = call(
+    shift = lambda x, far: lax.ppermute(
+        x, "patch", [(i, (i + far) % PATCHES) for i in range(PATCHES)]
+    )
+
+    first, state, opposite = call(
         first_body,
-        (fast((2 * COLS, WIDTH), BF), fast(whole, F32), stats_shape),
+        (fast((HEAD + COLS, WIDTH), BF), fast(whole, F32), fast((8, 128), F32)),
         (latent, HBM),
         (stale_attn.reshape(full), FAR),
         (stale_conv.reshape(full), FAR),
@@ -393,17 +437,15 @@
     table = np.ones((8, 128), np.float32)
     table.reshape(-1)[:1000] = alpha_table()
     weights = (conv_weight, q_weight, kv_weight, out_weight)
-    trim = lambda blocks, after=(): call(
-        trim_body,
-        tuple(fast(full, BF) for _ in blocks),
+    trim = lambda rows, blocks, after=(): call(
+        functools.partial(trim_body, rows),
+        tuple(fast((rows, WIDTH), BF) for _ in blocks),
         *[(one, VMEM) for one in blocks],
         after=after,
     )
 
-    ring1 = [up(pair), down(pair)]
-    stats = gather_stats(stats)
-    passing = trim(ring1, (stats,))
-    ring2 = [up(passing[0]), down(passing[1])]
+    ring1 = [up(first), down(first)]
+    opposite = shift(opposite, PATCHES // 2)
     prep, conv_w, q_w, kv_w, out_w = call(
         load_body,
         (fast((8, WIDTH), F32),) + tuple(fast(w.shape, w.dtype) for w in weights),
@@ -415,52 +457,52 @@
         (gn_gain, HBM),
         (ln_gain, HBM),
         scratch=(pltpu.SemaphoreType.DMA((4,)),),
-        after=(stats,),
+        after=(first,),
         limit=2,
     )
-    keys = lambda blocks, after=(), micros=0.1: call(
+    passing = trim(HEAD, ring1, (prep, opposite))
+    ring2 = [up(passing[0]), down(passing[1])]
+    keys = lambda blocks, after=(): call(
         keys_body,
         fast((len(blocks) * COLS, 2 * WIDTH), BF),
         *near(blocks),
         (kv_w, VMEM),
         after=after,
-        micros=micros,
-    )
-    conv_rims = lambda after=(), micros=0.1: call(
-        rims_body,
+    )
+    conv_rims = lambda start, blocks, after=(): call(
+        functools.partial(rims_body, start),
         fast(full, F32),
         (place, SCALARS),
-        *[(one, VMEM) for one in ring1],
+        *[(one, VMEM) for one in blocks],
         (conv_w, VMEM),
         after=after,
-        micros=micros,
-    )
-    rims = conv_rims()
-    ring2 = later(ring2, (prep,))
+    )
+    rims = conv_rims(HEAD, ring1, (passing[0],))
+    near_keys = keys(ring1, (rims,))
+    ring2 = later(ring2, (near_keys,))
     ring3 = [up(ring2[0]), down(ring2[1])]
-    pair, hidden, query = call(
+    mid_keys = keys(ring2, (ring2[0],))
+    ring3 = later(ring3, (mid_keys,))
+    ring4 = [up(ring3[0])]
+    far_keys = keys(ring3, (ring3[0],))
+    conv_in, hidden, attn_in, query = call(
         level_body,
-        (fast((2 * COLS, WIDTH), BF), fast(full, F32), fast(full, BF)),
-        (stats, VMEM),
+        (fast(full, BF), fast(full, F32), fast(full, BF), fast(full, BF)),
         (state, VMEM),
         (rims, VMEM),
         (prep, VMEM),
         (conv_w, VMEM),
         (q_w, VMEM),
-    )
-    near_keys = keys(ring1, (rims,))
-    ring3 = later(ring3, (near_keys,))
-    ring4 = [up(ring3[0])]
-    mid_keys = keys(ring2, (ring3[0],))
-    far_keys = keys(ring3, (mid_keys,))
-    ring1 = [up(pair), down(pair)]
+        *[(one, VMEM) for one in [first, *ring1, *ring2, *ring3, opposite]],
+    )
+    ring1 = [up(attn_in), down(attn_in)]
     attend_to = lambda weights, early, late: call(
         functools.partial(attend_body, len(early), len(late)),
         fast(full, BF),
         (query, VMEM),
         (hidden, VMEM),
         *early,
-        (pair, VMEM),
+        (attn_in, VMEM),
         *near(late),
         *[(w, VMEM) for w in weights],
         scratch=(pltpu.VMEM(((1 + len(late)) * COLS, 2 * WIDTH), BF), pltpu.VMEM(full, BF)),
@@ -470,10 +512,12 @@
     eps = attend_to((kv_w, out_w), early, ring4)
     exchange = lambda x: lax.ppermute(x, "cfg", [(0, 1), (1, 0)])
     other = exchange(eps)
-    passing = trim(ring1, (eps,))
-    ring2 = [up(passing[0]), down(passing[1])]
-    near_keys = keys(ring1, (passing[0],), 6.0)
-    rims = conv_rims((near_keys,), 6.0)
+    block = fast((2 * COLS, WIDTH), BF)
+    joined = call(
+        join_body, (block, block), (conv_in, VMEM), *[(one, VMEM) for one in ring1], after=(eps,)
+    )
+    ring2 = [up(joined[0]), down(joined[1])]
+    near_keys = keys(ring1, (joined[0],))
     state, stats = call(
         functools.partial(update_body, 0),
         (fast(whole, F32), stats_shape),
@@ -482,34 +526,40 @@
         (state, VMEM),
         (eps, VMEM),
         (other, VMEM),
-        after=(rims,),
-    )
-    ring2 = later(ring2, (state,))
-    ring3 = [up(ring2[0]), down(ring2[1])]
-    stats = gather_stats(stats)
-    ring3 = later(ring3, (stats,))
+        after=(near_keys,),
+    )
+    block = fast((HEAD, WIDTH), BF)
+    packed = call(
+        pack_body, (block, block), (stats, VMEM), *[(one, VMEM) for one in ring2], after=(state,)
+    )
+    ring3 = [up(packed[0]), down(packed[1])]
+    rims = conv_rims(COLS, ring2, (packed[0],))
+    mid_keys = keys(ring2, (rims,))
+    three, two = call(
+        partial_body,
+        (stats_shape, stats_shape),
+        (stats, VMEM),
+        *[(one, VMEM) for one in ring3],
+        after=(mid_keys,),
+    )
+    before, behind = shift(three, 3), shift(two, -3)
+    ring3 = later(ring3, (three,))
     ring4 = [up(ring3[0])]
-    pair, hidden, query, kv_w, out_w = call(
+    far_keys = keys(ring3, (ring3[0],))
+    attn_in, hidden, query = call(
         second_body,
-        (fast(full, BF), fast(full, F32), fast(full, BF))
-        + tuple(fast(w.shape, w.dtype) for w in weights[2:]),
-        (stats, NEAR),
-        (state, NEAR),
-        (conv_weight, FAR),
-        (rims, NEAR),
-        (prep, NEAR),
-        (q_weight, HBM),
-        (kv_weight, FAR),
-        (out_weight, FAR),
-        scratch=(
-            pltpu.VMEM((3, WIDTH, WIDTH), BF),
-            pltpu.SemaphoreType.DMA((3,)),
-            pltpu.SemaphoreType.DMA((2,)),
-        ),
-        after=(ring3[0],),
-    )
-    mid_keys = keys(ring2)
-    eps = attend_to((kv_w, out_w), [(near_keys, NEAR), (mid_keys, VMEM)], ring3 + ring4)
+        (fast(full, BF), fast(full, F32), fast(full, BF)),
+        (three, VMEM),
+        (before, VMEM),
+        (behind, VMEM),
+        (state, VMEM),
+        (rims, VMEM),
+        (prep, VMEM),
+        (conv_w, VMEM),
+        (q_w, VMEM),
+    )
+    early = [(one, VMEM) for one in (near_keys, mid_keys, far_keys)]
+    eps = attend_to((kv_w, out_w), early, ring4)
     other = exchange(eps)
     return call(
         functools.partial(update_body, 1),

time: 95.5 us -> 87.5 us (0.916); the launches traced: 95.3 us -> 86.2 us
  blocking collectives: 23.5 us -> 0 us
  waiting for transfers between devices: 12 us -> 23.3 us
  starting transfers between devices: 27.8 us -> 33.4 us
  Pallas kernels: 31.1 us -> 28.6 us
    all_to_all x2 -> x0, blocking collectives: 23.5 us -> none  [shards(): gather_stats = lambda x: lax.all_to_all(x, 'patch', 0, 0)]
    ppermute x0 -> x3, starting transfers between devices: none -> 7.72 us  [shards(): lax.ppermute(x, 'patch', [(i, (i + far) % PATCHES) for i in range(PATCHES)])]
    ppermute x0 -> x3, waiting for transfers between devices: none -> 5.92 us  [shards(): lax.ppermute(x, 'patch', [(i, (i + far) % PATCHES) for i in range(PATCHES)])]
    ppermute x6, starting transfers between devices: 19.6 us -> 15.6 us  [shards(): down = lambda x: lax.ppermute(x, 'patch', downward)]
    ppermute x8, waiting for transfers between devices: 5.88 us -> 9.67 us  [shards(): up = lambda x: lax.ppermute(x, 'patch', upward)]
    pallas_call x17 -> x20, Pallas kernels: 31.1 us -> 28.6 us  [call(): pl.pallas_call(wrapped, out_shape=jax.tree.unflatten(tree, leaves), in_sp...]
    ppermute x2, starting transfers between devices: 4.1 us -> 6.47 us  [shards(): exchange = lambda x: lax.ppermute(x, 'cfg', [(0, 1), (1, 0)])]
    ppermute x6, waiting for transfers between devices: 0.03 us -> 1.52 us  [shards(): down = lambda x: lax.ppermute(x, 'patch', downward)]
  transfers between devices with their start and end apart: 16 -> 19, of which waited for: 3 -> 11; matrix products, arithmetic and copies ran while one was open for 0% -> 0% of each run, Pallas kernels for 24% -> 25%
where the time goes in v3:
time: 87.5 us; the launch traced here: 86.2 us
  starting transfers between devices  33.4 us (38%)
  Pallas kernels  28.6 us (33%)
  waiting for transfers between devices  23.3 us (27%)
    pallas_call x20, Pallas kernels, call(): pl.pallas_call(wrapped, out_shape=jax.tree.unflatten(tree, leaves), in_sp...  28.6 us
    ppermute x6, starting transfers between devices, shards(): down = lambda x: lax.ppermute(x, 'patch', downward)  15.6 us
    ppermute x8, waiting for transfers between devices, shards(): up = lambda x: lax.ppermute(x, 'patch', upward)  9.67 us
    ppermute x3, starting transfers between devices, shards(): lax.ppermute(x, 'patch', [(i, (i + far) % PATCHES) for i in range(PATCHES)])  7.72 us
    ppermute x2, starting transfers between devices, shards(): exchange = lambda x: lax.ppermute(x, 'cfg', [(0, 1), (1, 0)])  6.47 us
    ppermute x2, waiting for transfers between devices, shards(): exchange = lambda x: lax.ppermute(x, 'cfg', [(0, 1), (1, 0)])  6.16 us
    ppermute x3, waiting for transfers between devices, shards(): lax.ppermute(x, 'patch', [(i, (i + far) % PATCHES) for i in range(PATCHES)])  5.92 us
    ppermute x8, starting transfers between devices, shards(): up = lambda x: lax.ppermute(x, 'patch', upward)  3.62 us
  transfers between devices with their start and end apart: 19, of which 11 were waited for; matrix products, arithmetic and copies ran while one was open for 0% of the time, Pallas kernels for 25%

profile of v3, /device:TPU:2, one launch (start us, length us, event | category | flops | bytes accessed | tf_op | source)
XLA Modules:
  0.0 86.2 jit_solution(8852836778157569639)
XLA Ops:
  0.6 0.1 add_convert_fusion.refs_3_.refs_0_
  0.7 1.8 %shard_map.140 = (bf16[272,640]{1,0:T(8,128)(2,1)S(1)}, f32[1,128,640]{2,1,0:T(8,128)S(1)}, f32[8,128]{1,0:T(8,128)S(1)}) custom-call(f32[1,128,640]{2,1,0:T(8,128)} %refs_0_.2, bf16[128,640]{1,0:T(8,128)(2,1)} %bitcast.6, bf16[128,640]{1,0:T(8,128)(2,1)} %bitcast.7, f32[3]{0:T(128)S(1)} %add_convert_fusion.refs_3_.refs_0_), custom_call_target="tpu_custom_call" | custom-call | bytes 340000 | tf_op jit(solution)/shard_map/pallas_call | solution.py:94
  2.5 5.9 %collective-permute-start.1 = (bf16[272,640]{1,0:T(8,128)(2,1)S(1)}, bf16[272,640]{1,0:T(8,128)(2,1)S(1)}, u32[]{:S(2)}, u32[]{:S(2)}) collective-permute-start(bf16[272,640]{1,0:T(8,128)(2,1)S(1)} %get-tuple-element.33.refs_10_.refs_5_), channel_id=1, source_target_pairs={{2,0},{4,2},{6,4},{8,6},{10,8},{12,10},{14,12},{0,14},{3,1},{5,3},... | collective-permute-start | bytes 1044488 | tf_op jit(solution)/shard_map/ppermute | solution.py:419
  8.4 0.0 collective-permute-start
  8.4 3.4 %collective-permute-start.2 = (f32[8,128]{1,0:T(8,128)S(1)}, f32[8,128]{1,0:T(8,128)S(1)}, u32[]{:S(2)}, u32[]{:S(2)}) collective-permute-start(f32[8,128]{1,0:T(8,128)S(1)} %get-tuple-element.37), channel_id=1, source_target_pairs={{0,8},{2,10},{4,12},{6,14},{8,0},{10,2},{12,4},{14,6},{1,9},{3,11}... | collective-permute-start | bytes 12296 | tf_op jit(solution)/shard_map/ppermute | solution.py:424
  11.8 4.1 %shard_map.141 = (f32[8,640]{1,0:T(8,128)S(1)}, bf16[3,3,640,640]{3,2,1,0:T(8,128)(2,1)S(1)}, bf16[640,640]{1,0:T(8,128)(2,1)S(1)}, bf16[640,1280]{1,0:T(8,128)(2,1)S(1)}, bf16[640,640]{1,0:T(8,128)(2,1)S(1)}) custom-call(bf16[3,3,640,640]{3,2,1,0:T(8,128)(2,1)} %refs_0_.3, bf16[640,640]{1,0:T(8,128)(2,1)} %refs_1_.1, bf16[640,1280]{1,0:T(8,128)(2,1)} %refs_2_.1, ...), custom_call_target="tpu_custom_call" | custom-call | bytes 340000 | tf_op jit(solution)/shard_map/pallas_call | solution.py:94
  15.9 3.6 %collective-permute-done.2.refs_3_.refs_12_ = f32[8,128]{1,0:T(8,128)S(1)} collective-permute-done((f32[8,128]{1,0:T(8,128)S(1)}, f32[8,128]{1,0:T(8,128)S(1)}, u32[]{:S(2)}, u32[]{:S(2)}) %collective-permute-start.2) | collective-permute-done | bytes 4128 | tf_op jit(solution)/shard_map/ppermute | solution.py:424
  19.6 0.0 collective-permute-done.1.refs_1_.refs_2_.refs_7_
  19.6 0.2 collective-permute-start.4
  19.8 1.9 %collective-permute-start.3 = (bf16[144,640]{1,0:T(8,128)(2,1)S(1)}, bf16[144,640]{1,0:T(8,128)(2,1)S(1)}, u32[]{:S(2)}, u32[]{:S(2)}) collective-permute-start(bf16[144,640]{1,0:T(8,128)(2,1)S(1)} %get-tuple-element.38.refs_4_), channel_id=1, source_target_pairs={{0,2},{2,4},{4,6},{6,8},{8,10},{10,12},{12,14},{14,0},{1,3},{3,5},... | collective-permute-start | bytes 552968 | tf_op jit(solution)/shard_map/ppermute | solution.py:418
  21.7 1.7 %shard_map.143.refs_3_.refs_1_ = f32[128,640]{1,0:T(8,128)S(1)} custom-call(f32[3]{0:T(128)S(1)} %add_convert_fusion.refs_3_.refs_0_, bf16[272,640]{1,0:T(8,128)(2,1)S(1)} %collective-permute-done.refs_0_.refs_1_.refs_6_, bf16[272,640]{1,0:T(8,128)(2,1)S(1)} %collective-permute-done.1.refs_1_.refs_2_.refs_7_, ...), custom_call_target="tpu_custom_call" | custom-call | bytes 340000 | tf_op jit(solution)/shard_map/pallas_call | solution.py:94
  23.4 1.0 %shard_map.144.refs_2_ = bf16[256,1280]{1,0:T(8,128)(2,1)S(1)} custom-call(bf16[272,640]{1,0:T(8,128)(2,1)S(1)} %collective-permute-done.refs_0_.refs_1_.refs_6_, bf16[272,640]{1,0:T(8,128)(2,1)S(1)} %collective-permute-done.1.refs_1_.refs_2_.refs_7_, bf16[640,1280]{1,0:T(8,128)(2,1)S(1)} %get-tuple-element.41.refs_2_.refs_7_, ...), custom_call_target="tpu_custom_call" | custom-call | bytes 340000 | tf_op jit(solution)/shard_map/pallas_call | solution.py:94
  24.4 0.9 collective-permute-done.4.refs_1_
  25.2 1.4 %collective-permute-done.3.refs_0_ = bf16[144,640]{1,0:T(8,128)(2,1)S(1)} collective-permute-done((bf16[144,640]{1,0:T(8,128)(2,1)S(1)}, bf16[144,640]{1,0:T(8,128)(2,1)S(1)}, u32[]{:S(2)}, u32[]{:S(2)}) %collective-permute-start.3) | collective-permute-done | bytes 184352 | tf_op jit(solution)/shard_map/ppermute | solution.py:418
  26.6 0.8 collective-permute-start.5
  27.3 2.5 %collective-permute-start.6 = (bf16[144,640]{1,0:T(8,128)(2,1)S(1)}, bf16[144,640]{1,0:T(8,128)(2,1)S(1)}, u32[]{:S(2)}, u32[]{:S(2)}) collective-permute-start(bf16[144,640]{1,0:T(8,128)(2,1)S(1)} %get-tuple-element.43.refs_1_.refs_9_), channel_id=1, source_target_pairs={{2,0},{4,2},{6,4},{8,6},{10,8},{12,10},{14,12},{0,14},{3,1},{5,3},... | collective-permute-start | bytes 552968 | tf_op jit(solution)/shard_map/ppermute | solution.py:419
  29.8 1.2 %shard_map.146.refs_2_.refs_3_ = bf16[256,1280]{1,0:T(8,128)(2,1)S(1)} custom-call(bf16[144,640]{1,0:T(8,128)(2,1)S(1)} %get-tuple-element.42.refs_0_.refs_3_.refs_8_, bf16[144,640]{1,0:T(8,128)(2,1)S(1)} %get-tuple-element.43.refs_1_.refs_9_, bf16[640,1280]{1,0:T(8,128)(2,1)S(1)} %get-tuple-element.41.refs_2_.refs_7_, ...), custom_call_target="tpu_custom_call" | custom-call | bytes 340000 | tf_op jit(solution)/shard_map/pallas_call | solution.py:94
  31.0 2.4 %collective-permute-done.5.refs_0_ = bf16[144,640]{1,0:T(8,128)(2,1)S(1)} collective-permute-done((bf16[144,640]{1,0:T(8,128)(2,1)S(1)}, bf16[144,640]{1,0:T(8,128)(2,1)S(1)}, u32[]{:S(2)}, u32[]{:S(2)}) %collective-permute-start.5) | collective-permute-done | bytes 184352 | tf_op jit(solution)/shard_map/ppermute | solution.py:418
  33.3 1.4 %shard_map.148 = (bf16[128,640]{1,0:T(8,128)(2,1)S(1)}, f32[128,640]{1,0:T(8,128)S(1)}, bf16[128,640]{1,0:T(8,128)(2,1)S(1)}, bf16[128,640]{1,0:T(8,128)(2,1)S(1)}) custom-call(f32[1,128,640]{2,1,0:T(8,128)S(1)} %get-tuple-element.35.refs_0_.refs_2_, f32[128,640]{1,0:T(8,128)S(1)} %shard_map.143.refs_3_.refs_1_, ...), custom_call_target="tpu_custom_call" | custom-call | bytes 340000 | tf_op jit(solution)/shard_map/pallas_call | solution.py:94
  34.7 3.3 %collective-permute-start.10 = (bf16[128,640]{1,0:T(8,128)(2,1)S(1)}, bf16[128,640]{1,0:T(8,128)(2,1)S(1)}, u32[]{:S(2)}, u32[]{:S(2)}) collective-permute-start(bf16[128,640]{1,0:T(8,128)(2,1)S(1)} %get-tuple-element.48.refs_5_), channel_id=1, source_target_pairs={{2,0},{4,2},{6,4},{8,6},{10,8},{12,10},{14,12},{0,14},{3,1},{5,3},... | collective-permute-start | bytes 491528 | tf_op jit(solution)/shard_map/ppermute | solution.py:419
  38.0 0.0 collective-permute-start.9
  38.1 1.2 %shard_map.149.refs_4_ = bf16[256,1280]{1,0:T(8,128)(2,1)S(1)} custom-call(bf16[144,640]{1,0:T(8,128)(2,1)S(1)} %get-tuple-element.44.refs_10_.refs_0_.refs_3_, bf16[144,640]{1,0:T(8,128)(2,1)S(1)} %get-tuple-element.45.refs_11_.refs_1_, bf16[640,1280]{1,0:T(8,128)(2,1)S(1)} %get-tuple-element.41.refs_2_.refs_7_, ...), custom_call_target="tpu_custom_call" | custom-call | bytes 340000 | tf_op jit(solution)/shard_map/pallas_call | solution.py:94
  39.2 2.1 %collective-permute-done.7.refs_6_ = bf16[144,640]{1,0:T(8,128)(2,1)S(1)} collective-permute-done((bf16[144,640]{1,0:T(8,128)(2,1)S(1)}, bf16[144,640]{1,0:T(8,128)(2,1)S(1)}, u32[]{:S(2)}, u32[]{:S(2)}) %collective-permute-start.7) | collective-permute-done | bytes 184352 | tf_op jit(solution)/shard_map/ppermute | solution.py:418
  41.4 3.6 %shard_map.150.refs_3_ = bf16[128,640]{1,0:T(8,128)(2,1)S(1)} custom-call(bf16[128,640]{1,0:T(8,128)(2,1)S(1)} %get-tuple-element.46.refs_0_, f32[128,640]{1,0:T(8,128)S(1)} %get-tuple-element.47.refs_1_, bf16[256,1280]{1,0:T(8,128)(2,1)S(1)} %shard_map.144.refs_2_, bf16[256,1280]{1,0:T(8,128)(2,1)S(1)} %shard_map.146.refs_2_.refs_3_, ...), custom_call_target="tpu_custom_call" | custom-call | bytes 13600000 | tf_op jit(solution)/shard_map/pallas_call | solution.py:94
  45.0 0.1 shard_map.151
  45.1 1.2 %collective-permute-start.12 = (bf16[256,640]{1,0:T(8,128)(2,1)S(1)}, bf16[256,640]{1,0:T(8,128)(2,1)S(1)}, u32[]{:S(2)}, u32[]{:S(2)}) collective-permute-start(bf16[256,640]{1,0:T(8,128)(2,1)S(1)} %get-tuple-element.54), channel_id=1, source_target_pairs={{2,0},{4,2},{6,4},{8,6},{10,8},{12,10},{14,12},{0,14},{3,1},{5,3},... | collective-permute-start | bytes 983048 | tf_op jit(solution)/shard_map/ppermute | solution.py:419
  46.3 0.9 %collective-permute-start.11 = (bf16[256,640]{1,0:T(8,128)(2,1)S(1)}, bf16[256,640]{1,0:T(8,128)(2,1)S(1)}, u32[]{:S(2)}, u32[]{:S(2)}) collective-permute-start(bf16[256,640]{1,0:T(8,128)(2,1)S(1)} %get-tuple-element.51.refs_3_), channel_id=1, source_target_pairs={{0,2},{2,4},{4,6},{6,8},{8,10},{10,12},{12,14},{14,0},{1,3},{3,5},... | collective-permute-start | bytes 983048 | tf_op jit(solution)/shard_map/ppermute | solution.py:418
  47.2 3.2 %collective-permute-start.8 = (bf16[128,640]{1,0:T(8,128)(2,1)S(1)}, bf16[128,640]{1,0:T(8,128)(2,1)S(1)}, u32[]{:S(2)}, u32[]{:S(2)}) collective-permute-start(bf16[128,640]{1,0:T(8,128)(2,1)S(1)} %shard_map.150.refs_3_), channel_id=1, source_target_pairs={{0,1},{1,0},{2,3},{3,2},{4,5},{5,4},{6,7},{7,6},{8,9},{9,8},{10,11... | collective-permute-start | bytes 491528 | tf_op jit(solution)/shard_map/ppermute | solution.py:513
  50.4 1.1 %shard_map.152.refs_5_.refs_2_ = bf16[256,1280]{1,0:T(8,128)(2,1)S(1)} custom-call(bf16[128,640]{1,0:T(8,128)(2,1)S(1)} %collective-permute-done.9.refs_1_.refs_0_, bf16[128,640]{1,0:T(8,128)(2,1)S(1)} %collective-permute-done.10.refs_2_.refs_1_, bf16[640,1280]{1,0:T(8,128)(2,1)S(1)} %get-tuple-element.41.refs_2_.refs_7_, ...), custom_call_target="tpu_custom_call" | custom-call | bytes 340000 | tf_op jit(solution)/shard_map/pallas_call | solution.py:94
  51.5 2.5 %collective-permute-done.8.refs_4_ = bf16[128,640]{1,0:T(8,128)(2,1)S(1)} collective-permute-done((bf16[128,640]{1,0:T(8,128)(2,1)S(1)}, bf16[128,640]{1,0:T(8,128)(2,1)S(1)}, u32[]{:S(2)}, u32[]{:S(2)}) %collective-permute-start.8) | collective-permute-done | bytes 163872 | tf_op jit(solution)/shard_map/ppermute | solution.py:513
  54.0 1.3 %shard_map.153 = (f32[1,128,640]{2,1,0:T(8,128)S(1)}, f32[8,128]{1,0:T(8,128)S(1)}) custom-call(f32[3]{0:T(128)S(1)} %add_convert_fusion.refs_3_.refs_0_, f32[8,640]{1,0:T(8,128)S(1)} %get-tuple-element.34.refs_2_.refs_1_.refs_5_, f32[1,128,640]{2,1,0:T(8,128)S(1)} %get-tuple-element.35.refs_0_.refs_2_, bf16[128,640]{1,0:T(8,128)(2,1)S(1)} %shard_map.150.refs_3_, ...), custom_call_target="tpu_custom_call" | custom-call | bytes 340000 | tf_op jit(solution)/shard_map/pallas_call | solution.py:94
  55.3 0.0 collective-permute-done.11.refs_1_.refs_0_
  55.4 2.4 %collective-permute-start.14 = (bf16[144,640]{1,0:T(8,128)(2,1)S(1)}, bf16[144,640]{1,0:T(8,128)(2,1)S(1)}, u32[]{:S(2)}, u32[]{:S(2)}) collective-permute-start(bf16[144,640]{1,0:T(8,128)(2,1)S(1)} %get-tuple-element.56), channel_id=1, source_target_pairs={{2,0},{4,2},{6,4},{8,6},{10,8},{12,10},{14,12},{0,14},{3,1},{5,3},... | collective-permute-start | bytes 552968 | tf_op jit(solution)/shard_map/ppermute | solution.py:419
  57.8 1.7 %shard_map.155.refs_3_.refs_4_ = f32[128,640]{1,0:T(8,128)S(1)} custom-call(f32[3]{0:T(128)S(1)} %add_convert_fusion.refs_3_.refs_0_, bf16[256,640]{1,0:T(8,128)(2,1)S(1)} %collective-permute-done.11.refs_1_.refs_0_, bf16[256,640]{1,0:T(8,128)(2,1)S(1)} %collective-permute-done.12.refs_2_.refs_1_, ...), custom_call_target="tpu_custom_call" | custom-call | bytes 340000 | tf_op jit(solution)/shard_map/pallas_call | solution.py:94
  59.5 0.9 %shard_map.156.refs_3_ = bf16[256,1280]{1,0:T(8,128)(2,1)S(1)} custom-call(bf16[256,640]{1,0:T(8,128)(2,1)S(1)} %collective-permute-done.11.refs_1_.refs_0_, bf16[256,640]{1,0:T(8,128)(2,1)S(1)} %collective-permute-done.12.refs_2_.refs_1_, bf16[640,1280]{1,0:T(8,128)(2,1)S(1)} %get-tuple-element.41.refs_2_.refs_7_, f32[128,640]{1,0:T(8,128)S(1)} %shard_map.155.refs_3_.refs_4_), custom_call_target="tpu_custom_call" | custom-call | bytes 340000 | tf_op jit(solution)/shard_map/pallas_call | solution.py:94
  60.4 0.7 collective-permute-done.14.refs_2_.refs_1_
  61.1 3.8 %collective-permute-done.13.refs_1_.refs_0_ = bf16[144,640]{1,0:T(8,128)(2,1)S(1)} collective-permute-done((bf16[144,640]{1,0:T(8,128)(2,1)S(1)}, bf16[144,640]{1,0:T(8,128)(2,1)S(1)}, u32[]{:S(2)}, u32[]{:S(2)}) %collective-permute-start.13) | collective-permute-done | bytes 184352 | tf_op jit(solution)/shard_map/ppermute | solution.py:418
  64.9 0.1 collective-permute-start.17
  65.0 1.2 %collective-permute-start.16 = (f32[8,128]{1,0:T(8,128)S(1)}, f32[8,128]{1,0:T(8,128)S(1)}, u32[]{:S(2)}, u32[]{:S(2)}) collective-permute-start(f32[8,128]{1,0:T(8,128)S(1)} %get-tuple-element.58), channel_id=1, source_target_pairs={{0,10},{2,12},{4,14},{6,0},{8,2},{10,4},{12,6},{14,8},{1,11},{3,13... | collective-permute-start | bytes 12296 | tf_op jit(solution)/shard_map/ppermute | solution.py:424
  66.2 3.2 %collective-permute-start.15 = (f32[8,128]{1,0:T(8,128)S(1)}, f32[8,128]{1,0:T(8,128)S(1)}, u32[]{:S(2)}, u32[]{:S(2)}) collective-permute-start(f32[8,128]{1,0:T(8,128)S(1)} %get-tuple-element.57.refs_0_.refs_2_), channel_id=1, source_target_pairs={{0,6},{2,8},{4,10},{6,12},{8,14},{10,0},{12,2},{14,4},{1,7},{3,9},... | collective-permute-start | bytes 12296 | tf_op jit(solution)/shard_map/ppermute | solution.py:424
  69.3 1.2 %shard_map.160.refs_4_ = bf16[256,1280]{1,0:T(8,128)(2,1)S(1)} custom-call(bf16[144,640]{1,0:T(8,128)(2,1)S(1)} %get-tuple-element.61.refs_0_.refs_3_, bf16[144,640]{1,0:T(8,128)(2,1)S(1)} %get-tuple-element.62.refs_1_, bf16[640,1280]{1,0:T(8,128)(2,1)S(1)} %get-tuple-element.41.refs_2_.refs_7_, bf16[144,640]{1,0:T(8,128)(2,1)S(1)} %get-tuple-element.61.refs_0_.refs_3_), custom_call_target="tpu_custom_call" | custom-call | bytes 340000 | tf_op jit(solution)/shard_map/pallas_call | solution.py:94
  70.5 0.4 collective-permute-done.16.refs_2_
  70.9 1.9 %collective-permute-done.15.refs_1_ = f32[8,128]{1,0:T(8,128)S(1)} collective-permute-done((f32[8,128]{1,0:T(8,128)S(1)}, f32[8,128]{1,0:T(8,128)S(1)}, u32[]{:S(2)}, u32[]{:S(2)}) %collective-permute-start.15) | collective-permute-done | bytes 4128 | tf_op jit(solution)/shard_map/ppermute | solution.py:424
  72.8 1.4 %shard_map.158 = (bf16[128,640]{1,0:T(8,128)(2,1)S(1)}, f32[128,640]{1,0:T(8,128)S(1)}, bf16[128,640]{1,0:T(8,128)(2,1)S(1)}) custom-call(f32[8,128]{1,0:T(8,128)S(1)} %get-tuple-element.57.refs_0_.refs_2_, f32[8,128]{1,0:T(8,128)S(1)} %collective-permute-done.15.refs_1_, f32[8,128]{1,0:T(8,128)S(1)} %collective-permute-done.16.refs_2_, ...), custom_call_target="tpu_custom_call" | custom-call | bytes 340000 | tf_op jit(solution)/shard_map/pallas_call | solution.py:94
  74.2 3.6 %shard_map.161.refs_3_ = bf16[128,640]{1,0:T(8,128)(2,1)S(1)} custom-call(bf16[128,640]{1,0:T(8,128)(2,1)S(1)} %get-tuple-element.59.refs_0_, f32[128,640]{1,0:T(8,128)S(1)} %get-tuple-element.60.refs_1_, bf16[256,1280]{1,0:T(8,128)(2,1)S(1)} %shard_map.152.refs_5_.refs_2_, bf16[256,1280]{1,0:T(8,128)(2,1)S(1)} %shard_map.156.refs_3_, ...), custom_call_target="tpu_custom_call" | custom-call | bytes 13600000 | tf_op jit(solution)/shard_map/pallas_call | solution.py:94
  77.8 3.3 %collective-permute-start.18 = (bf16[128,640]{1,0:T(8,128)(2,1)S(1)}, bf16[128,640]{1,0:T(8,128)(2,1)S(1)}, u32[]{:S(2)}, u32[]{:S(2)}) collective-permute-start(bf16[128,640]{1,0:T(8,128)(2,1)S(1)} %shard_map.161.refs_3_), channel_id=1, source_target_pairs={{0,1},{1,0},{2,3},{3,2},{4,5},{5,4},{6,7},{7,6},{8,9},{9,8},{10,11... | collective-permute-start | bytes 491528 | tf_op jit(solution)/shard_map/ppermute | solution.py:513
  81.1 3.6 %collective-permute-done.18.refs_4_ = bf16[128,640]{1,0:T(8,128)(2,1)S(1)} collective-permute-done((bf16[128,640]{1,0:T(8,128)(2,1)S(1)}, bf16[128,640]{1,0:T(8,128)(2,1)S(1)}, u32[]{:S(2)}, u32[]{:S(2)}) %collective-permute-start.18) | collective-permute-done | bytes 163872 | tf_op jit(solution)/shard_map/ppermute | solution.py:513
  84.7 1.5 %shard_map.162 = (f32[1,128,640]{2,1,0:T(8,128)}, f32[1,128,640]{2,1,0:T(8,128)}) custom-call(f32[3]{0:T(128)S(1)} %add_convert_fusion.refs_3_.refs_0_, f32[8,640]{1,0:T(8,128)S(1)} %get-tuple-element.34.refs_2_.refs_1_.refs_5_, f32[1,128,640]{2,1,0:T(8,128)S(1)} %get-tuple-element.52.refs_3_.refs_2_, bf16[128,640]{1,0:T(8,128)(2,1)S(1)} %shard_map.161.refs_3_, ...), custom_call_target="tpu_custom_call" | custom-call | bytes 340000 | tf_op jit(solution)/shard_map/pallas_call | solution.py:94
  (14 shorter events, 0.1 us)
Async XLA Ops:
  2.5 17.1 %collective-permute-start.1 = (bf16[272,640]{1,0:T(8,128)(2,1)S(1)}, bf16[272,640]{1,0:T(8,128)(2,1)S(1)}, u32[]{:S(2)}, u32[]{:S(2)}) collective-permute-start(bf16[272,640]{1,0:T(8,128)(2,1)S(1)} %get-tuple-element.33.refs_10_.refs_5_), channel_id=1, source_target_pairs={{2,0},{4,2},{6,4},{8,6},{10,8},{12,10},{14,12},{0,14},{3,1},{5,3},... | collective-permute-start | bytes 1044488 | tf_op jit(solution)/shard_map/ppermute | solution.py:419
  8.4 11.1 %collective-permute-start = (bf16[272,640]{1,0:T(8,128)(2,1)S(1)}, bf16[272,640]{1,0:T(8,128)(2,1)S(1)}, u32[]{:S(2)}, u32[]{:S(2)}) collective-permute-start(bf16[272,640]{1,0:T(8,128)(2,1)S(1)} %get-tuple-element.33.refs_10_.refs_5_), channel_id=1, source_target_pairs={{0,2},{2,4},{4,6},{6,8},{8,10},{10,12},{12,14},{14,0},{1,3},{3,5},... | collective-permute-start | bytes 1044488 | tf_op jit(solution)/shard_map/ppermute | solution.py:418
  8.4 11.1 %collective-permute-start.2 = (f32[8,128]{1,0:T(8,128)S(1)}, f32[8,128]{1,0:T(8,128)S(1)}, u32[]{:S(2)}, u32[]{:S(2)}) collective-permute-start(f32[8,128]{1,0:T(8,128)S(1)} %get-tuple-element.37), channel_id=1, source_target_pairs={{0,8},{2,10},{4,12},{6,14},{8,0},{10,2},{12,4},{14,6},{1,9},{3,11}... | collective-permute-start | bytes 12296 | tf_op jit(solution)/shard_map/ppermute | solution.py:424
  19.6 5.6 %collective-permute-start.4 = (bf16[144,640]{1,0:T(8,128)(2,1)S(1)}, bf16[144,640]{1,0:T(8,128)(2,1)S(1)}, u32[]{:S(2)}, u32[]{:S(2)}) collective-permute-start(bf16[144,640]{1,0:T(8,128)(2,1)S(1)} %get-tuple-element.40), channel_id=1, source_target_pairs={{2,0},{4,2},{6,4},{8,6},{10,8},{12,10},{14,12},{0,14},{3,1},{5,3},... | collective-permute-start | bytes 552968 | tf_op jit(solution)/shard_map/ppermute | solution.py:419
  19.8 6.7 %collective-permute-start.3 = (bf16[144,640]{1,0:T(8,128)(2,1)S(1)}, bf16[144,640]{1,0:T(8,128)(2,1)S(1)}, u32[]{:S(2)}, u32[]{:S(2)}) collective-permute-start(bf16[144,640]{1,0:T(8,128)(2,1)S(1)} %get-tuple-element.38.refs_4_), channel_id=1, source_target_pairs={{0,2},{2,4},{4,6},{6,8},{8,10},{10,12},{12,14},{14,0},{1,3},{3,5},... | collective-permute-start | bytes 552968 | tf_op jit(solution)/shard_map/ppermute | solution.py:418
  26.6 6.7 %collective-permute-start.5 = (bf16[144,640]{1,0:T(8,128)(2,1)S(1)}, bf16[144,640]{1,0:T(8,128)(2,1)S(1)}, u32[]{:S(2)}, u32[]{:S(2)}) collective-permute-start(bf16[144,640]{1,0:T(8,128)(2,1)S(1)} %get-tuple-element.42.refs_0_.refs_3_.refs_8_), channel_id=1, source_target_pairs={{0,2},{2,4},{4,6},{6,8},{8,10},{10,12},{12,14},{14,0},{1,3},{3,5},... | collective-permute-start | bytes 552968 | tf_op jit(solution)/shard_map/ppermute | solution.py:418
  27.3 6.0 %collective-permute-start.6 = (bf16[144,640]{1,0:T(8,128)(2,1)S(1)}, bf16[144,640]{1,0:T(8,128)(2,1)S(1)}, u32[]{:S(2)}, u32[]{:S(2)}) collective-permute-start(bf16[144,640]{1,0:T(8,128)(2,1)S(1)} %get-tuple-element.43.refs_1_.refs_9_), channel_id=1, source_target_pairs={{2,0},{4,2},{6,4},{8,6},{10,8},{12,10},{14,12},{0,14},{3,1},{5,3},... | collective-permute-start | bytes 552968 | tf_op jit(solution)/shard_map/ppermute | solution.py:419
  33.3 8.0 %collective-permute-start.7 = (bf16[144,640]{1,0:T(8,128)(2,1)S(1)}, bf16[144,640]{1,0:T(8,128)(2,1)S(1)}, u32[]{:S(2)}, u32[]{:S(2)}) collective-permute-start(bf16[144,640]{1,0:T(8,128)(2,1)S(1)} %get-tuple-element.44.refs_10_.refs_0_.refs_3_), channel_id=1, source_target_pairs={{0,2},{2,4},{4,6},{6,8},{8,10},{10,12},{12,14},{14,0},{1,3},{3,5},... | collective-permute-start | bytes 552968 | tf_op jit(solution)/shard_map/ppermute | solution.py:418
  34.7 10.3 %collective-permute-start.10 = (bf16[128,640]{1,0:T(8,128)(2,1)S(1)}, bf16[128,640]{1,0:T(8,128)(2,1)S(1)}, u32[]{:S(2)}, u32[]{:S(2)}) collective-permute-start(bf16[128,640]{1,0:T(8,128)(2,1)S(1)} %get-tuple-element.48.refs_5_), channel_id=1, source_target_pairs={{2,0},{4,2},{6,4},{8,6},{10,8},{12,10},{14,12},{0,14},{3,1},{5,3},... | collective-permute-start | bytes 491528 | tf_op jit(solution)/shard_map/ppermute | solution.py:419
  38.0 7.0 %collective-permute-start.9 = (bf16[128,640]{1,0:T(8,128)(2,1)S(1)}, bf16[128,640]{1,0:T(8,128)(2,1)S(1)}, u32[]{:S(2)}, u32[]{:S(2)}) collective-permute-start(bf16[128,640]{1,0:T(8,128)(2,1)S(1)} %get-tuple-element.48.refs_5_), channel_id=1, source_target_pairs={{0,2},{2,4},{4,6},{6,8},{8,10},{10,12},{12,14},{14,0},{1,3},{3,5},... | collective-permute-start | bytes 491528 | tf_op jit(solution)/shard_map/ppermute | solution.py:418
  45.1 10.3 %collective-permute-start.12 = (bf16[256,640]{1,0:T(8,128)(2,1)S(1)}, bf16[256,640]{1,0:T(8,128)(2,1)S(1)}, u32[]{:S(2)}, u32[]{:S(2)}) collective-permute-start(bf16[256,640]{1,0:T(8,128)(2,1)S(1)} %get-tuple-element.54), channel_id=1, source_target_pairs={{2,0},{4,2},{6,4},{8,6},{10,8},{12,10},{14,12},{0,14},{3,1},{5,3},... | collective-permute-start | bytes 983048 | tf_op jit(solution)/shard_map/ppermute | solution.py:419
  46.3 9.1 %collective-permute-start.11 = (bf16[256,640]{1,0:T(8,128)(2,1)S(1)}, bf16[256,640]{1,0:T(8,128)(2,1)S(1)}, u32[]{:S(2)}, u32[]{:S(2)}) collective-permute-start(bf16[256,640]{1,0:T(8,128)(2,1)S(1)} %get-tuple-element.51.refs_3_), channel_id=1, source_target_pairs={{0,2},{2,4},{4,6},{6,8},{8,10},{10,12},{12,14},{14,0},{1,3},{3,5},... | collective-permute-start | bytes 983048 | tf_op jit(solution)/shard_map/ppermute | solution.py:418
  47.2 6.8 %collective-permute-start.8 = (bf16[128,640]{1,0:T(8,128)(2,1)S(1)}, bf16[128,640]{1,0:T(8,128)(2,1)S(1)}, u32[]{:S(2)}, u32[]{:S(2)}) collective-permute-start(bf16[128,640]{1,0:T(8,128)(2,1)S(1)} %shard_map.150.refs_3_), channel_id=1, source_target_pairs={{0,1},{1,0},{2,3},{3,2},{4,5},{5,4},{6,7},{7,6},{8,9},{9,8},{10,11... | collective-permute-start | bytes 491528 | tf_op jit(solution)/shard_map/ppermute | solution.py:513
  55.4 5.7 %collective-permute-start.14 = (bf16[144,640]{1,0:T(8,128)(2,1)S(1)}, bf16[144,640]{1,0:T(8,128)(2,1)S(1)}, u32[]{:S(2)}, u32[]{:S(2)}) collective-permute-start(bf16[144,640]{1,0:T(8,128)(2,1)S(1)} %get-tuple-element.56), channel_id=1, source_target_pairs={{2,0},{4,2},{6,4},{8,6},{10,8},{12,10},{14,12},{0,14},{3,1},{5,3},... | collective-permute-start | bytes 552968 | tf_op jit(solution)/shard_map/ppermute | solution.py:419
  57.8 7.0 %collective-permute-start.13 = (bf16[144,640]{1,0:T(8,128)(2,1)S(1)}, bf16[144,640]{1,0:T(8,128)(2,1)S(1)}, u32[]{:S(2)}, u32[]{:S(2)}) collective-permute-start(bf16[144,640]{1,0:T(8,128)(2,1)S(1)} %get-tuple-element.55.refs_4_), channel_id=1, source_target_pairs={{0,2},{2,4},{4,6},{6,8},{8,10},{10,12},{12,14},{14,0},{1,3},{3,5},... | collective-permute-start | bytes 552968 | tf_op jit(solution)/shard_map/ppermute | solution.py:418
  64.9 9.3 %collective-permute-start.17 = (bf16[144,640]{1,0:T(8,128)(2,1)S(1)}, bf16[144,640]{1,0:T(8,128)(2,1)S(1)}, u32[]{:S(2)}, u32[]{:S(2)}) collective-permute-start(bf16[144,640]{1,0:T(8,128)(2,1)S(1)} %get-tuple-element.61.refs_0_.refs_3_), channel_id=1, source_target_pairs={{0,2},{2,4},{4,6},{6,8},{8,10},{10,12},{12,14},{14,0},{1,3},{3,5},... | collective-permute-start | bytes 552968 | tf_op jit(solution)/shard_map/ppermute | solution.py:418
  65.0 5.9 %collective-permute-start.16 = (f32[8,128]{1,0:T(8,128)S(1)}, f32[8,128]{1,0:T(8,128)S(1)}, u32[]{:S(2)}, u32[]{:S(2)}) collective-permute-start(f32[8,128]{1,0:T(8,128)S(1)} %get-tuple-element.58), channel_id=1, source_target_pairs={{0,10},{2,12},{4,14},{6,0},{8,2},{10,4},{12,6},{14,8},{1,11},{3,13... | collective-permute-start | bytes 12296 | tf_op jit(solution)/shard_map/ppermute | solution.py:424
  66.2 6.6 %collective-permute-start.15 = (f32[8,128]{1,0:T(8,128)S(1)}, f32[8,128]{1,0:T(8,128)S(1)}, u32[]{:S(2)}, u32[]{:S(2)}) collective-permute-start(f32[8,128]{1,0:T(8,128)S(1)} %get-tuple-element.57.refs_0_.refs_2_), channel_id=1, source_target_pairs={{0,6},{2,8},{4,10},{6,12},{8,14},{10,0},{12,2},{14,4},{1,7},{3,9},... | collective-permute-start | bytes 12296 | tf_op jit(solution)/shard_map/ppermute | solution.py:424
  77.8 6.9 %collective-permute-start.18 = (bf16[128,640]{1,0:T(8,128)(2,1)S(1)}, bf16[128,640]{1,0:T(8,128)(2,1)S(1)}, u32[]{:S(2)}, u32[]{:S(2)}) collective-permute-start(bf16[128,640]{1,0:T(8,128)(2,1)S(1)} %shard_map.161.refs_3_), channel_id=1, source_target_pairs={{0,1},{1,0},{2,3},{3,2},{4,5},{5,4},{6,7},{7,6},{8,9},{9,8},{10,11... | collective-permute-start | bytes 491528 | tf_op jit(solution)/shard_map/ppermute | solution.py:513

commit v4 on v3

--- a/solution.py
+++ b/solution.py
@@ -40,7 +40,7 @@
     return dot(high, b) + (dot(mid, b) + dot(low, b))
 
 
-HBM, FAR, NEAR, VMEM, SCALARS = "hbm", "far", "near", "vmem", "scalars"
+HBM, FAR, VMEM, SCALARS = "hbm", "far", "vmem", "scalars"
 
 
 class Arriving:
@@ -61,12 +61,11 @@
 
 def call(body, outs, *args, scratch=(), after=(), micros=0.1, limit=12):
     args += tuple((one, "token") for one in after)
-    count, far = len(args), [i for i, (_, where) in enumerate(args) if where in (HBM, NEAR)]
+    count, far = len(args), [i for i, (_, where) in enumerate(args) if where == HBM]
     leaves, tree = jax.tree.flatten(outs)
     specs = {
         HBM: pl.BlockSpec(memory_space=pl.ANY),
         FAR: pl.BlockSpec(memory_space=pl.ANY),
-        NEAR: pl.BlockSpec(memory_space=pl.ANY),
         "token": pl.BlockSpec(memory_space=pl.ANY),
         VMEM: pl.BlockSpec(memory_space=pltpu.VMEM),
         SCALARS: pl.BlockSpec(memory_space=pltpu.SMEM),
@@ -202,6 +201,7 @@
 GN_ROW, LN_ROW = 3 * STEPS, 3 * STEPS + 1
 EXTRA = 16
 HEAD = COLS + EXTRA
+PAD = 32
 
 
 def stats_rows(stats):
@@ -245,12 +245,6 @@
     block_ref[COLS:HEAD] = stats_rows(stats)
     for copy in copies:
         copy.wait()
-
-
-def join_body(low_ref, up_ref, down_ref, up_block_ref, down_block_ref):
-    for source, target in ((up_ref, up_block_ref), (down_ref, down_block_ref)):
-        target[:COLS] = source[...]
-        target[COLS:] = low_ref[...]
 
 
 def pack_body(stats_ref, up_ref, down_ref, up_block_ref, down_block_ref):
@@ -321,9 +315,10 @@
     for ref in refs[: PATCHES - 1]:
         total = merge(total, patches(1, stats_of(ref)))
     taps = [w_ref.at[1, t] for t in range(3)]
-    conv_in_ref[...], h_ref[...], attn_in_ref[...], query_ref[...] = level(
+    conv_in_ref[:COLS], h_ref[...], attn_in_ref[...], query_ref[...] = level(
         0, total, x_ref[...], rims_ref, prep_ref, taps, q_ref
     )
+    conv_in_ref[COLS:] = jnp.zeros((PAD, WIDTH), BF)
 
 
 def keys_of(rows, kv_ref, out_ref):
@@ -334,22 +329,29 @@
     keys_of(refs[:-2], *refs[-2:])
 
 
+def pair_scores(query_ref, parts, pair):
+    first_half = lax.broadcasted_iota(jnp.int32, (COLS, 128), 1) < WIDTH // HEADS
+    lanes = slice(pair * 128, (pair + 1) * 128)
+    query = query_ref[:, lanes]
+    zero = jnp.zeros_like(query)
+    stacked = jnp.concatenate(
+        [jnp.where(first_half, query, zero), jnp.where(first_half, zero, query)], axis=0
+    )
+    return [
+        lax.dot_general(stacked, ref[:, lanes], (((1,), (1,)), ((), ())), preferred_element_type=F32)
+        for ref in parts
+    ]
+
+
 def attend(query_ref, parts, mixed_ref):
     first_half = lax.broadcasted_iota(jnp.int32, (COLS, 128), 1) < WIDTH // HEADS
+    following = pair_scores(query_ref, parts, 0)
     for pair in range(PAIRS):
         lanes = slice(pair * 128, (pair + 1) * 128)
         values = slice(WIDTH + pair * 128, WIDTH + (pair + 1) * 128)
-        query = query_ref[:, lanes]
-        zero = jnp.zeros_like(query)
-        stacked = jnp.concatenate(
-            [jnp.where(first_half, query, zero), jnp.where(first_half, zero, query)], axis=0
-        )
-        scores = [
-            lax.dot_general(
-                stacked, ref[:, lanes], (((1,), (1,)), ((), ())), preferred_element_type=F32
-            )
-            for ref in parts
-        ]
+        scores = following
+        if pair + 1 < PAIRS:
+            following = pair_scores(query_ref, parts, pair + 1)
         top = functools.reduce(jnp.maximum, [jnp.max(s, axis=1, keepdims=True) for s in scores])
         weights = [jnp.exp2(s - top) for s in scores]
         total = sum(jnp.sum(w, axis=1, keepdims=True) for w in weights)
@@ -420,7 +422,6 @@
     full = (COLS, WIDTH)
     whole = (1,) + full
     stats_shape = fast((8, 128), F32)
-    near = lambda arrays: [(one, NEAR) for one in arrays]
     shift = lambda x, far: lax.ppermute(
         x, "patch", [(i, (i + far) % PATCHES) for i in range(PATCHES)]
     )
@@ -465,7 +466,7 @@
     keys = lambda blocks, after=(): call(
         keys_body,
         fast((len(blocks) * COLS, 2 * WIDTH), BF),
-        *near(blocks),
+        *[(one, VMEM) for one in blocks],
         (kv_w, VMEM),
         after=after,
     )
@@ -487,7 +488,7 @@
     far_keys = keys(ring3, (ring3[0],))
     conv_in, hidden, attn_in, query = call(
         level_body,
-        (fast(full, BF), fast(full, F32), fast(full, BF), fast(full, BF)),
+        (fast((COLS + PAD, WIDTH), BF), fast(full, F32), fast(full, BF), fast(full, BF)),
         (state, VMEM),
         (rims, VMEM),
         (prep, VMEM),
@@ -503,21 +504,20 @@
         (hidden, VMEM),
         *early,
         (attn_in, VMEM),
-        *near(late),
+        *[(one, VMEM) for one in late],
         *[(w, VMEM) for w in weights],
         scratch=(pltpu.VMEM(((1 + len(late)) * COLS, 2 * WIDTH), BF), pltpu.VMEM(full, BF)),
-        micros=4.0,
+        limit=20,
     )
     early = [(one, VMEM) for one in (near_keys, mid_keys, far_keys)]
     eps = attend_to((kv_w, out_w), early, ring4)
     exchange = lambda x: lax.ppermute(x, "cfg", [(0, 1), (1, 0)])
     other = exchange(eps)
-    block = fast((2 * COLS, WIDTH), BF)
-    joined = call(
-        join_body, (block, block), (conv_in, VMEM), *[(one, VMEM) for one in ring1], after=(eps,)
-    )
-    ring2 = [up(joined[0]), down(joined[1])]
-    near_keys = keys(ring1, (joined[0],))
+    ring1 = later(ring1, (eps,))
+    ring2 = [up(ring1[0]), down(ring1[1])]
+    near_keys = keys(ring1, (eps,))
+    (conv_in,) = later([conv_in], (near_keys,))
+    rims_in = [up(conv_in), down(conv_in)]
     state, stats = call(
         functools.partial(update_body, 0),
         (fast(whole, F32), stats_shape),
@@ -533,7 +533,7 @@
         pack_body, (block, block), (stats, VMEM), *[(one, VMEM) for one in ring2], after=(state,)
     )
     ring3 = [up(packed[0]), down(packed[1])]
-    rims = conv_rims(COLS, ring2, (packed[0],))
+    rims = conv_rims(0, rims_in, (packed[0],))
     mid_keys = keys(ring2, (rims,))
     three, two = call(
         partial_body,

time: 87.5 us -> 86.1 us (0.984)
  Pallas kernels: 28.6 us -> 24.8 us
  starting transfers between devices: 33.4 us -> 35.2 us
    pallas_call x20 -> x19, Pallas kernels: 28.6 us -> 24.7 us  [call(): pl.pallas_call(wrapped, out_shape=jax.tree.unflatten(tree, leaves), in_sp...]
    ppermute x6 -> x7, starting transfers between devices: 15.6 us -> 17.7 us  [shards(): down = lambda x: lax.ppermute(x, 'patch', downward)]
    ppermute x8 -> x9, waiting for transfers between devices: 9.67 us -> 11.3 us  [shards(): up = lambda x: lax.ppermute(x, 'patch', upward)]
    ppermute x2, waiting for transfers between devices: 6.16 us -> 4.89 us  [shards(): exchange = lambda x: lax.ppermute(x, 'cfg', [(0, 1), (1, 0)])]
    ppermute x2, starting transfers between devices: 6.47 us -> 5.3 us  [shards(): exchange = lambda x: lax.ppermute(x, 'cfg', [(0, 1), (1, 0)])]
    ppermute x8 -> x9, starting transfers between devices: 3.62 us -> 4.74 us  [shards(): up = lambda x: lax.ppermute(x, 'patch', upward)]
  transfers between devices with their start and end apart: 19 -> 21, of which waited for: 11 -> 10; matrix products, arithmetic and copies ran while one was open for 0% -> 0% of each run, Pallas kernels for 25% -> 22%
where the time goes in v4:
time: 86.1 us; the launch traced here: 85 us
  starting transfers between devices  35.2 us (41%)
  Pallas kernels  24.8 us (29%)
  waiting for transfers between devices  24.1 us (28%)
    pallas_call x19, Pallas kernels, call(): pl.pallas_call(wrapped, out_shape=jax.tree.unflatten(tree, leaves), in_sp...  24.7 us
    ppermute x7, starting transfers between devices, shards(): down = lambda x: lax.ppermute(x, 'patch', downward)  17.7 us
    ppermute x9, waiting for transfers between devices, shards(): up = lambda x: lax.ppermute(x, 'patch', upward)  11.3 us
    ppermute x3, starting transfers between devices, shards(): lax.ppermute(x, 'patch', [(i, (i + far) % PATCHES) for i in range(PATCHES)])  7.48 us
    ppermute x3, waiting for transfers between devices, shards(): lax.ppermute(x, 'patch', [(i, (i + far) % PATCHES) for i in range(PATCHES)])  6.77 us
    ppermute x2, starting transfers between devices, shards(): exchange = lambda x: lax.ppermute(x, 'cfg', [(0, 1), (1, 0)])  5.3 us
    ppermute x2, waiting for transfers between devices, shards(): exchange = lambda x: lax.ppermute(x, 'cfg', [(0, 1), (1, 0)])  4.89 us
    ppermute x9, starting transfers between devices, shards(): up = lambda x: lax.ppermute(x, 'patch', upward)  4.74 us
  transfers between devices with their start and end apart: 21, of which 10 were waited for; matrix products, arithmetic and copies ran while one was open for 0% of the time, Pallas kernels for 22%

profile of v4, /device:TPU:2, one launch (start us, length us, event | category | flops | bytes accessed | tf_op | source)
XLA Modules:
  0.0 85.0 jit_solution(2668755335817229677)
XLA Ops:
  0.6 0.1 add_convert_fusion.refs_3_.refs_0_
  0.7 1.8 %shard_map.140 = (bf16[272,640]{1,0:T(8,128)(2,1)S(1)}, f32[1,128,640]{2,1,0:T(8,128)S(1)}, f32[8,128]{1,0:T(8,128)S(1)}) custom-call(f32[1,128,640]{2,1,0:T(8,128)} %refs_0_.2, bf16[128,640]{1,0:T(8,128)(2,1)} %bitcast.6, bf16[128,640]{1,0:T(8,128)(2,1)} %bitcast.7, f32[3]{0:T(128)S(1)} %add_convert_fusion.refs_3_.refs_0_), custom_call_target="tpu_custom_call" | custom-call | bytes 340000 | tf_op jit(solution)/shard_map/pallas_call | solution.py:93
  2.5 5.9 %collective-permute-start.1 = (bf16[272,640]{1,0:T(8,128)(2,1)S(1)}, bf16[272,640]{1,0:T(8,128)(2,1)S(1)}, u32[]{:S(2)}, u32[]{:S(2)}) collective-permute-start(bf16[272,640]{1,0:T(8,128)(2,1)S(1)} %get-tuple-element.33.refs_10_.refs_5_), channel_id=1, source_target_pairs={{2,0},{4,2},{6,4},{8,6},{10,8},{12,10},{14,12},{0,14},{3,1},{5,3},... | collective-permute-start | bytes 1044488 | tf_op jit(solution)/shard_map/ppermute | solution.py:421
  8.4 0.0 collective-permute-start
  8.4 3.4 %collective-permute-start.2 = (f32[8,128]{1,0:T(8,128)S(1)}, f32[8,128]{1,0:T(8,128)S(1)}, u32[]{:S(2)}, u32[]{:S(2)}) collective-permute-start(f32[8,128]{1,0:T(8,128)S(1)} %get-tuple-element.37), channel_id=1, source_target_pairs={{0,8},{2,10},{4,12},{6,14},{8,0},{10,2},{12,4},{14,6},{1,9},{3,11}... | collective-permute-start | bytes 12296 | tf_op jit(solution)/shard_map/ppermute | solution.py:425
  11.8 4.1 %shard_map.141 = (f32[8,640]{1,0:T(8,128)S(1)}, bf16[3,3,640,640]{3,2,1,0:T(8,128)(2,1)S(1)}, bf16[640,640]{1,0:T(8,128)(2,1)S(1)}, bf16[640,1280]{1,0:T(8,128)(2,1)S(1)}, bf16[640,640]{1,0:T(8,128)(2,1)S(1)}) custom-call(bf16[3,3,640,640]{3,2,1,0:T(8,128)(2,1)} %refs_0_.3, bf16[640,640]{1,0:T(8,128)(2,1)} %refs_1_.1, bf16[640,1280]{1,0:T(8,128)(2,1)} %refs_2_.1, ...), custom_call_target="tpu_custom_call" | custom-call | bytes 340000 | tf_op jit(solution)/shard_map/pallas_call | solution.py:93
  15.9 3.6 %collective-permute-done.2.refs_3_.refs_12_ = f32[8,128]{1,0:T(8,128)S(1)} collective-permute-done((f32[8,128]{1,0:T(8,128)S(1)}, f32[8,128]{1,0:T(8,128)S(1)}, u32[]{:S(2)}, u32[]{:S(2)}) %collective-permute-start.2) | collective-permute-done | bytes 4128 | tf_op jit(solution)/shard_map/ppermute | solution.py:425
  19.6 0.0 collective-permute-done.1.refs_1_.refs_2_.refs_7_
  19.6 0.2 collective-permute-start.4
  19.8 1.9 %collective-permute-start.3 = (bf16[144,640]{1,0:T(8,128)(2,1)S(1)}, bf16[144,640]{1,0:T(8,128)(2,1)S(1)}, u32[]{:S(2)}, u32[]{:S(2)}) collective-permute-start(bf16[144,640]{1,0:T(8,128)(2,1)S(1)} %get-tuple-element.38.refs_4_), channel_id=1, source_target_pairs={{0,2},{2,4},{4,6},{6,8},{8,10},{10,12},{12,14},{14,0},{1,3},{3,5},... | collective-permute-start | bytes 552968 | tf_op jit(solution)/shard_map/ppermute | solution.py:420
  21.7 1.7 %shard_map.143.refs_3_.refs_1_ = f32[128,640]{1,0:T(8,128)S(1)} custom-call(f32[3]{0:T(128)S(1)} %add_convert_fusion.refs_3_.refs_0_, bf16[272,640]{1,0:T(8,128)(2,1)S(1)} %collective-permute-done.refs_0_.refs_1_.refs_6_, bf16[272,640]{1,0:T(8,128)(2,1)S(1)} %collective-permute-done.1.refs_1_.refs_2_.refs_7_, ...), custom_call_target="tpu_custom_call" | custom-call | bytes 340000 | tf_op jit(solution)/shard_map/pallas_call | solution.py:93
  23.4 0.7 shard_map.144.refs_2_
  24.1 1.1 %collective-permute-done.4.refs_1_ = bf16[144,640]{1,0:T(8,128)(2,1)S(1)} collective-permute-done((bf16[144,640]{1,0:T(8,128)(2,1)S(1)}, bf16[144,640]{1,0:T(8,128)(2,1)S(1)}, u32[]{:S(2)}, u32[]{:S(2)}) %collective-permute-start.4) | collective-permute-done | bytes 184352 | tf_op jit(solution)/shard_map/ppermute | solution.py:421
  25.2 1.4 %collective-permute-done.3.refs_0_ = bf16[144,640]{1,0:T(8,128)(2,1)S(1)} collective-permute-done((bf16[144,640]{1,0:T(8,128)(2,1)S(1)}, bf16[144,640]{1,0:T(8,128)(2,1)S(1)}, u32[]{:S(2)}, u32[]{:S(2)}) %collective-permute-start.3) | collective-permute-done | bytes 184352 | tf_op jit(solution)/shard_map/ppermute | solution.py:420
  26.6 0.8 collective-permute-start.5
  27.3 2.5 %collective-permute-start.6 = (bf16[144,640]{1,0:T(8,128)(2,1)S(1)}, bf16[144,640]{1,0:T(8,128)(2,1)S(1)}, u32[]{:S(2)}, u32[]{:S(2)}) collective-permute-start(bf16[144,640]{1,0:T(8,128)(2,1)S(1)} %get-tuple-element.43.refs_1_.refs_9_), channel_id=1, source_target_pairs={{2,0},{4,2},{6,4},{8,6},{10,8},{12,10},{14,12},{0,14},{3,1},{5,3},... | collective-permute-start | bytes 552968 | tf_op jit(solution)/shard_map/ppermute | solution.py:421
  29.8 0.7 shard_map.146.refs_2_.refs_3_
  30.5 2.8 %collective-permute-done.5.refs_0_ = bf16[144,640]{1,0:T(8,128)(2,1)S(1)} collective-permute-done((bf16[144,640]{1,0:T(8,128)(2,1)S(1)}, bf16[144,640]{1,0:T(8,128)(2,1)S(1)}, u32[]{:S(2)}, u32[]{:S(2)}) %collective-permute-start.5) | collective-permute-done | bytes 184352 | tf_op jit(solution)/shard_map/ppermute | solution.py:420
  33.3 0.0 collective-permute-done.6.refs_1_
  33.3 1.4 %shard_map.148 = (bf16[160,640]{1,0:T(8,128)(2,1)S(1)}, f32[128,640]{1,0:T(8,128)S(1)}, bf16[128,640]{1,0:T(8,128)(2,1)S(1)}, bf16[128,640]{1,0:T(8,128)(2,1)S(1)}) custom-call(f32[1,128,640]{2,1,0:T(8,128)S(1)} %get-tuple-element.35.refs_0_.refs_2_, f32[128,640]{1,0:T(8,128)S(1)} %shard_map.143.refs_3_.refs_1_, ...), custom_call_target="tpu_custom_call" | custom-call | bytes 340000 | tf_op jit(solution)/shard_map/pallas_call | solution.py:93
  34.7 3.3 %collective-permute-start.10 = (bf16[128,640]{1,0:T(8,128)(2,1)S(1)}, bf16[128,640]{1,0:T(8,128)(2,1)S(1)}, u32[]{:S(2)}, u32[]{:S(2)}) collective-permute-start(bf16[128,640]{1,0:T(8,128)(2,1)S(1)} %get-tuple-element.48.refs_5_), channel_id=1, source_target_pairs={{2,0},{4,2},{6,4},{8,6},{10,8},{12,10},{14,12},{0,14},{3,1},{5,3},... | collective-permute-start | bytes 491528 | tf_op jit(solution)/shard_map/ppermute | solution.py:421
  38.0 0.0 collective-permute-start.9
  38.0 0.7 shard_map.149.refs_4_
  38.7 2.6 %collective-permute-done.7.refs_6_ = bf16[144,640]{1,0:T(8,128)(2,1)S(1)} collective-permute-done((bf16[144,640]{1,0:T(8,128)(2,1)S(1)}, bf16[144,640]{1,0:T(8,128)(2,1)S(1)}, u32[]{:S(2)}, u32[]{:S(2)}) %collective-permute-start.7) | collective-permute-done | bytes 184352 | tf_op jit(solution)/shard_map/ppermute | solution.py:420
  41.4 2.9 %shard_map.150.refs_2_.refs_3_ = bf16[128,640]{1,0:T(8,128)(2,1)S(1)} custom-call(bf16[128,640]{1,0:T(8,128)(2,1)S(1)} %get-tuple-element.46.refs_0_, f32[128,640]{1,0:T(8,128)S(1)} %get-tuple-element.47.refs_1_, bf16[256,1280]{1,0:T(8,128)(2,1)S(1)} %shard_map.144.refs_2_, bf16[256,1280]{1,0:T(8,128)(2,1)S(1)} %shard_map.146.refs_2_.refs_3_, ...), custom_call_target="tpu_custom_call" | custom-call | bytes 340000 | tf_op jit(solution)/shard_map/pallas_call | solution.py:93
  44.3 3.3 %collective-permute-start.8 = (bf16[128,640]{1,0:T(8,128)(2,1)S(1)}, bf16[128,640]{1,0:T(8,128)(2,1)S(1)}, u32[]{:S(2)}, u32[]{:S(2)}) collective-permute-start(bf16[128,640]{1,0:T(8,128)(2,1)S(1)} %shard_map.150.refs_2_.refs_3_), channel_id=1, source_target_pairs={{0,1},{1,0},{2,3},{3,2},{4,5},{5,4},{6,7},{7,6},{8,9},{9,8},{10,11... | collective-permute-start | bytes 491528 | tf_op jit(solution)/shard_map/ppermute | solution.py:514
  47.6 3.2 %collective-permute-start.12 = (bf16[128,640]{1,0:T(8,128)(2,1)S(1)}, bf16[128,640]{1,0:T(8,128)(2,1)S(1)}, u32[]{:S(2)}, u32[]{:S(2)}) collective-permute-start(bf16[128,640]{1,0:T(8,128)(2,1)S(1)} %get-tuple-element.51.refs_1_), channel_id=1, source_target_pairs={{2,0},{4,2},{6,4},{8,6},{10,8},{12,10},{14,12},{0,14},{3,1},{5,3},... | collective-permute-start | bytes 491528 | tf_op jit(solution)/shard_map/ppermute | solution.py:421
  50.8 0.7 shard_map.152.refs_5_.refs_1_.refs_2_
  51.5 0.1 collective-permute-start.16
  51.6 2.0 %collective-permute-start.15 = (bf16[160,640]{1,0:T(8,128)(2,1)S(1)}, bf16[160,640]{1,0:T(8,128)(2,1)S(1)}, u32[]{:S(2)}, u32[]{:S(2)}) collective-permute-start(bf16[160,640]{1,0:T(8,128)(2,1)S(1)} %shard_map.155), channel_id=1, source_target_pairs={{0,2},{2,4},{4,6},{6,8},{8,10},{10,12},{12,14},{14,0},{1,3},{3,5},... | collective-permute-start | bytes 614408 | tf_op jit(solution)/shard_map/ppermute | solution.py:420
  53.6 1.3 %shard_map.153 = (f32[1,128,640]{2,1,0:T(8,128)S(1)}, f32[8,128]{1,0:T(8,128)S(1)}) custom-call(f32[3]{0:T(128)S(1)} %add_convert_fusion.refs_3_.refs_0_, f32[8,640]{1,0:T(8,128)S(1)} %get-tuple-element.34.refs_2_.refs_1_.refs_5_, f32[1,128,640]{2,1,0:T(8,128)S(1)} %get-tuple-element.35.refs_0_.refs_2_, bf16[128,640]{1,0:T(8,128)(2,1)S(1)} %shard_map.150.refs_2_.refs_3_, ...), custom_call_target="tpu_custom_call" | custom-call | bytes 340000 | tf_op jit(solution)/shard_map/pallas_call | solution.py:93
  54.9 0.0 collective-permute-done.12.refs_2_.refs_1_
  55.0 2.4 %collective-permute-start.14 = (bf16[144,640]{1,0:T(8,128)(2,1)S(1)}, bf16[144,640]{1,0:T(8,128)(2,1)S(1)}, u32[]{:S(2)}, u32[]{:S(2)}) collective-permute-start(bf16[144,640]{1,0:T(8,128)(2,1)S(1)} %get-tuple-element.55), channel_id=1, source_target_pairs={{2,0},{4,2},{6,4},{8,6},{10,8},{12,10},{14,12},{0,14},{3,1},{5,3},... | collective-permute-start | bytes 552968 | tf_op jit(solution)/shard_map/ppermute | solution.py:421
  57.4 1.2 %collective-permute-done.15.refs_1_ = bf16[160,640]{1,0:T(8,128)(2,1)S(1)} collective-permute-done((bf16[160,640]{1,0:T(8,128)(2,1)S(1)}, bf16[160,640]{1,0:T(8,128)(2,1)S(1)}, u32[]{:S(2)}, u32[]{:S(2)}) %collective-permute-start.15) | collective-permute-done | bytes 204832 | tf_op jit(solution)/shard_map/ppermute | solution.py:420
  58.6 1.7 %shard_map.156.refs_3_.refs_4_ = f32[128,640]{1,0:T(8,128)S(1)} custom-call(f32[3]{0:T(128)S(1)} %add_convert_fusion.refs_3_.refs_0_, bf16[160,640]{1,0:T(8,128)(2,1)S(1)} %collective-permute-done.15.refs_1_, bf16[160,640]{1,0:T(8,128)(2,1)S(1)} %collective-permute-done.16.refs_2_, bf16[3,3,640,640]{3,2,1,0:T(8,128)(2,1)S(1)} %get-tuple-element.36.refs_3_.refs_6_, ...), custom_call_target="tpu_custom_call" | custom-call | bytes 340000 | tf_op jit(solution)/shard_map/pallas_call | solution.py:93
  60.3 0.7 shard_map.157.refs_3_
  61.0 3.3 %collective-permute-done.13.refs_1_.refs_0_ = bf16[144,640]{1,0:T(8,128)(2,1)S(1)} collective-permute-done((bf16[144,640]{1,0:T(8,128)(2,1)S(1)}, bf16[144,640]{1,0:T(8,128)(2,1)S(1)}, u32[]{:S(2)}, u32[]{:S(2)}) %collective-permute-start.13) | collective-permute-done | bytes 184352 | tf_op jit(solution)/shard_map/ppermute | solution.py:420
  64.3 0.1 collective-permute-start.19
  64.4 1.3 %collective-permute-start.18 = (f32[8,128]{1,0:T(8,128)S(1)}, f32[8,128]{1,0:T(8,128)S(1)}, u32[]{:S(2)}, u32[]{:S(2)}) collective-permute-start(f32[8,128]{1,0:T(8,128)S(1)} %get-tuple-element.58), channel_id=1, source_target_pairs={{0,10},{2,12},{4,14},{6,0},{8,2},{10,4},{12,6},{14,8},{1,11},{3,13... | collective-permute-start | bytes 12296 | tf_op jit(solution)/shard_map/ppermute | solution.py:425
  65.7 2.8 %collective-permute-start.17 = (f32[8,128]{1,0:T(8,128)S(1)}, f32[8,128]{1,0:T(8,128)S(1)}, u32[]{:S(2)}, u32[]{:S(2)}) collective-permute-start(f32[8,128]{1,0:T(8,128)S(1)} %get-tuple-element.57.refs_0_.refs_2_), channel_id=1, source_target_pairs={{0,6},{2,8},{4,10},{6,12},{8,14},{10,0},{12,2},{14,4},{1,7},{3,9},... | collective-permute-start | bytes 12296 | tf_op jit(solution)/shard_map/ppermute | solution.py:425
  68.5 0.7 shard_map.161.refs_4_
  69.2 0.9 %collective-permute-done.18.refs_2_ = f32[8,128]{1,0:T(8,128)S(1)} collective-permute-done((f32[8,128]{1,0:T(8,128)S(1)}, f32[8,128]{1,0:T(8,128)S(1)}, u32[]{:S(2)}, u32[]{:S(2)}) %collective-permute-start.18) | collective-permute-done | bytes 4128 | tf_op jit(solution)/shard_map/ppermute | solution.py:425
  70.1 2.2 %collective-permute-done.17.refs_1_ = f32[8,128]{1,0:T(8,128)S(1)} collective-permute-done((f32[8,128]{1,0:T(8,128)S(1)}, f32[8,128]{1,0:T(8,128)S(1)}, u32[]{:S(2)}, u32[]{:S(2)}) %collective-permute-start.17) | collective-permute-done | bytes 4128 | tf_op jit(solution)/shard_map/ppermute | solution.py:425
  72.3 1.4 %shard_map.159 = (bf16[128,640]{1,0:T(8,128)(2,1)S(1)}, f32[128,640]{1,0:T(8,128)S(1)}, bf16[128,640]{1,0:T(8,128)(2,1)S(1)}) custom-call(f32[8,128]{1,0:T(8,128)S(1)} %get-tuple-element.57.refs_0_.refs_2_, f32[8,128]{1,0:T(8,128)S(1)} %collective-permute-done.17.refs_1_, f32[8,128]{1,0:T(8,128)S(1)} %collective-permute-done.18.refs_2_, ...), custom_call_target="tpu_custom_call" | custom-call | bytes 340000 | tf_op jit(solution)/shard_map/pallas_call | solution.py:93
  73.7 2.9 %shard_map.162.refs_3_ = bf16[128,640]{1,0:T(8,128)(2,1)S(1)} custom-call(bf16[128,640]{1,0:T(8,128)(2,1)S(1)} %get-tuple-element.59.refs_0_, f32[128,640]{1,0:T(8,128)S(1)} %get-tuple-element.60.refs_1_, bf16[256,1280]{1,0:T(8,128)(2,1)S(1)} %shard_map.152.refs_5_.refs_1_.refs_2_, bf16[256,1280]{1,0:T(8,128)(2,1)S(1)} %shard_map.157.refs_3_, ...), custom_call_target="tpu_custom_call" | custom-call | bytes 340000 | tf_op jit(solution)/shard_map/pallas_call | solution.py:93
  76.6 2.0 %collective-permute-start.20 = (bf16[128,640]{1,0:T(8,128)(2,1)S(1)}, bf16[128,640]{1,0:T(8,128)(2,1)S(1)}, u32[]{:S(2)}, u32[]{:S(2)}) collective-permute-start(bf16[128,640]{1,0:T(8,128)(2,1)S(1)} %shard_map.162.refs_3_), channel_id=1, source_target_pairs={{0,1},{1,0},{2,3},{3,2},{4,5},{5,4},{6,7},{7,6},{8,9},{9,8},{10,11... | collective-permute-start | bytes 491528 | tf_op jit(solution)/shard_map/ppermute | solution.py:514
  78.6 4.9 %collective-permute-done.20.refs_4_ = bf16[128,640]{1,0:T(8,128)(2,1)S(1)} collective-permute-done((bf16[128,640]{1,0:T(8,128)(2,1)S(1)}, bf16[128,640]{1,0:T(8,128)(2,1)S(1)}, u32[]{:S(2)}, u32[]{:S(2)}) %collective-permute-start.20) | collective-permute-done | bytes 163872 | tf_op jit(solution)/shard_map/ppermute | solution.py:514
  83.5 1.5 %shard_map.163 = (f32[1,128,640]{2,1,0:T(8,128)}, f32[1,128,640]{2,1,0:T(8,128)}) custom-call(f32[3]{0:T(128)S(1)} %add_convert_fusion.refs_3_.refs_0_, f32[8,640]{1,0:T(8,128)S(1)} %get-tuple-element.34.refs_2_.refs_1_.refs_5_, f32[1,128,640]{2,1,0:T(8,128)S(1)} %get-tuple-element.52.refs_3_.refs_2_, bf16[128,640]{1,0:T(8,128)(2,1)S(1)} %shard_map.162.refs_3_, ...), custom_call_target="tpu_custom_call" | custom-call | bytes 340000 | tf_op jit(solution)/shard_map/pallas_call | solution.py:93
  (19 shorter events, 0.1 us)
Async XLA Ops:
  2.5 17.1 %collective-permute-start.1 = (bf16[272,640]{1,0:T(8,128)(2,1)S(1)}, bf16[272,640]{1,0:T(8,128)(2,1)S(1)}, u32[]{:S(2)}, u32[]{:S(2)}) collective-permute-start(bf16[272,640]{1,0:T(8,128)(2,1)S(1)} %get-tuple-element.33.refs_10_.refs_5_), channel_id=1, source_target_pairs={{2,0},{4,2},{6,4},{8,6},{10,8},{12,10},{14,12},{0,14},{3,1},{5,3},... | collective-permute-start | bytes 1044488 | tf_op jit(solution)/shard_map/ppermute | solution.py:421
  8.4 11.1 %collective-permute-start = (bf16[272,640]{1,0:T(8,128)(2,1)S(1)}, bf16[272,640]{1,0:T(8,128)(2,1)S(1)}, u32[]{:S(2)}, u32[]{:S(2)}) collective-permute-start(bf16[272,640]{1,0:T(8,128)(2,1)S(1)} %get-tuple-element.33.refs_10_.refs_5_), channel_id=1, source_target_pairs={{0,2},{2,4},{4,6},{6,8},{8,10},{10,12},{12,14},{14,0},{1,3},{3,5},... | collective-permute-start | bytes 1044488 | tf_op jit(solution)/shard_map/ppermute | solution.py:420
  8.4 11.1 %collective-permute-start.2 = (f32[8,128]{1,0:T(8,128)S(1)}, f32[8,128]{1,0:T(8,128)S(1)}, u32[]{:S(2)}, u32[]{:S(2)}) collective-permute-start(f32[8,128]{1,0:T(8,128)S(1)} %get-tuple-element.37), channel_id=1, source_target_pairs={{0,8},{2,10},{4,12},{6,14},{8,0},{10,2},{12,4},{14,6},{1,9},{3,11}... | collective-permute-start | bytes 12296 | tf_op jit(solution)/shard_map/ppermute | solution.py:425
  19.6 5.6 %collective-permute-start.4 = (bf16[144,640]{1,0:T(8,128)(2,1)S(1)}, bf16[144,640]{1,0:T(8,128)(2,1)S(1)}, u32[]{:S(2)}, u32[]{:S(2)}) collective-permute-start(bf16[144,640]{1,0:T(8,128)(2,1)S(1)} %get-tuple-element.40), channel_id=1, source_target_pairs={{2,0},{4,2},{6,4},{8,6},{10,8},{12,10},{14,12},{0,14},{3,1},{5,3},... | collective-permute-start | bytes 552968 | tf_op jit(solution)/shard_map/ppermute | solution.py:421
  19.8 6.7 %collective-permute-start.3 = (bf16[144,640]{1,0:T(8,128)(2,1)S(1)}, bf16[144,640]{1,0:T(8,128)(2,1)S(1)}, u32[]{:S(2)}, u32[]{:S(2)}) collective-permute-start(bf16[144,640]{1,0:T(8,128)(2,1)S(1)} %get-tuple-element.38.refs_4_), channel_id=1, source_target_pairs={{0,2},{2,4},{4,6},{6,8},{8,10},{10,12},{12,14},{14,0},{1,3},{3,5},... | collective-permute-start | bytes 552968 | tf_op jit(solution)/shard_map/ppermute | solution.py:420
  26.6 6.7 %collective-permute-start.5 = (bf16[144,640]{1,0:T(8,128)(2,1)S(1)}, bf16[144,640]{1,0:T(8,128)(2,1)S(1)}, u32[]{:S(2)}, u32[]{:S(2)}) collective-permute-start(bf16[144,640]{1,0:T(8,128)(2,1)S(1)} %get-tuple-element.42.refs_0_.refs_3_.refs_8_), channel_id=1, source_target_pairs={{0,2},{2,4},{4,6},{6,8},{8,10},{10,12},{12,14},{14,0},{1,3},{3,5},... | collective-permute-start | bytes 552968 | tf_op jit(solution)/shard_map/ppermute | solution.py:420
  27.3 6.0 %collective-permute-start.6 = (bf16[144,640]{1,0:T(8,128)(2,1)S(1)}, bf16[144,640]{1,0:T(8,128)(2,1)S(1)}, u32[]{:S(2)}, u32[]{:S(2)}) collective-permute-start(bf16[144,640]{1,0:T(8,128)(2,1)S(1)} %get-tuple-element.43.refs_1_.refs_9_), channel_id=1, source_target_pairs={{2,0},{4,2},{6,4},{8,6},{10,8},{12,10},{14,12},{0,14},{3,1},{5,3},... | collective-permute-start | bytes 552968 | tf_op jit(solution)/shard_map/ppermute | solution.py:421
  33.3 8.0 %collective-permute-start.7 = (bf16[144,640]{1,0:T(8,128)(2,1)S(1)}, bf16[144,640]{1,0:T(8,128)(2,1)S(1)}, u32[]{:S(2)}, u32[]{:S(2)}) collective-permute-start(bf16[144,640]{1,0:T(8,128)(2,1)S(1)} %get-tuple-element.44.refs_10_.refs_0_.refs_3_), channel_id=1, source_target_pairs={{0,2},{2,4},{4,6},{6,8},{8,10},{10,12},{12,14},{14,0},{1,3},{3,5},... | collective-permute-start | bytes 552968 | tf_op jit(solution)/shard_map/ppermute | solution.py:420
  34.7 12.8 %collective-permute-start.10 = (bf16[128,640]{1,0:T(8,128)(2,1)S(1)}, bf16[128,640]{1,0:T(8,128)(2,1)S(1)}, u32[]{:S(2)}, u32[]{:S(2)}) collective-permute-start(bf16[128,640]{1,0:T(8,128)(2,1)S(1)} %get-tuple-element.48.refs_5_), channel_id=1, source_target_pairs={{2,0},{4,2},{6,4},{8,6},{10,8},{12,10},{14,12},{0,14},{3,1},{5,3},... | collective-permute-start | bytes 491528 | tf_op jit(solution)/shard_map/ppermute | solution.py:421
  38.0 9.5 %collective-permute-start.9 = (bf16[128,640]{1,0:T(8,128)(2,1)S(1)}, bf16[128,640]{1,0:T(8,128)(2,1)S(1)}, u32[]{:S(2)}, u32[]{:S(2)}) collective-permute-start(bf16[128,640]{1,0:T(8,128)(2,1)S(1)} %get-tuple-element.48.refs_5_), channel_id=1, source_target_pairs={{0,2},{2,4},{4,6},{6,8},{8,10},{10,12},{12,14},{14,0},{1,3},{3,5},... | collective-permute-start | bytes 491528 | tf_op jit(solution)/shard_map/ppermute | solution.py:420
  44.3 9.3 %collective-permute-start.8 = (bf16[128,640]{1,0:T(8,128)(2,1)S(1)}, bf16[128,640]{1,0:T(8,128)(2,1)S(1)}, u32[]{:S(2)}, u32[]{:S(2)}) collective-permute-start(bf16[128,640]{1,0:T(8,128)(2,1)S(1)} %shard_map.150.refs_2_.refs_3_), channel_id=1, source_target_pairs={{0,1},{1,0},{2,3},{3,2},{4,5},{5,4},{6,7},{7,6},{8,9},{9,8},{10,11... | collective-permute-start | bytes 491528 | tf_op jit(solution)/shard_map/ppermute | solution.py:514
  47.5 7.4 %collective-permute-start.11 = (bf16[128,640]{1,0:T(8,128)(2,1)S(1)}, bf16[128,640]{1,0:T(8,128)(2,1)S(1)}, u32[]{:S(2)}, u32[]{:S(2)}) collective-permute-start(bf16[128,640]{1,0:T(8,128)(2,1)S(1)} %get-tuple-element.50.refs_0_), channel_id=1, source_target_pairs={{0,2},{2,4},{4,6},{6,8},{8,10},{10,12},{12,14},{14,0},{1,3},{3,5},... | collective-permute-start | bytes 491528 | tf_op jit(solution)/shard_map/ppermute | solution.py:420
  47.6 7.4 %collective-permute-start.12 = (bf16[128,640]{1,0:T(8,128)(2,1)S(1)}, bf16[128,640]{1,0:T(8,128)(2,1)S(1)}, u32[]{:S(2)}, u32[]{:S(2)}) collective-permute-start(bf16[128,640]{1,0:T(8,128)(2,1)S(1)} %get-tuple-element.51.refs_1_), channel_id=1, source_target_pairs={{2,0},{4,2},{6,4},{8,6},{10,8},{12,10},{14,12},{0,14},{3,1},{5,3},... | collective-permute-start | bytes 491528 | tf_op jit(solution)/shard_map/ppermute | solution.py:421
  51.5 6.0 %collective-permute-start.16 = (bf16[160,640]{1,0:T(8,128)(2,1)S(1)}, bf16[160,640]{1,0:T(8,128)(2,1)S(1)}, u32[]{:S(2)}, u32[]{:S(2)}) collective-permute-start(bf16[160,640]{1,0:T(8,128)(2,1)S(1)} %shard_map.155), channel_id=1, source_target_pairs={{2,0},{4,2},{6,4},{8,6},{10,8},{12,10},{14,12},{0,14},{3,1},{5,3},... | collective-permute-start | bytes 614408 | tf_op jit(solution)/shard_map/ppermute | solution.py:421
  51.6 7.0 %collective-permute-start.15 = (bf16[160,640]{1,0:T(8,128)(2,1)S(1)}, bf16[160,640]{1,0:T(8,128)(2,1)S(1)}, u32[]{:S(2)}, u32[]{:S(2)}) collective-permute-start(bf16[160,640]{1,0:T(8,128)(2,1)S(1)} %shard_map.155), channel_id=1, source_target_pairs={{0,2},{2,4},{4,6},{6,8},{8,10},{10,12},{12,14},{14,0},{1,3},{3,5},... | collective-permute-start | bytes 614408 | tf_op jit(solution)/shard_map/ppermute | solution.py:420
  55.0 6.0 %collective-permute-start.14 = (bf16[144,640]{1,0:T(8,128)(2,1)S(1)}, bf16[144,640]{1,0:T(8,128)(2,1)S(1)}, u32[]{:S(2)}, u32[]{:S(2)}) collective-permute-start(bf16[144,640]{1,0:T(8,128)(2,1)S(1)} %get-tuple-element.55), channel_id=1, source_target_pairs={{2,0},{4,2},{6,4},{8,6},{10,8},{12,10},{14,12},{0,14},{3,1},{5,3},... | collective-permute-start | bytes 552968 | tf_op jit(solution)/shard_map/ppermute | solution.py:421
  57.4 6.8 %collective-permute-start.13 = (bf16[144,640]{1,0:T(8,128)(2,1)S(1)}, bf16[144,640]{1,0:T(8,128)(2,1)S(1)}, u32[]{:S(2)}, u32[]{:S(2)}) collective-permute-start(bf16[144,640]{1,0:T(8,128)(2,1)S(1)} %get-tuple-element.54.refs_4_), channel_id=1, source_target_pairs={{0,2},{2,4},{4,6},{6,8},{8,10},{10,12},{12,14},{14,0},{1,3},{3,5},... | collective-permute-start | bytes 552968 | tf_op jit(solution)/shard_map/ppermute | solution.py:420
  64.3 9.4 %collective-permute-start.19 = (bf16[144,640]{1,0:T(8,128)(2,1)S(1)}, bf16[144,640]{1,0:T(8,128)(2,1)S(1)}, u32[]{:S(2)}, u32[]{:S(2)}) collective-permute-start(bf16[144,640]{1,0:T(8,128)(2,1)S(1)} %get-tuple-element.61.refs_0_.refs_3_), channel_id=1, source_target_pairs={{0,2},{2,4},{4,6},{6,8},{8,10},{10,12},{12,14},{14,0},{1,3},{3,5},... | collective-permute-start | bytes 552968 | tf_op jit(solution)/shard_map/ppermute | solution.py:420
  64.4 5.7 %collective-permute-start.18 = (f32[8,128]{1,0:T(8,128)S(1)}, f32[8,128]{1,0:T(8,128)S(1)}, u32[]{:S(2)}, u32[]{:S(2)}) collective-permute-start(f32[8,128]{1,0:T(8,128)S(1)} %get-tuple-element.58), channel_id=1, source_target_pairs={{0,10},{2,12},{4,14},{6,0},{8,2},{10,4},{12,6},{14,8},{1,11},{3,13... | collective-permute-start | bytes 12296 | tf_op jit(solution)/shard_map/ppermute | solution.py:425
  65.7 6.6 %collective-permute-start.17 = (f32[8,128]{1,0:T(8,128)S(1)}, f32[8,128]{1,0:T(8,128)S(1)}, u32[]{:S(2)}, u32[]{:S(2)}) collective-permute-start(f32[8,128]{1,0:T(8,128)S(1)} %get-tuple-element.57.refs_0_.refs_2_), channel_id=1, source_target_pairs={{0,6},{2,8},{4,10},{6,12},{8,14},{10,0},{12,2},{14,4},{1,7},{3,9},... | collective-permute-start | bytes 12296 | tf_op jit(solution)/shard_map/ppermute | solution.py:425
  76.6 6.9 %collective-permute-start.20 = (bf16[128,640]{1,0:T(8,128)(2,1)S(1)}, bf16[128,640]{1,0:T(8,128)(2,1)S(1)}, u32[]{:S(2)}, u32[]{:S(2)}) collective-permute-start(bf16[128,640]{1,0:T(8,128)(2,1)S(1)} %shard_map.162.refs_3_), channel_id=1, source_target_pairs={{0,1},{1,0},{2,3},{3,2},{4,5},{5,4},{6,7},{7,6},{8,9},{9,8},{10,11... | collective-permute-start | bytes 491528 | tf_op jit(solution)/shard_map/ppermute | solution.py:514

commit v5 on v4

--- a/solution.py
+++ b/solution.py
@@ -17,7 +17,6 @@
 WIDTH = 640
 PAIRS = HEADS // 2
 PER_GROUP = WIDTH // GROUPS
-BYTES_PER_MICRO = 3.4e6
 BF = jnp.bfloat16
 F32 = jnp.float32
 
@@ -33,11 +32,11 @@
 
 
 def dot_exact(a, b):
-    high = a.astype(BF)
-    rest = a - high.astype(F32)
-    mid = rest.astype(BF)
-    low = (rest - mid.astype(F32)).astype(BF)
-    return dot(high, b) + (dot(mid, b) + dot(low, b))
+    rows = a.shape[0]
+    high = a.astype(BF).astype(F32)
+    mid = (a - high).astype(BF).astype(F32)
+    product = dot(jnp.concatenate([high, mid, (a - high) - mid], axis=0).astype(BF), b)
+    return product[:rows] + (product[rows : 2 * rows] + product[2 * rows :])
 
 
 HBM, FAR, VMEM, SCALARS = "hbm", "far", "vmem", "scalars"
@@ -59,7 +58,7 @@
         return self.target[index]
 
 
-def call(body, outs, *args, scratch=(), after=(), micros=0.1, limit=12):
+def call(body, outs, *args, scratch=(), after=(), outs_far=False, limit=12):
     args += tuple((one, "token") for one in after)
     count, far = len(args), [i for i, (_, where) in enumerate(args) if where == HBM]
     leaves, tree = jax.tree.flatten(outs)
@@ -94,12 +93,9 @@
         wrapped,
         out_shape=jax.tree.unflatten(tree, leaves),
         in_specs=[specs[where] for _, where in args],
-        out_specs=jax.tree.unflatten(tree, [specs[VMEM] for _ in leaves]),
+        out_specs=jax.tree.unflatten(tree, [specs[FAR if outs_far else VMEM] for _ in leaves]),
         scratch_shapes=list(scratch) + buffers,
         compiler_params=pltpu.CompilerParams(vmem_limit_bytes=limit * 2**20),
-        cost_estimate=pl.CostEstimate(
-            flops=0, bytes_accessed=int(micros * BYTES_PER_MICRO), transcendentals=0
-        ),
     )(*[put(arg, where) for arg, where in args])
 
 
@@ -202,6 +198,7 @@
 EXTRA = 16
 HEAD = COLS + EXTRA
 PAD = 32
+CHUNKS = 4
 
 
 def stats_rows(stats):
@@ -294,10 +291,10 @@
 def level(step, moments, x, rims, prep_ref, taps, q_w):
     _, mean, dev = moments
     scale = 1.0 / jnp.sqrt(dev * (1.0 / (PATCHES * COLS * PER_GROUP)) + 1e-05)
-    rows = jnp.concatenate([jnp.broadcast_to(mean, (8, 128)), jnp.broadcast_to(scale, (8, 128))], axis=0)
-    wide = dot_exact(rows, spread_matrix())
+    first_rows = lax.broadcasted_iota(jnp.int32, (8, 128), 0) < 4
+    wide = dot_exact(jnp.where(first_rows, mean, scale), spread_matrix())
     x = x[0]
-    normed = (x - wide[0:1]) * (wide[8:9] * prep_ref[GN_ROW : GN_ROW + 1])
+    normed = (x - wide[0:1]) * (wide[4:5] * prep_ref[GN_ROW : GN_ROW + 1])
     conv_in = normed * jax.nn.sigmoid(normed)
     hidden = x + (conv_row(conv_in, taps) + rims[...]) + prep_ref[step : step + 1]
     mid = jnp.mean(hidden, axis=1, keepdims=True)
@@ -360,10 +357,12 @@
         mixed_ref[:, lanes] = jnp.where(first_half, product[:COLS], product[COLS:]).astype(BF)
 
 
-def attend_body(early, late, query_ref, h_ref, *refs):
-    parts, rows = refs[:early], refs[early : early + 1 + late]
-    kv_ref, out_w_ref, eps_ref, late_ref, mixed_ref = refs[early + 1 + late :]
-    keys_of(rows, kv_ref, late_ref)
+def attend_body(early, late, ready, query_ref, h_ref, *refs):
+    parts, rows, done = refs[:early], refs[early : early + 1 + late], refs[early + 1 + late :][:ready]
+    kv_ref, out_w_ref, eps_ref, late_ref, mixed_ref = refs[early + 1 + late + ready :]
+    keys_of(rows, kv_ref, late_ref.at[: (1 + late) * COLS])
+    for ref in done:
+        late_ref[COLS:] = ref[...]
     attend(query_ref, (*parts, late_ref), mixed_ref)
     eps_ref[...] = (h_ref[...] + dot(mixed_ref[...], out_w_ref[...])).astype(eps_ref.dtype)
 
@@ -380,23 +379,37 @@
     )
 
 
-def guide(place_ref, own_ref, other_ref):
-    own, other = own_ref[...].astype(F32), other_ref[...].astype(F32)
-    first = place_ref[2] == 0.0
+def guide(first, own, other):
     uncond = jnp.where(first, own, other)
     cond = jnp.where(first, other, own)
     return uncond + 3.0 * (cond - uncond)
 
 
-def update_body(step, place_ref, prep_ref, x_ref, own_ref, other_ref, state_ref, *refs):
-    guided = guide(place_ref, own_ref, other_ref)
-    prep, row = prep_ref[...], STEPS + 2 * step
-    state = prep[row : row + 1] * x_ref[0] + prep[row + 1 : row + 2] * guided
+def update_body(place_ref, prep_ref, x_ref, own_ref, other_ref, state_ref, stats_ref):
+    own, other = own_ref[...].astype(F32), other_ref[...].astype(F32)
+    guided = guide(place_ref[2] == 0.0, own, other)
+    state = prep_ref[STEPS : STEPS + 1] * x_ref[0] + prep_ref[STEPS + 1 : STEPS + 2] * guided
     state_ref[0] = state
-    if step + 1 < STEPS:
-        refs[0][0:2] = local_stats(state)
-    else:
-        refs[0][0] = guided
+    stats_ref[0:2] = local_stats(state)
+
+
+def last_body(
+    place_ref, prep_ref, x_ref, own_ref, other_ref, state_ref, guided_ref, state_held, guided_held, sem
+):
+    row, step = STEPS + 2 * (STEPS - 1), COLS // CHUNKS
+    copies = []
+    for k in range(CHUNKS):
+        part = slice(k * step, (k + 1) * step)
+        own, other = own_ref[part].astype(F32), other_ref[part].astype(F32)
+        guided = guide(place_ref[2] == 0.0, own, other)
+        guided_held[part] = guided
+        state_held[part] = prep_ref[row : row + 1] * x_ref[0, part] + prep_ref[row + 1 : row + 2] * guided
+        for one, (held, target) in enumerate(((guided_held, guided_ref), (state_held, state_ref))):
+            copy = pltpu.make_async_copy(held.at[part], target.at[0, part], sem.at[2 * k + one])
+            copy.start()
+            copies.append(copy)
+    for copy in copies:
+        copy.wait()
 
 
 def shards(
@@ -497,20 +510,21 @@
         *[(one, VMEM) for one in [first, *ring1, *ring2, *ring3, opposite]],
     )
     ring1 = [up(attn_in), down(attn_in)]
-    attend_to = lambda weights, early, late: call(
-        functools.partial(attend_body, len(early), len(late)),
+    attend_to = lambda weights, early, late, ready: call(
+        functools.partial(attend_body, len(early), len(late), len(ready)),
         fast(full, BF),
         (query, VMEM),
         (hidden, VMEM),
         *early,
         (attn_in, VMEM),
         *[(one, VMEM) for one in late],
+        *[(one, VMEM) for one in ready],
         *[(w, VMEM) for w in weights],
-        scratch=(pltpu.VMEM(((1 + len(late)) * COLS, 2 * WIDTH), BF), pltpu.VMEM(full, BF)),
+        scratch=(pltpu.VMEM((2 * COLS, 2 * WIDTH), BF), pltpu.VMEM(full, BF)),
         limit=20,
     )
     early = [(one, VMEM) for one in (near_keys, mid_keys, far_keys)]
-    eps = attend_to((kv_w, out_w), early, ring4)
+    eps = attend_to((kv_w, out_w), early, ring4, [])
     exchange = lambda x: lax.ppermute(x, "cfg", [(0, 1), (1, 0)])
     other = exchange(eps)
     ring1 = later(ring1, (eps,))
@@ -519,7 +533,7 @@
     (conv_in,) = later([conv_in], (near_keys,))
     rims_in = [up(conv_in), down(conv_in)]
     state, stats = call(
-        functools.partial(update_body, 0),
+        update_body,
         (fast(whole, F32), stats_shape),
         (place, SCALARS),
         (prep, VMEM),
@@ -546,6 +560,7 @@
     ring3 = later(ring3, (three,))
     ring4 = [up(ring3[0])]
     far_keys = keys(ring3, (ring3[0],))
+    last_keys = keys(ring4, (far_keys,))
     attn_in, hidden, query = call(
         second_body,
         (fast(full, BF), fast(full, F32), fast(full, BF)),
@@ -557,18 +572,25 @@
         (prep, VMEM),
         (conv_w, VMEM),
         (q_w, VMEM),
+        after=(last_keys,),
     )
     early = [(one, VMEM) for one in (near_keys, mid_keys, far_keys)]
-    eps = attend_to((kv_w, out_w), early, ring4)
+    eps = attend_to((kv_w, out_w), early, [], [last_keys])
     other = exchange(eps)
     return call(
-        functools.partial(update_body, 1),
+        last_body,
         (shape(whole, F32), shape(whole, F32)),
         (place, SCALARS),
         (prep, VMEM),
         (state, VMEM),
         (eps, VMEM),
         (other, VMEM),
+        scratch=(
+            pltpu.VMEM(full, F32),
+            pltpu.VMEM(full, F32),
+            pltpu.SemaphoreType.DMA((2 * CHUNKS,)),
+        ),
+        outs_far=True,
     )
 
 

time: 86.1 us -> 85.5 us (level)
    ppermute x3, waiting for transfers between devices: 6.77 us -> 4.36 us  [shards(): lax.ppermute(x, 'patch', [(i, (i + far) % PATCHES) for i in range(PATCHES)])]
    ppermute x9, waiting for transfers between devices: 11.3 us -> 13.5 us  [shards(): up = lambda x: lax.ppermute(x, 'patch', upward)]
    pallas_call x19 -> x20, Pallas kernels: 24.7 us -> 24.2 us  [call(): pl.pallas_call(wrapped, out_shape=jax.tree.unflatten(tree, leaves), in_sp...]
  transfers between devices with their start and end apart: 21 -> 21, of which waited for: 10 -> 11; matrix products, arithmetic and copies ran while one was open for 0% -> 0% of each run, Pallas kernels for 22% -> 20%
where the time goes in v5:
time: 85.5 us; the launch traced here: 84.4 us
  starting transfers between devices  35.2 us (41%)
  Pallas kernels  24.2 us (28%)
  waiting for transfers between devices  23.9 us (28%)
  between operations  1.02 us (1%)
    pallas_call x20, Pallas kernels, call(): pl.pallas_call(wrapped, out_shape=jax.tree.unflatten(tree, leaves), in_sp...  24.2 us
    ppermute x7, starting transfers between devices, shards(): down = lambda x: lax.ppermute(x, 'patch', downward)  17.7 us
    ppermute x9, waiting for transfers between devices, shards(): up = lambda x: lax.ppermute(x, 'patch', upward)  13.5 us
    ppermute x3, starting transfers between devices, shards(): lax.ppermute(x, 'patch', [(i, (i + far) % PATCHES) for i in range(PATCHES)])  7.48 us
    ppermute x2, starting transfers between devices, shards(): exchange = lambda x: lax.ppermute(x, 'cfg', [(0, 1), (1, 0)])  5.3 us
    ppermute x2, waiting for transfers between devices, shards(): exchange = lambda x: lax.ppermute(x, 'cfg', [(0, 1), (1, 0)])  4.89 us
    ppermute x9, starting transfers between devices, shards(): up = lambda x: lax.ppermute(x, 'patch', upward)  4.74 us
    ppermute x3, waiting for transfers between devices, shards(): lax.ppermute(x, 'patch', [(i, (i + far) % PATCHES) for i in range(PATCHES)])  4.36 us
  transfers between devices with their start and end apart: 21, of which 11 were waited for; matrix products, arithmetic and copies ran while one was open for 0% of the time, Pallas kernels for 20%

profile of v5, /device:TPU:2, one launch (start us, length us, event | category | flops | bytes accessed | tf_op | source)
XLA Modules:
  0.0 84.4 jit_solution(15292041007241102949)
XLA Ops:
  0.6 0.1 add_convert_fusion.refs_3_.refs_0_
  0.7 1.6 %shard_map.140 = (bf16[272,640]{1,0:T(8,128)(2,1)S(1)}, f32[1,128,640]{2,1,0:T(8,128)S(1)}, f32[8,128]{1,0:T(8,128)S(1)}) custom-call(f32[1,128,640]{2,1,0:T(8,128)} %refs_0_.2, bf16[128,640]{1,0:T(8,128)(2,1)} %bitcast.6, bf16[128,640]{1,0:T(8,128)(2,1)} %bitcast.7, f32[3]{0:T(128)S(1)} %add_convert_fusion.refs_3_.refs_0_), custom_call_target="tpu_custom_call" | custom-call | tf_op jit(solution)/shard_map/pallas_call | solution.py:92
  2.4 5.9 %collective-permute-start.1 = (bf16[272,640]{1,0:T(8,128)(2,1)S(1)}, bf16[272,640]{1,0:T(8,128)(2,1)S(1)}, u32[]{:S(2)}, u32[]{:S(2)}) collective-permute-start(bf16[272,640]{1,0:T(8,128)(2,1)S(1)} %get-tuple-element.33.refs_10_.refs_5_), channel_id=1, source_target_pairs={{2,0},{4,2},{6,4},{8,6},{10,8},{12,10},{14,12},{0,14},{3,1},{5,3},... | collective-permute-start | bytes 1044488 | tf_op jit(solution)/shard_map/ppermute | solution.py:434
  8.3 3.4 %collective-permute-start.2 = (f32[8,128]{1,0:T(8,128)S(1)}, f32[8,128]{1,0:T(8,128)S(1)}, u32[]{:S(2)}, u32[]{:S(2)}) collective-permute-start(f32[8,128]{1,0:T(8,128)S(1)} %get-tuple-element.37), channel_id=1, source_target_pairs={{0,8},{2,10},{4,12},{6,14},{8,0},{10,2},{12,4},{14,6},{1,9},{3,11}... | collective-permute-start | bytes 12296 | tf_op jit(solution)/shard_map/ppermute | solution.py:438
  11.7 4.1 %shard_map.141 = (f32[8,640]{1,0:T(8,128)S(1)}, bf16[3,3,640,640]{3,2,1,0:T(8,128)(2,1)S(1)}, bf16[640,640]{1,0:T(8,128)(2,1)S(1)}, bf16[640,1280]{1,0:T(8,128)(2,1)S(1)}, bf16[640,640]{1,0:T(8,128)(2,1)S(1)}) custom-call(bf16[3,3,640,640]{3,2,1,0:T(8,128)(2,1)} %refs_0_.3, bf16[640,640]{1,0:T(8,128)(2,1)} %refs_1_.1, bf16[640,1280]{1,0:T(8,128)(2,1)} %refs_2_.1, ...), custom_call_target="tpu_custom_call" | custom-call | tf_op jit(solution)/shard_map/pallas_call | solution.py:92
  15.8 3.6 %collective-permute-done.2.refs_3_.refs_12_ = f32[8,128]{1,0:T(8,128)S(1)} collective-permute-done((f32[8,128]{1,0:T(8,128)S(1)}, f32[8,128]{1,0:T(8,128)S(1)}, u32[]{:S(2)}, u32[]{:S(2)}) %collective-permute-start.2) | collective-permute-done | bytes 4128 | tf_op jit(solution)/shard_map/ppermute | solution.py:438
  19.4 0.0 collective-permute-done.1.refs_1_.refs_2_.refs_7_
  19.4 0.0 collective-permute-done.refs_0_.refs_1_.refs_6_
  19.5 0.2 collective-permute-start.4
  19.7 1.9 %collective-permute-start.3 = (bf16[144,640]{1,0:T(8,128)(2,1)S(1)}, bf16[144,640]{1,0:T(8,128)(2,1)S(1)}, u32[]{:S(2)}, u32[]{:S(2)}) collective-permute-start(bf16[144,640]{1,0:T(8,128)(2,1)S(1)} %get-tuple-element.38.refs_4_), channel_id=1, source_target_pairs={{0,2},{2,4},{4,6},{6,8},{8,10},{10,12},{12,14},{14,0},{1,3},{3,5},... | collective-permute-start | bytes 552968 | tf_op jit(solution)/shard_map/ppermute | solution.py:433
  21.6 1.6 %shard_map.143.refs_3_.refs_1_ = f32[128,640]{1,0:T(8,128)S(1)} custom-call(f32[3]{0:T(128)S(1)} %add_convert_fusion.refs_3_.refs_0_, bf16[272,640]{1,0:T(8,128)(2,1)S(1)} %collective-permute-done.refs_0_.refs_1_.refs_6_, bf16[272,640]{1,0:T(8,128)(2,1)S(1)} %collective-permute-done.1.refs_1_.refs_2_.refs_7_, ...), custom_call_target="tpu_custom_call" | custom-call | tf_op jit(solution)/shard_map/pallas_call | solution.py:92
  23.2 0.7 shard_map.144.refs_2_
  23.9 1.2 %collective-permute-done.4.refs_1_ = bf16[144,640]{1,0:T(8,128)(2,1)S(1)} collective-permute-done((bf16[144,640]{1,0:T(8,128)(2,1)S(1)}, bf16[144,640]{1,0:T(8,128)(2,1)S(1)}, u32[]{:S(2)}, u32[]{:S(2)}) %collective-permute-start.4) | collective-permute-done | bytes 184352 | tf_op jit(solution)/shard_map/ppermute | solution.py:434
  25.1 1.4 %collective-permute-done.3.refs_0_ = bf16[144,640]{1,0:T(8,128)(2,1)S(1)} collective-permute-done((bf16[144,640]{1,0:T(8,128)(2,1)S(1)}, bf16[144,640]{1,0:T(8,128)(2,1)S(1)}, u32[]{:S(2)}, u32[]{:S(2)}) %collective-permute-start.3) | collective-permute-done | bytes 184352 | tf_op jit(solution)/shard_map/ppermute | solution.py:433
  26.4 0.8 collective-permute-start.5
  27.2 2.5 %collective-permute-start.6 = (bf16[144,640]{1,0:T(8,128)(2,1)S(1)}, bf16[144,640]{1,0:T(8,128)(2,1)S(1)}, u32[]{:S(2)}, u32[]{:S(2)}) collective-permute-start(bf16[144,640]{1,0:T(8,128)(2,1)S(1)} %get-tuple-element.43.refs_1_.refs_9_), channel_id=1, source_target_pairs={{2,0},{4,2},{6,4},{8,6},{10,8},{12,10},{14,12},{0,14},{3,1},{5,3},... | collective-permute-start | bytes 552968 | tf_op jit(solution)/shard_map/ppermute | solution.py:434
  29.7 0.7 shard_map.146.refs_2_.refs_3_
  30.4 2.8 %collective-permute-done.5.refs_0_ = bf16[144,640]{1,0:T(8,128)(2,1)S(1)} collective-permute-done((bf16[144,640]{1,0:T(8,128)(2,1)S(1)}, bf16[144,640]{1,0:T(8,128)(2,1)S(1)}, u32[]{:S(2)}, u32[]{:S(2)}) %collective-permute-start.5) | collective-permute-done | bytes 184352 | tf_op jit(solution)/shard_map/ppermute | solution.py:433
  33.2 1.3 %shard_map.148 = (bf16[160,640]{1,0:T(8,128)(2,1)S(1)}, f32[128,640]{1,0:T(8,128)S(1)}, bf16[128,640]{1,0:T(8,128)(2,1)S(1)}, bf16[128,640]{1,0:T(8,128)(2,1)S(1)}) custom-call(f32[1,128,640]{2,1,0:T(8,128)S(1)} %get-tuple-element.35.refs_0_.refs_2_, f32[128,640]{1,0:T(8,128)S(1)} %shard_map.143.refs_3_.refs_1_, ...), custom_call_target="tpu_custom_call" | custom-call | tf_op jit(solution)/shard_map/pallas_call | solution.py:92
  34.5 3.3 %collective-permute-start.10 = (bf16[128,640]{1,0:T(8,128)(2,1)S(1)}, bf16[128,640]{1,0:T(8,128)(2,1)S(1)}, u32[]{:S(2)}, u32[]{:S(2)}) collective-permute-start(bf16[128,640]{1,0:T(8,128)(2,1)S(1)} %get-tuple-element.48.refs_5_), channel_id=1, source_target_pairs={{2,0},{4,2},{6,4},{8,6},{10,8},{12,10},{14,12},{0,14},{3,1},{5,3},... | collective-permute-start | bytes 491528 | tf_op jit(solution)/shard_map/ppermute | solution.py:434
  37.8 0.0 collective-permute-start.9
  37.8 0.7 shard_map.149.refs_4_
  38.5 2.6 %collective-permute-done.7.refs_6_ = bf16[144,640]{1,0:T(8,128)(2,1)S(1)} collective-permute-done((bf16[144,640]{1,0:T(8,128)(2,1)S(1)}, bf16[144,640]{1,0:T(8,128)(2,1)S(1)}, u32[]{:S(2)}, u32[]{:S(2)}) %collective-permute-start.7) | collective-permute-done | bytes 184352 | tf_op jit(solution)/shard_map/ppermute | solution.py:433
  41.2 2.8 %shard_map.150.refs_2_.refs_3_ = bf16[128,640]{1,0:T(8,128)(2,1)S(1)} custom-call(bf16[128,640]{1,0:T(8,128)(2,1)S(1)} %get-tuple-element.46.refs_0_, f32[128,640]{1,0:T(8,128)S(1)} %get-tuple-element.47.refs_1_, bf16[256,1280]{1,0:T(8,128)(2,1)S(1)} %shard_map.144.refs_2_, bf16[256,1280]{1,0:T(8,128)(2,1)S(1)} %shard_map.146.refs_2_.refs_3_, ...), custom_call_target="tpu_custom_call" | custom-call | tf_op jit(solution)/shard_map/pallas_call | solution.py:92
  44.0 3.3 %collective-permute-start.8 = (bf16[128,640]{1,0:T(8,128)(2,1)S(1)}, bf16[128,640]{1,0:T(8,128)(2,1)S(1)}, u32[]{:S(2)}, u32[]{:S(2)}) collective-permute-start(bf16[128,640]{1,0:T(8,128)(2,1)S(1)} %shard_map.150.refs_2_.refs_3_), channel_id=1, source_target_pairs={{0,1},{1,0},{2,3},{3,2},{4,5},{5,4},{6,7},{7,6},{8,9},{9,8},{10,11... | collective-permute-start | bytes 491528 | tf_op jit(solution)/shard_map/ppermute | solution.py:528
  47.3 3.2 %collective-permute-start.12 = (bf16[128,640]{1,0:T(8,128)(2,1)S(1)}, bf16[128,640]{1,0:T(8,128)(2,1)S(1)}, u32[]{:S(2)}, u32[]{:S(2)}) collective-permute-start(bf16[128,640]{1,0:T(8,128)(2,1)S(1)} %get-tuple-element.51.refs_1_), channel_id=1, source_target_pairs={{2,0},{4,2},{6,4},{8,6},{10,8},{12,10},{14,12},{0,14},{3,1},{5,3},... | collective-permute-start | bytes 491528 | tf_op jit(solution)/shard_map/ppermute | solution.py:434
  50.5 0.7 shard_map.152.refs_5_.refs_1_.refs_2_
  51.2 0.1 collective-permute-start.16
  51.3 2.0 %collective-permute-start.15 = (bf16[160,640]{1,0:T(8,128)(2,1)S(1)}, bf16[160,640]{1,0:T(8,128)(2,1)S(1)}, u32[]{:S(2)}, u32[]{:S(2)}) collective-permute-start(bf16[160,640]{1,0:T(8,128)(2,1)S(1)} %shard_map.155), channel_id=1, source_target_pairs={{0,2},{2,4},{4,6},{6,8},{8,10},{10,12},{12,14},{14,0},{1,3},{3,5},... | collective-permute-start | bytes 614408 | tf_op jit(solution)/shard_map/ppermute | solution.py:433
  53.3 1.2 %shard_map.153 = (f32[1,128,640]{2,1,0:T(8,128)S(1)}, f32[8,128]{1,0:T(8,128)S(1)}) custom-call(f32[3]{0:T(128)S(1)} %add_convert_fusion.refs_3_.refs_0_, f32[8,640]{1,0:T(8,128)S(1)} %get-tuple-element.34.refs_2_.refs_1_.refs_5_, f32[1,128,640]{2,1,0:T(8,128)S(1)} %get-tuple-element.35.refs_0_.refs_2_, bf16[128,640]{1,0:T(8,128)(2,1)S(1)} %shard_map.150.refs_2_.refs_3_, ...), custom_call_target="tpu_custom_call" | custom-call | tf_op jit(solution)/shard_map/pallas_call | solution.py:92
  54.5 0.2 collective-permute-done.11.refs_1_.refs_0_
  54.7 2.4 %collective-permute-start.14 = (bf16[144,640]{1,0:T(8,128)(2,1)S(1)}, bf16[144,640]{1,0:T(8,128)(2,1)S(1)}, u32[]{:S(2)}, u32[]{:S(2)}) collective-permute-start(bf16[144,640]{1,0:T(8,128)(2,1)S(1)} %get-tuple-element.55), channel_id=1, source_target_pairs={{2,0},{4,2},{6,4},{8,6},{10,8},{12,10},{14,12},{0,14},{3,1},{5,3},... | collective-permute-start | bytes 552968 | tf_op jit(solution)/shard_map/ppermute | solution.py:434
  57.2 1.2 %collective-permute-done.15.refs_1_ = bf16[160,640]{1,0:T(8,128)(2,1)S(1)} collective-permute-done((bf16[160,640]{1,0:T(8,128)(2,1)S(1)}, bf16[160,640]{1,0:T(8,128)(2,1)S(1)}, u32[]{:S(2)}, u32[]{:S(2)}) %collective-permute-start.15) | collective-permute-done | bytes 204832 | tf_op jit(solution)/shard_map/ppermute | solution.py:433
  58.3 1.6 %shard_map.156.refs_3_.refs_4_ = f32[128,640]{1,0:T(8,128)S(1)} custom-call(f32[3]{0:T(128)S(1)} %add_convert_fusion.refs_3_.refs_0_, bf16[160,640]{1,0:T(8,128)(2,1)S(1)} %collective-permute-done.15.refs_1_, bf16[160,640]{1,0:T(8,128)(2,1)S(1)} %collective-permute-done.16.refs_2_, bf16[3,3,640,640]{3,2,1,0:T(8,128)(2,1)S(1)} %get-tuple-element.36.refs_3_.refs_6_, ...), custom_call_target="tpu_custom_call" | custom-call | tf_op jit(solution)/shard_map/pallas_call | solution.py:92
  60.0 0.7 shard_map.157.refs_3_
  60.7 3.3 %collective-permute-done.13.refs_1_.refs_0_ = bf16[144,640]{1,0:T(8,128)(2,1)S(1)} collective-permute-done((bf16[144,640]{1,0:T(8,128)(2,1)S(1)}, bf16[144,640]{1,0:T(8,128)(2,1)S(1)}, u32[]{:S(2)}, u32[]{:S(2)}) %collective-permute-start.13) | collective-permute-done | bytes 184352 | tf_op jit(solution)/shard_map/ppermute | solution.py:433
  64.0 0.1 collective-permute-start.19
  64.1 1.3 %collective-permute-start.18 = (f32[8,128]{1,0:T(8,128)S(1)}, f32[8,128]{1,0:T(8,128)S(1)}, u32[]{:S(2)}, u32[]{:S(2)}) collective-permute-start(f32[8,128]{1,0:T(8,128)S(1)} %get-tuple-element.58), channel_id=1, source_target_pairs={{0,10},{2,12},{4,14},{6,0},{8,2},{10,4},{12,6},{14,8},{1,11},{3,13... | collective-permute-start | bytes 12296 | tf_op jit(solution)/shard_map/ppermute | solution.py:438
  65.4 2.8 %collective-permute-start.17 = (f32[8,128]{1,0:T(8,128)S(1)}, f32[8,128]{1,0:T(8,128)S(1)}, u32[]{:S(2)}, u32[]{:S(2)}) collective-permute-start(f32[8,128]{1,0:T(8,128)S(1)} %get-tuple-element.57.refs_2_.refs_0_), channel_id=1, source_target_pairs={{0,6},{2,8},{4,10},{6,12},{8,14},{10,0},{12,2},{14,4},{1,7},{3,9},... | collective-permute-start | bytes 12296 | tf_op jit(solution)/shard_map/ppermute | solution.py:438
  68.2 0.7 shard_map.160.refs_2_.refs_4_
  68.9 1.9 %collective-permute-done.19.refs_0_ = bf16[144,640]{1,0:T(8,128)(2,1)S(1)} collective-permute-done((bf16[144,640]{1,0:T(8,128)(2,1)S(1)}, bf16[144,640]{1,0:T(8,128)(2,1)S(1)}, u32[]{:S(2)}, u32[]{:S(2)}) %collective-permute-start.19) | collective-permute-done | bytes 184352 | tf_op jit(solution)/shard_map/ppermute | solution.py:433
  70.8 0.4 shard_map.161.refs_8_.refs_6_
  71.3 0.7 collective-permute-done.17.refs_1_
  72.0 1.3 %shard_map.162 = (bf16[128,640]{1,0:T(8,128)(2,1)S(1)}, f32[128,640]{1,0:T(8,128)S(1)}, bf16[128,640]{1,0:T(8,128)(2,1)S(1)}) custom-call(f32[8,128]{1,0:T(8,128)S(1)} %get-tuple-element.57.refs_2_.refs_0_, f32[8,128]{1,0:T(8,128)S(1)} %collective-permute-done.17.refs_1_, f32[8,128]{1,0:T(8,128)S(1)} %collective-permute-done.18.refs_2_, ...), custom_call_target="tpu_custom_call" | custom-call | tf_op jit(solution)/shard_map/pallas_call | solution.py:92
  73.3 2.6 %shard_map.163.refs_3_ = bf16[128,640]{1,0:T(8,128)(2,1)S(1)} custom-call(bf16[128,640]{1,0:T(8,128)(2,1)S(1)} %get-tuple-element.61.refs_0_, f32[128,640]{1,0:T(8,128)S(1)} %get-tuple-element.62.refs_1_, bf16[256,1280]{1,0:T(8,128)(2,1)S(1)} %shard_map.152.refs_5_.refs_1_.refs_2_, bf16[256,1280]{1,0:T(8,128)(2,1)S(1)} %shard_map.157.refs_3_, ...), custom_call_target="tpu_custom_call" | custom-call | tf_op jit(solution)/shard_map/pallas_call | solution.py:92
  75.9 2.0 %collective-permute-start.20 = (bf16[128,640]{1,0:T(8,128)(2,1)S(1)}, bf16[128,640]{1,0:T(8,128)(2,1)S(1)}, u32[]{:S(2)}, u32[]{:S(2)}) collective-permute-start(bf16[128,640]{1,0:T(8,128)(2,1)S(1)} %shard_map.163.refs_3_), channel_id=1, source_target_pairs={{0,1},{1,0},{2,3},{3,2},{4,5},{5,4},{6,7},{7,6},{8,9},{9,8},{10,11... | collective-permute-start | bytes 491528 | tf_op jit(solution)/shard_map/ppermute | solution.py:528
  77.9 4.9 %collective-permute-done.20.refs_4_ = bf16[128,640]{1,0:T(8,128)(2,1)S(1)} collective-permute-done((bf16[128,640]{1,0:T(8,128)(2,1)S(1)}, bf16[128,640]{1,0:T(8,128)(2,1)S(1)}, u32[]{:S(2)}, u32[]{:S(2)}) %collective-permute-start.20) | collective-permute-done | bytes 163872 | tf_op jit(solution)/shard_map/ppermute | solution.py:528
  82.8 1.5 %shard_map.164 = (f32[1,128,640]{2,1,0:T(8,128)}, f32[1,128,640]{2,1,0:T(8,128)}) custom-call(f32[3]{0:T(128)S(1)} %add_convert_fusion.refs_3_.refs_0_, f32[8,640]{1,0:T(8,128)S(1)} %get-tuple-element.34.refs_2_.refs_1_.refs_5_, f32[1,128,640]{2,1,0:T(8,128)S(1)} %get-tuple-element.52.refs_3_.refs_2_, bf16[128,640]{1,0:T(8,128)(2,1)S(1)} %shard_map.163.refs_3_, ...), custom_call_target="tpu_custom_call" | custom-call | tf_op jit(solution)/shard_map/pallas_call | solution.py:92
  (20 shorter events, 0.1 us)
Async XLA Ops:
  2.4 17.1 %collective-permute-start.1 = (bf16[272,640]{1,0:T(8,128)(2,1)S(1)}, bf16[272,640]{1,0:T(8,128)(2,1)S(1)}, u32[]{:S(2)}, u32[]{:S(2)}) collective-permute-start(bf16[272,640]{1,0:T(8,128)(2,1)S(1)} %get-tuple-element.33.refs_10_.refs_5_), channel_id=1, source_target_pairs={{2,0},{4,2},{6,4},{8,6},{10,8},{12,10},{14,12},{0,14},{3,1},{5,3},... | collective-permute-start | bytes 1044488 | tf_op jit(solution)/shard_map/ppermute | solution.py:434
  8.3 11.1 %collective-permute-start = (bf16[272,640]{1,0:T(8,128)(2,1)S(1)}, bf16[272,640]{1,0:T(8,128)(2,1)S(1)}, u32[]{:S(2)}, u32[]{:S(2)}) collective-permute-start(bf16[272,640]{1,0:T(8,128)(2,1)S(1)} %get-tuple-element.33.refs_10_.refs_5_), channel_id=1, source_target_pairs={{0,2},{2,4},{4,6},{6,8},{8,10},{10,12},{12,14},{14,0},{1,3},{3,5},... | collective-permute-start | bytes 1044488 | tf_op jit(solution)/shard_map/ppermute | solution.py:433
  8.3 11.1 %collective-permute-start.2 = (f32[8,128]{1,0:T(8,128)S(1)}, f32[8,128]{1,0:T(8,128)S(1)}, u32[]{:S(2)}, u32[]{:S(2)}) collective-permute-start(f32[8,128]{1,0:T(8,128)S(1)} %get-tuple-element.37), channel_id=1, source_target_pairs={{0,8},{2,10},{4,12},{6,14},{8,0},{10,2},{12,4},{14,6},{1,9},{3,11}... | collective-permute-start | bytes 12296 | tf_op jit(solution)/shard_map/ppermute | solution.py:438
  19.5 5.6 %collective-permute-start.4 = (bf16[144,640]{1,0:T(8,128)(2,1)S(1)}, bf16[144,640]{1,0:T(8,128)(2,1)S(1)}, u32[]{:S(2)}, u32[]{:S(2)}) collective-permute-start(bf16[144,640]{1,0:T(8,128)(2,1)S(1)} %get-tuple-element.40), channel_id=1, source_target_pairs={{2,0},{4,2},{6,4},{8,6},{10,8},{12,10},{14,12},{0,14},{3,1},{5,3},... | collective-permute-start | bytes 552968 | tf_op jit(solution)/shard_map/ppermute | solution.py:434
  19.7 6.7 %collective-permute-start.3 = (bf16[144,640]{1,0:T(8,128)(2,1)S(1)}, bf16[144,640]{1,0:T(8,128)(2,1)S(1)}, u32[]{:S(2)}, u32[]{:S(2)}) collective-permute-start(bf16[144,640]{1,0:T(8,128)(2,1)S(1)} %get-tuple-element.38.refs_4_), channel_id=1, source_target_pairs={{0,2},{2,4},{4,6},{6,8},{8,10},{10,12},{12,14},{14,0},{1,3},{3,5},... | collective-permute-start | bytes 552968 | tf_op jit(solution)/shard_map/ppermute | solution.py:433
  26.4 6.7 %collective-permute-start.5 = (bf16[144,640]{1,0:T(8,128)(2,1)S(1)}, bf16[144,640]{1,0:T(8,128)(2,1)S(1)}, u32[]{:S(2)}, u32[]{:S(2)}) collective-permute-start(bf16[144,640]{1,0:T(8,128)(2,1)S(1)} %get-tuple-element.42.refs_0_.refs_3_.refs_8_), channel_id=1, source_target_pairs={{0,2},{2,4},{4,6},{6,8},{8,10},{10,12},{12,14},{14,0},{1,3},{3,5},... | collective-permute-start | bytes 552968 | tf_op jit(solution)/shard_map/ppermute | solution.py:433
  27.2 6.0 %collective-permute-start.6 = (bf16[144,640]{1,0:T(8,128)(2,1)S(1)}, bf16[144,640]{1,0:T(8,128)(2,1)S(1)}, u32[]{:S(2)}, u32[]{:S(2)}) collective-permute-start(bf16[144,640]{1,0:T(8,128)(2,1)S(1)} %get-tuple-element.43.refs_1_.refs_9_), channel_id=1, source_target_pairs={{2,0},{4,2},{6,4},{8,6},{10,8},{12,10},{14,12},{0,14},{3,1},{5,3},... | collective-permute-start | bytes 552968 | tf_op jit(solution)/shard_map/ppermute | solution.py:434
  33.2 8.0 %collective-permute-start.7 = (bf16[144,640]{1,0:T(8,128)(2,1)S(1)}, bf16[144,640]{1,0:T(8,128)(2,1)S(1)}, u32[]{:S(2)}, u32[]{:S(2)}) collective-permute-start(bf16[144,640]{1,0:T(8,128)(2,1)S(1)} %get-tuple-element.44.refs_10_.refs_0_.refs_3_), channel_id=1, source_target_pairs={{0,2},{2,4},{4,6},{6,8},{8,10},{10,12},{12,14},{14,0},{1,3},{3,5},... | collective-permute-start | bytes 552968 | tf_op jit(solution)/shard_map/ppermute | solution.py:433
  34.5 12.8 %collective-permute-start.10 = (bf16[128,640]{1,0:T(8,128)(2,1)S(1)}, bf16[128,640]{1,0:T(8,128)(2,1)S(1)}, u32[]{:S(2)}, u32[]{:S(2)}) collective-permute-start(bf16[128,640]{1,0:T(8,128)(2,1)S(1)} %get-tuple-element.48.refs_5_), channel_id=1, source_target_pairs={{2,0},{4,2},{6,4},{8,6},{10,8},{12,10},{14,12},{0,14},{3,1},{5,3},... | collective-permute-start | bytes 491528 | tf_op jit(solution)/shard_map/ppermute | solution.py:434
  37.8 9.5 %collective-permute-start.9 = (bf16[128,640]{1,0:T(8,128)(2,1)S(1)}, bf16[128,640]{1,0:T(8,128)(2,1)S(1)}, u32[]{:S(2)}, u32[]{:S(2)}) collective-permute-start(bf16[128,640]{1,0:T(8,128)(2,1)S(1)} %get-tuple-element.48.refs_5_), channel_id=1, source_target_pairs={{0,2},{2,4},{4,6},{6,8},{8,10},{10,12},{12,14},{14,0},{1,3},{3,5},... | collective-permute-start | bytes 491528 | tf_op jit(solution)/shard_map/ppermute | solution.py:433
  44.0 9.3 %collective-permute-start.8 = (bf16[128,640]{1,0:T(8,128)(2,1)S(1)}, bf16[128,640]{1,0:T(8,128)(2,1)S(1)}, u32[]{:S(2)}, u32[]{:S(2)}) collective-permute-start(bf16[128,640]{1,0:T(8,128)(2,1)S(1)} %shard_map.150.refs_2_.refs_3_), channel_id=1, source_target_pairs={{0,1},{1,0},{2,3},{3,2},{4,5},{5,4},{6,7},{7,6},{8,9},{9,8},{10,11... | collective-permute-start | bytes 491528 | tf_op jit(solution)/shard_map/ppermute | solution.py:528
  47.3 7.4 %collective-permute-start.11 = (bf16[128,640]{1,0:T(8,128)(2,1)S(1)}, bf16[128,640]{1,0:T(8,128)(2,1)S(1)}, u32[]{:S(2)}, u32[]{:S(2)}) collective-permute-start(bf16[128,640]{1,0:T(8,128)(2,1)S(1)} %get-tuple-element.50.refs_0_), channel_id=1, source_target_pairs={{0,2},{2,4},{4,6},{6,8},{8,10},{10,12},{12,14},{14,0},{1,3},{3,5},... | collective-permute-start | bytes 491528 | tf_op jit(solution)/shard_map/ppermute | solution.py:433
  47.3 7.4 %collective-permute-start.12 = (bf16[128,640]{1,0:T(8,128)(2,1)S(1)}, bf16[128,640]{1,0:T(8,128)(2,1)S(1)}, u32[]{:S(2)}, u32[]{:S(2)}) collective-permute-start(bf16[128,640]{1,0:T(8,128)(2,1)S(1)} %get-tuple-element.51.refs_1_), channel_id=1, source_target_pairs={{2,0},{4,2},{6,4},{8,6},{10,8},{12,10},{14,12},{0,14},{3,1},{5,3},... | collective-permute-start | bytes 491528 | tf_op jit(solution)/shard_map/ppermute | solution.py:434
  51.2 5.9 %collective-permute-start.16 = (bf16[160,640]{1,0:T(8,128)(2,1)S(1)}, bf16[160,640]{1,0:T(8,128)(2,1)S(1)}, u32[]{:S(2)}, u32[]{:S(2)}) collective-permute-start(bf16[160,640]{1,0:T(8,128)(2,1)S(1)} %shard_map.155), channel_id=1, source_target_pairs={{2,0},{4,2},{6,4},{8,6},{10,8},{12,10},{14,12},{0,14},{3,1},{5,3},... | collective-permute-start | bytes 614408 | tf_op jit(solution)/shard_map/ppermute | solution.py:434
  51.3 7.0 %collective-permute-start.15 = (bf16[160,640]{1,0:T(8,128)(2,1)S(1)}, bf16[160,640]{1,0:T(8,128)(2,1)S(1)}, u32[]{:S(2)}, u32[]{:S(2)}) collective-permute-start(bf16[160,640]{1,0:T(8,128)(2,1)S(1)} %shard_map.155), channel_id=1, source_target_pairs={{0,2},{2,4},{4,6},{6,8},{8,10},{10,12},{12,14},{14,0},{1,3},{3,5},... | collective-permute-start | bytes 614408 | tf_op jit(solution)/shard_map/ppermute | solution.py:433
  54.7 5.9 %collective-permute-start.14 = (bf16[144,640]{1,0:T(8,128)(2,1)S(1)}, bf16[144,640]{1,0:T(8,128)(2,1)S(1)}, u32[]{:S(2)}, u32[]{:S(2)}) collective-permute-start(bf16[144,640]{1,0:T(8,128)(2,1)S(1)} %get-tuple-element.55), channel_id=1, source_target_pairs={{2,0},{4,2},{6,4},{8,6},{10,8},{12,10},{14,12},{0,14},{3,1},{5,3},... | collective-permute-start | bytes 552968 | tf_op jit(solution)/shard_map/ppermute | solution.py:434
  57.2 6.8 %collective-permute-start.13 = (bf16[144,640]{1,0:T(8,128)(2,1)S(1)}, bf16[144,640]{1,0:T(8,128)(2,1)S(1)}, u32[]{:S(2)}, u32[]{:S(2)}) collective-permute-start(bf16[144,640]{1,0:T(8,128)(2,1)S(1)} %get-tuple-element.54.refs_4_), channel_id=1, source_target_pairs={{0,2},{2,4},{4,6},{6,8},{8,10},{10,12},{12,14},{14,0},{1,3},{3,5},... | collective-permute-start | bytes 552968 | tf_op jit(solution)/shard_map/ppermute | solution.py:433
  64.0 6.8 %collective-permute-start.19 = (bf16[144,640]{1,0:T(8,128)(2,1)S(1)}, bf16[144,640]{1,0:T(8,128)(2,1)S(1)}, u32[]{:S(2)}, u32[]{:S(2)}) collective-permute-start(bf16[144,640]{1,0:T(8,128)(2,1)S(1)} %get-tuple-element.59.refs_0_.refs_3_), channel_id=1, source_target_pairs={{0,2},{2,4},{4,6},{6,8},{8,10},{10,12},{12,14},{14,0},{1,3},{3,5},... | collective-permute-start | bytes 552968 | tf_op jit(solution)/shard_map/ppermute | solution.py:433
  64.1 7.2 %collective-permute-start.18 = (f32[8,128]{1,0:T(8,128)S(1)}, f32[8,128]{1,0:T(8,128)S(1)}, u32[]{:S(2)}, u32[]{:S(2)}) collective-permute-start(f32[8,128]{1,0:T(8,128)S(1)} %get-tuple-element.58), channel_id=1, source_target_pairs={{0,10},{2,12},{4,14},{6,0},{8,2},{10,4},{12,6},{14,8},{1,11},{3,13... | collective-permute-start | bytes 12296 | tf_op jit(solution)/shard_map/ppermute | solution.py:438
  65.4 6.6 %collective-permute-start.17 = (f32[8,128]{1,0:T(8,128)S(1)}, f32[8,128]{1,0:T(8,128)S(1)}, u32[]{:S(2)}, u32[]{:S(2)}) collective-permute-start(f32[8,128]{1,0:T(8,128)S(1)} %get-tuple-element.57.refs_2_.refs_0_), channel_id=1, source_target_pairs={{0,6},{2,8},{4,10},{6,12},{8,14},{10,0},{12,2},{14,4},{1,7},{3,9},... | collective-permute-start | bytes 12296 | tf_op jit(solution)/shard_map/ppermute | solution.py:438
  75.9 6.9 %collective-permute-start.20 = (bf16[128,640]{1,0:T(8,128)(2,1)S(1)}, bf16[128,640]{1,0:T(8,128)(2,1)S(1)}, u32[]{:S(2)}, u32[]{:S(2)}) collective-permute-start(bf16[128,640]{1,0:T(8,128)(2,1)S(1)} %shard_map.163.refs_3_), channel_id=1, source_target_pairs={{0,1},{1,0},{2,3},{3,2},{4,5},{5,4},{6,7},{7,6},{8,9},{9,8},{10,11... | collective-permute-start | bytes 491528 | tf_op jit(solution)/shard_map/ppermute | solution.py:528

commit v6 on v5

--- a/solution.py
+++ b/solution.py
@@ -197,7 +197,7 @@
 GN_ROW, LN_ROW = 3 * STEPS, 3 * STEPS + 1
 EXTRA = 16
 HEAD = COLS + EXTRA
-PAD = 32
+PAD = 16
 CHUNKS = 4
 
 

time: 85.5 us -> 85.6 us (level)
  no operation moved by 1% of the time
where the time goes in v6:
time: 85.6 us; the launch traced here: 84.2 us
  starting transfers between devices  35.4 us (41%)
  Pallas kernels  24.2 us (28%)
  waiting for transfers between devices  23.5 us (27%)
  between operations  1.02 us (1%)
    pallas_call x20, Pallas kernels, call(): pl.pallas_call(wrapped, out_shape=jax.tree.unflatten(tree, leaves), in_sp...  24.2 us
    ppermute x7, starting transfers between devices, shards(): down = lambda x: lax.ppermute(x, 'patch', downward)  17.7 us
    ppermute x9, waiting for transfers between devices, shards(): up = lambda x: lax.ppermute(x, 'patch', upward)  13.4 us
    ppermute x3, starting transfers between devices, shards(): lax.ppermute(x, 'patch', [(i, (i + far) % PATCHES) for i in range(PATCHES)])  7.48 us
    ppermute x2, starting transfers between devices, shards(): exchange = lambda x: lax.ppermute(x, 'cfg', [(0, 1), (1, 0)])  5.47 us
    ppermute x9, starting transfers between devices, shards(): up = lambda x: lax.ppermute(x, 'patch', upward)  4.74 us
    ppermute x2, waiting for transfers between devices, shards(): exchange = lambda x: lax.ppermute(x, 'cfg', [(0, 1), (1, 0)])  4.69 us
    ppermute x3, waiting for transfers between devices, shards(): lax.ppermute(x, 'patch', [(i, (i + far) % PATCHES) for i in range(PATCHES)])  4.18 us
  transfers between devices with their start and end apart: 21, of which 11 were waited for; matrix products, arithmetic and copies ran while one was open for 0% of the time, Pallas kernels for 20%

profile of v6, /device:TPU:2, one launch (start us, length us, event | category | flops | bytes accessed | tf_op | source)
XLA Modules:
  0.0 84.2 jit_solution(8729856576640111408)
XLA Ops:
  0.6 0.1 add_convert_fusion.refs_3_.refs_0_
  0.7 1.6 %shard_map.140 = (bf16[272,640]{1,0:T(8,128)(2,1)S(1)}, f32[1,128,640]{2,1,0:T(8,128)S(1)}, f32[8,128]{1,0:T(8,128)S(1)}) custom-call(f32[1,128,640]{2,1,0:T(8,128)} %refs_0_.2, bf16[128,640]{1,0:T(8,128)(2,1)} %bitcast.6, bf16[128,640]{1,0:T(8,128)(2,1)} %bitcast.7, f32[3]{0:T(128)S(1)} %add_convert_fusion.refs_3_.refs_0_), custom_call_target="tpu_custom_call" | custom-call | tf_op jit(solution)/shard_map/pallas_call | solution.py:92
  2.4 5.9 %collective-permute-start.1 = (bf16[272,640]{1,0:T(8,128)(2,1)S(1)}, bf16[272,640]{1,0:T(8,128)(2,1)S(1)}, u32[]{:S(2)}, u32[]{:S(2)}) collective-permute-start(bf16[272,640]{1,0:T(8,128)(2,1)S(1)} %get-tuple-element.33.refs_10_.refs_5_), channel_id=1, source_target_pairs={{2,0},{4,2},{6,4},{8,6},{10,8},{12,10},{14,12},{0,14},{3,1},{5,3},... | collective-permute-start | bytes 1044488 | tf_op jit(solution)/shard_map/ppermute | solution.py:434
  8.3 3.4 %collective-permute-start.2 = (f32[8,128]{1,0:T(8,128)S(1)}, f32[8,128]{1,0:T(8,128)S(1)}, u32[]{:S(2)}, u32[]{:S(2)}) collective-permute-start(f32[8,128]{1,0:T(8,128)S(1)} %get-tuple-element.37), channel_id=1, source_target_pairs={{0,8},{2,10},{4,12},{6,14},{8,0},{10,2},{12,4},{14,6},{1,9},{3,11}... | collective-permute-start | bytes 12296 | tf_op jit(solution)/shard_map/ppermute | solution.py:438
  11.7 4.1 %shard_map.141 = (f32[8,640]{1,0:T(8,128)S(1)}, bf16[3,3,640,640]{3,2,1,0:T(8,128)(2,1)S(1)}, bf16[640,640]{1,0:T(8,128)(2,1)S(1)}, bf16[640,1280]{1,0:T(8,128)(2,1)S(1)}, bf16[640,640]{1,0:T(8,128)(2,1)S(1)}) custom-call(bf16[3,3,640,640]{3,2,1,0:T(8,128)(2,1)} %refs_0_.3, bf16[640,640]{1,0:T(8,128)(2,1)} %refs_1_.1, bf16[640,1280]{1,0:T(8,128)(2,1)} %refs_2_.1, ...), custom_call_target="tpu_custom_call" | custom-call | tf_op jit(solution)/shard_map/pallas_call | solution.py:92
  15.8 3.6 %collective-permute-done.2.refs_3_.refs_12_ = f32[8,128]{1,0:T(8,128)S(1)} collective-permute-done((f32[8,128]{1,0:T(8,128)S(1)}, f32[8,128]{1,0:T(8,128)S(1)}, u32[]{:S(2)}, u32[]{:S(2)}) %collective-permute-start.2) | collective-permute-done | bytes 4128 | tf_op jit(solution)/shard_map/ppermute | solution.py:438
  19.4 0.0 collective-permute-done.1.refs_1_.refs_2_.refs_7_
  19.4 0.0 collective-permute-done.refs_0_.refs_1_.refs_6_
  19.5 0.2 collective-permute-start.4
  19.7 1.9 %collective-permute-start.3 = (bf16[144,640]{1,0:T(8,128)(2,1)S(1)}, bf16[144,640]{1,0:T(8,128)(2,1)S(1)}, u32[]{:S(2)}, u32[]{:S(2)}) collective-permute-start(bf16[144,640]{1,0:T(8,128)(2,1)S(1)} %get-tuple-element.38.refs_4_), channel_id=1, source_target_pairs={{0,2},{2,4},{4,6},{6,8},{8,10},{10,12},{12,14},{14,0},{1,3},{3,5},... | collective-permute-start | bytes 552968 | tf_op jit(solution)/shard_map/ppermute | solution.py:433
  21.6 1.6 %shard_map.143.refs_3_.refs_1_ = f32[128,640]{1,0:T(8,128)S(1)} custom-call(f32[3]{0:T(128)S(1)} %add_convert_fusion.refs_3_.refs_0_, bf16[272,640]{1,0:T(8,128)(2,1)S(1)} %collective-permute-done.refs_0_.refs_1_.refs_6_, bf16[272,640]{1,0:T(8,128)(2,1)S(1)} %collective-permute-done.1.refs_1_.refs_2_.refs_7_, ...), custom_call_target="tpu_custom_call" | custom-call | tf_op jit(solution)/shard_map/pallas_call | solution.py:92
  23.2 0.7 shard_map.144.refs_2_
  23.9 1.2 %collective-permute-done.4.refs_1_ = bf16[144,640]{1,0:T(8,128)(2,1)S(1)} collective-permute-done((bf16[144,640]{1,0:T(8,128)(2,1)S(1)}, bf16[144,640]{1,0:T(8,128)(2,1)S(1)}, u32[]{:S(2)}, u32[]{:S(2)}) %collective-permute-start.4) | collective-permute-done | bytes 184352 | tf_op jit(solution)/shard_map/ppermute | solution.py:434
  25.1 1.4 %collective-permute-done.3.refs_0_ = bf16[144,640]{1,0:T(8,128)(2,1)S(1)} collective-permute-done((bf16[144,640]{1,0:T(8,128)(2,1)S(1)}, bf16[144,640]{1,0:T(8,128)(2,1)S(1)}, u32[]{:S(2)}, u32[]{:S(2)}) %collective-permute-start.3) | collective-permute-done | bytes 184352 | tf_op jit(solution)/shard_map/ppermute | solution.py:433
  26.4 0.8 collective-permute-start.5
  27.2 2.5 %collective-permute-start.6 = (bf16[144,640]{1,0:T(8,128)(2,1)S(1)}, bf16[144,640]{1,0:T(8,128)(2,1)S(1)}, u32[]{:S(2)}, u32[]{:S(2)}) collective-permute-start(bf16[144,640]{1,0:T(8,128)(2,1)S(1)} %get-tuple-element.43.refs_1_.refs_9_), channel_id=1, source_target_pairs={{2,0},{4,2},{6,4},{8,6},{10,8},{12,10},{14,12},{0,14},{3,1},{5,3},... | collective-permute-start | bytes 552968 | tf_op jit(solution)/shard_map/ppermute | solution.py:434
  29.7 0.7 shard_map.146.refs_2_.refs_3_
  30.4 2.8 %collective-permute-done.5.refs_0_ = bf16[144,640]{1,0:T(8,128)(2,1)S(1)} collective-permute-done((bf16[144,640]{1,0:T(8,128)(2,1)S(1)}, bf16[144,640]{1,0:T(8,128)(2,1)S(1)}, u32[]{:S(2)}, u32[]{:S(2)}) %collective-permute-start.5) | collective-permute-done | bytes 184352 | tf_op jit(solution)/shard_map/ppermute | solution.py:433
  33.2 1.3 %shard_map.148 = (bf16[144,640]{1,0:T(8,128)(2,1)S(1)}, f32[128,640]{1,0:T(8,128)S(1)}, bf16[128,640]{1,0:T(8,128)(2,1)S(1)}, bf16[128,640]{1,0:T(8,128)(2,1)S(1)}) custom-call(f32[1,128,640]{2,1,0:T(8,128)S(1)} %get-tuple-element.35.refs_0_.refs_2_, f32[128,640]{1,0:T(8,128)S(1)} %shard_map.143.refs_3_.refs_1_, ...), custom_call_target="tpu_custom_call" | custom-call | tf_op jit(solution)/shard_map/pallas_call | solution.py:92
  34.5 3.3 %collective-permute-start.10 = (bf16[128,640]{1,0:T(8,128)(2,1)S(1)}, bf16[128,640]{1,0:T(8,128)(2,1)S(1)}, u32[]{:S(2)}, u32[]{:S(2)}) collective-permute-start(bf16[128,640]{1,0:T(8,128)(2,1)S(1)} %get-tuple-element.48.refs_5_), channel_id=1, source_target_pairs={{2,0},{4,2},{6,4},{8,6},{10,8},{12,10},{14,12},{0,14},{3,1},{5,3},... | collective-permute-start | bytes 491528 | tf_op jit(solution)/shard_map/ppermute | solution.py:434
  37.8 0.0 collective-permute-start.9
  37.8 0.7 shard_map.149.refs_4_
  38.5 2.7 %collective-permute-done.7.refs_6_ = bf16[144,640]{1,0:T(8,128)(2,1)S(1)} collective-permute-done((bf16[144,640]{1,0:T(8,128)(2,1)S(1)}, bf16[144,640]{1,0:T(8,128)(2,1)S(1)}, u32[]{:S(2)}, u32[]{:S(2)}) %collective-permute-start.7) | collective-permute-done | bytes 184352 | tf_op jit(solution)/shard_map/ppermute | solution.py:433
  41.2 2.8 %shard_map.150.refs_2_.refs_3_ = bf16[128,640]{1,0:T(8,128)(2,1)S(1)} custom-call(bf16[128,640]{1,0:T(8,128)(2,1)S(1)} %get-tuple-element.46.refs_0_, f32[128,640]{1,0:T(8,128)S(1)} %get-tuple-element.47.refs_1_, bf16[256,1280]{1,0:T(8,128)(2,1)S(1)} %shard_map.144.refs_2_, bf16[256,1280]{1,0:T(8,128)(2,1)S(1)} %shard_map.146.refs_2_.refs_3_, ...), custom_call_target="tpu_custom_call" | custom-call | tf_op jit(solution)/shard_map/pallas_call | solution.py:92
  44.0 3.2 %collective-permute-start.8 = (bf16[128,640]{1,0:T(8,128)(2,1)S(1)}, bf16[128,640]{1,0:T(8,128)(2,1)S(1)}, u32[]{:S(2)}, u32[]{:S(2)}) collective-permute-start(bf16[128,640]{1,0:T(8,128)(2,1)S(1)} %shard_map.150.refs_2_.refs_3_), channel_id=1, source_target_pairs={{0,1},{1,0},{2,3},{3,2},{4,5},{5,4},{6,7},{7,6},{8,9},{9,8},{10,11... | collective-permute-start | bytes 491528 | tf_op jit(solution)/shard_map/ppermute | solution.py:528
  47.3 3.2 %collective-permute-start.12 = (bf16[128,640]{1,0:T(8,128)(2,1)S(1)}, bf16[128,640]{1,0:T(8,128)(2,1)S(1)}, u32[]{:S(2)}, u32[]{:S(2)}) collective-permute-start(bf16[128,640]{1,0:T(8,128)(2,1)S(1)} %get-tuple-element.51.refs_1_), channel_id=1, source_target_pairs={{2,0},{4,2},{6,4},{8,6},{10,8},{12,10},{14,12},{0,14},{3,1},{5,3},... | collective-permute-start | bytes 491528 | tf_op jit(solution)/shard_map/ppermute | solution.py:434
  50.5 0.7 shard_map.152.refs_5_.refs_1_.refs_2_
  51.2 0.1 collective-permute-start.16
  51.3 2.0 %collective-permute-start.15 = (bf16[144,640]{1,0:T(8,128)(2,1)S(1)}, bf16[144,640]{1,0:T(8,128)(2,1)S(1)}, u32[]{:S(2)}, u32[]{:S(2)}) collective-permute-start(bf16[144,640]{1,0:T(8,128)(2,1)S(1)} %shard_map.155), channel_id=1, source_target_pairs={{0,2},{2,4},{4,6},{6,8},{8,10},{10,12},{12,14},{14,0},{1,3},{3,5},... | collective-permute-start | bytes 552968 | tf_op jit(solution)/shard_map/ppermute | solution.py:433
  53.3 1.2 %shard_map.153 = (f32[1,128,640]{2,1,0:T(8,128)S(1)}, f32[8,128]{1,0:T(8,128)S(1)}) custom-call(f32[3]{0:T(128)S(1)} %add_convert_fusion.refs_3_.refs_0_, f32[8,640]{1,0:T(8,128)S(1)} %get-tuple-element.34.refs_2_.refs_1_.refs_5_, f32[1,128,640]{2,1,0:T(8,128)S(1)} %get-tuple-element.35.refs_0_.refs_2_, bf16[128,640]{1,0:T(8,128)(2,1)S(1)} %shard_map.150.refs_2_.refs_3_, ...), custom_call_target="tpu_custom_call" | custom-call | tf_op jit(solution)/shard_map/pallas_call | solution.py:92
  54.5 0.1 collective-permute-done.11.refs_1_.refs_0_
  54.7 2.5 %collective-permute-start.14 = (bf16[144,640]{1,0:T(8,128)(2,1)S(1)}, bf16[144,640]{1,0:T(8,128)(2,1)S(1)}, u32[]{:S(2)}, u32[]{:S(2)}) collective-permute-start(bf16[144,640]{1,0:T(8,128)(2,1)S(1)} %get-tuple-element.55), channel_id=1, source_target_pairs={{2,0},{4,2},{6,4},{8,6},{10,8},{12,10},{14,12},{0,14},{3,1},{5,3},... | collective-permute-start | bytes 552968 | tf_op jit(solution)/shard_map/ppermute | solution.py:434
  57.1 1.0 %collective-permute-done.15.refs_1_ = bf16[144,640]{1,0:T(8,128)(2,1)S(1)} collective-permute-done((bf16[144,640]{1,0:T(8,128)(2,1)S(1)}, bf16[144,640]{1,0:T(8,128)(2,1)S(1)}, u32[]{:S(2)}, u32[]{:S(2)}) %collective-permute-start.15) | collective-permute-done | bytes 184352 | tf_op jit(solution)/shard_map/ppermute | solution.py:433
  58.1 1.6 %shard_map.156.refs_3_.refs_4_ = f32[128,640]{1,0:T(8,128)S(1)} custom-call(f32[3]{0:T(128)S(1)} %add_convert_fusion.refs_3_.refs_0_, bf16[144,640]{1,0:T(8,128)(2,1)S(1)} %collective-permute-done.15.refs_1_, bf16[144,640]{1,0:T(8,128)(2,1)S(1)} %collective-permute-done.16.refs_2_, bf16[3,3,640,640]{3,2,1,0:T(8,128)(2,1)S(1)} %get-tuple-element.36.refs_3_.refs_6_, ...), custom_call_target="tpu_custom_call" | custom-call | tf_op jit(solution)/shard_map/pallas_call | solution.py:92
  59.7 0.7 shard_map.157.refs_3_
  60.4 3.5 %collective-permute-done.13.refs_1_.refs_0_ = bf16[144,640]{1,0:T(8,128)(2,1)S(1)} collective-permute-done((bf16[144,640]{1,0:T(8,128)(2,1)S(1)}, bf16[144,640]{1,0:T(8,128)(2,1)S(1)}, u32[]{:S(2)}, u32[]{:S(2)}) %collective-permute-start.13) | collective-permute-done | bytes 184352 | tf_op jit(solution)/shard_map/ppermute | solution.py:433
  64.0 0.1 collective-permute-start.19
  64.1 1.1 %collective-permute-start.18 = (f32[8,128]{1,0:T(8,128)S(1)}, f32[8,128]{1,0:T(8,128)S(1)}, u32[]{:S(2)}, u32[]{:S(2)}) collective-permute-start(f32[8,128]{1,0:T(8,128)S(1)} %get-tuple-element.58), channel_id=1, source_target_pairs={{0,10},{2,12},{4,14},{6,0},{8,2},{10,4},{12,6},{14,8},{1,11},{3,13... | collective-permute-start | bytes 12296 | tf_op jit(solution)/shard_map/ppermute | solution.py:438
  65.2 3.0 %collective-permute-start.17 = (f32[8,128]{1,0:T(8,128)S(1)}, f32[8,128]{1,0:T(8,128)S(1)}, u32[]{:S(2)}, u32[]{:S(2)}) collective-permute-start(f32[8,128]{1,0:T(8,128)S(1)} %get-tuple-element.57.refs_2_.refs_0_), channel_id=1, source_target_pairs={{0,6},{2,8},{4,10},{6,12},{8,14},{10,0},{12,2},{14,4},{1,7},{3,9},... | collective-permute-start | bytes 12296 | tf_op jit(solution)/shard_map/ppermute | solution.py:438
  68.2 0.7 shard_map.160.refs_2_.refs_4_
  68.9 1.9 %collective-permute-done.19.refs_0_ = bf16[144,640]{1,0:T(8,128)(2,1)S(1)} collective-permute-done((bf16[144,640]{1,0:T(8,128)(2,1)S(1)}, bf16[144,640]{1,0:T(8,128)(2,1)S(1)}, u32[]{:S(2)}, u32[]{:S(2)}) %collective-permute-start.19) | collective-permute-done | bytes 184352 | tf_op jit(solution)/shard_map/ppermute | solution.py:433
  70.8 0.4 shard_map.161.refs_8_.refs_6_
  71.3 0.5 collective-permute-done.17.refs_1_
  71.8 1.3 %shard_map.162 = (bf16[128,640]{1,0:T(8,128)(2,1)S(1)}, f32[128,640]{1,0:T(8,128)S(1)}, bf16[128,640]{1,0:T(8,128)(2,1)S(1)}) custom-call(f32[8,128]{1,0:T(8,128)S(1)} %get-tuple-element.57.refs_2_.refs_0_, f32[8,128]{1,0:T(8,128)S(1)} %collective-permute-done.17.refs_1_, f32[8,128]{1,0:T(8,128)S(1)} %collective-permute-done.18.refs_2_, ...), custom_call_target="tpu_custom_call" | custom-call | tf_op jit(solution)/shard_map/pallas_call | solution.py:92
  73.1 2.6 %shard_map.163.refs_3_ = bf16[128,640]{1,0:T(8,128)(2,1)S(1)} custom-call(bf16[128,640]{1,0:T(8,128)(2,1)S(1)} %get-tuple-element.61.refs_0_, f32[128,640]{1,0:T(8,128)S(1)} %get-tuple-element.62.refs_1_, bf16[256,1280]{1,0:T(8,128)(2,1)S(1)} %shard_map.152.refs_5_.refs_1_.refs_2_, bf16[256,1280]{1,0:T(8,128)(2,1)S(1)} %shard_map.157.refs_3_, ...), custom_call_target="tpu_custom_call" | custom-call | tf_op jit(solution)/shard_map/pallas_call | solution.py:92
  75.7 2.2 %collective-permute-start.20 = (bf16[128,640]{1,0:T(8,128)(2,1)S(1)}, bf16[128,640]{1,0:T(8,128)(2,1)S(1)}, u32[]{:S(2)}, u32[]{:S(2)}) collective-permute-start(bf16[128,640]{1,0:T(8,128)(2,1)S(1)} %shard_map.163.refs_3_), channel_id=1, source_target_pairs={{0,1},{1,0},{2,3},{3,2},{4,5},{5,4},{6,7},{7,6},{8,9},{9,8},{10,11... | collective-permute-start | bytes 491528 | tf_op jit(solution)/shard_map/ppermute | solution.py:528
  77.9 4.7 %collective-permute-done.20.refs_4_ = bf16[128,640]{1,0:T(8,128)(2,1)S(1)} collective-permute-done((bf16[128,640]{1,0:T(8,128)(2,1)S(1)}, bf16[128,640]{1,0:T(8,128)(2,1)S(1)}, u32[]{:S(2)}, u32[]{:S(2)}) %collective-permute-start.20) | collective-permute-done | bytes 163872 | tf_op jit(solution)/shard_map/ppermute | solution.py:528
  82.6 1.5 %shard_map.164 = (f32[1,128,640]{2,1,0:T(8,128)}, f32[1,128,640]{2,1,0:T(8,128)}) custom-call(f32[3]{0:T(128)S(1)} %add_convert_fusion.refs_3_.refs_0_, f32[8,640]{1,0:T(8,128)S(1)} %get-tuple-element.34.refs_2_.refs_1_.refs_5_, f32[1,128,640]{2,1,0:T(8,128)S(1)} %get-tuple-element.52.refs_3_.refs_2_, bf16[128,640]{1,0:T(8,128)(2,1)S(1)} %shard_map.163.refs_3_, ...), custom_call_target="tpu_custom_call" | custom-call | tf_op jit(solution)/shard_map/pallas_call | solution.py:92
  (20 shorter events, 0.1 us)
Async XLA Ops:
  2.4 17.1 %collective-permute-start.1 = (bf16[272,640]{1,0:T(8,128)(2,1)S(1)}, bf16[272,640]{1,0:T(8,128)(2,1)S(1)}, u32[]{:S(2)}, u32[]{:S(2)}) collective-permute-start(bf16[272,640]{1,0:T(8,128)(2,1)S(1)} %get-tuple-element.33.refs_10_.refs_5_), channel_id=1, source_target_pairs={{2,0},{4,2},{6,4},{8,6},{10,8},{12,10},{14,12},{0,14},{3,1},{5,3},... | collective-permute-start | bytes 1044488 | tf_op jit(solution)/shard_map/ppermute | solution.py:434
  8.3 11.1 %collective-permute-start = (bf16[272,640]{1,0:T(8,128)(2,1)S(1)}, bf16[272,640]{1,0:T(8,128)(2,1)S(1)}, u32[]{:S(2)}, u32[]{:S(2)}) collective-permute-start(bf16[272,640]{1,0:T(8,128)(2,1)S(1)} %get-tuple-element.33.refs_10_.refs_5_), channel_id=1, source_target_pairs={{0,2},{2,4},{4,6},{6,8},{8,10},{10,12},{12,14},{14,0},{1,3},{3,5},... | collective-permute-start | bytes 1044488 | tf_op jit(solution)/shard_map/ppermute | solution.py:433
  8.3 11.1 %collective-permute-start.2 = (f32[8,128]{1,0:T(8,128)S(1)}, f32[8,128]{1,0:T(8,128)S(1)}, u32[]{:S(2)}, u32[]{:S(2)}) collective-permute-start(f32[8,128]{1,0:T(8,128)S(1)} %get-tuple-element.37), channel_id=1, source_target_pairs={{0,8},{2,10},{4,12},{6,14},{8,0},{10,2},{12,4},{14,6},{1,9},{3,11}... | collective-permute-start | bytes 12296 | tf_op jit(solution)/shard_map/ppermute | solution.py:438
  19.5 5.6 %collective-permute-start.4 = (bf16[144,640]{1,0:T(8,128)(2,1)S(1)}, bf16[144,640]{1,0:T(8,128)(2,1)S(1)}, u32[]{:S(2)}, u32[]{:S(2)}) collective-permute-start(bf16[144,640]{1,0:T(8,128)(2,1)S(1)} %get-tuple-element.40), channel_id=1, source_target_pairs={{2,0},{4,2},{6,4},{8,6},{10,8},{12,10},{14,12},{0,14},{3,1},{5,3},... | collective-permute-start | bytes 552968 | tf_op jit(solution)/shard_map/ppermute | solution.py:434
  19.7 6.7 %collective-permute-start.3 = (bf16[144,640]{1,0:T(8,128)(2,1)S(1)}, bf16[144,640]{1,0:T(8,128)(2,1)S(1)}, u32[]{:S(2)}, u32[]{:S(2)}) collective-permute-start(bf16[144,640]{1,0:T(8,128)(2,1)S(1)} %get-tuple-element.38.refs_4_), channel_id=1, source_target_pairs={{0,2},{2,4},{4,6},{6,8},{8,10},{10,12},{12,14},{14,0},{1,3},{3,5},... | collective-permute-start | bytes 552968 | tf_op jit(solution)/shard_map/ppermute | solution.py:433
  26.4 6.7 %collective-permute-start.5 = (bf16[144,640]{1,0:T(8,128)(2,1)S(1)}, bf16[144,640]{1,0:T(8,128)(2,1)S(1)}, u32[]{:S(2)}, u32[]{:S(2)}) collective-permute-start(bf16[144,640]{1,0:T(8,128)(2,1)S(1)} %get-tuple-element.42.refs_0_.refs_3_.refs_8_), channel_id=1, source_target_pairs={{0,2},{2,4},{4,6},{6,8},{8,10},{10,12},{12,14},{14,0},{1,3},{3,5},... | collective-permute-start | bytes 552968 | tf_op jit(solution)/shard_map/ppermute | solution.py:433
  27.2 6.0 %collective-permute-start.6 = (bf16[144,640]{1,0:T(8,128)(2,1)S(1)}, bf16[144,640]{1,0:T(8,128)(2,1)S(1)}, u32[]{:S(2)}, u32[]{:S(2)}) collective-permute-start(bf16[144,640]{1,0:T(8,128)(2,1)S(1)} %get-tuple-element.43.refs_1_.refs_9_), channel_id=1, source_target_pairs={{2,0},{4,2},{6,4},{8,6},{10,8},{12,10},{14,12},{0,14},{3,1},{5,3},... | collective-permute-start | bytes 552968 | tf_op jit(solution)/shard_map/ppermute | solution.py:434
  33.2 8.0 %collective-permute-start.7 = (bf16[144,640]{1,0:T(8,128)(2,1)S(1)}, bf16[144,640]{1,0:T(8,128)(2,1)S(1)}, u32[]{:S(2)}, u32[]{:S(2)}) collective-permute-start(bf16[144,640]{1,0:T(8,128)(2,1)S(1)} %get-tuple-element.44.refs_10_.refs_0_.refs_3_), channel_id=1, source_target_pairs={{0,2},{2,4},{4,6},{6,8},{8,10},{10,12},{12,14},{14,0},{1,3},{3,5},... | collective-permute-start | bytes 552968 | tf_op jit(solution)/shard_map/ppermute | solution.py:433
  34.5 12.7 %collective-permute-start.10 = (bf16[128,640]{1,0:T(8,128)(2,1)S(1)}, bf16[128,640]{1,0:T(8,128)(2,1)S(1)}, u32[]{:S(2)}, u32[]{:S(2)}) collective-permute-start(bf16[128,640]{1,0:T(8,128)(2,1)S(1)} %get-tuple-element.48.refs_5_), channel_id=1, source_target_pairs={{2,0},{4,2},{6,4},{8,6},{10,8},{12,10},{14,12},{0,14},{3,1},{5,3},... | collective-permute-start | bytes 491528 | tf_op jit(solution)/shard_map/ppermute | solution.py:434
  37.8 9.4 %collective-permute-start.9 = (bf16[128,640]{1,0:T(8,128)(2,1)S(1)}, bf16[128,640]{1,0:T(8,128)(2,1)S(1)}, u32[]{:S(2)}, u32[]{:S(2)}) collective-permute-start(bf16[128,640]{1,0:T(8,128)(2,1)S(1)} %get-tuple-element.48.refs_5_), channel_id=1, source_target_pairs={{0,2},{2,4},{4,6},{6,8},{8,10},{10,12},{12,14},{14,0},{1,3},{3,5},... | collective-permute-start | bytes 491528 | tf_op jit(solution)/shard_map/ppermute | solution.py:433
  44.0 9.3 %collective-permute-start.8 = (bf16[128,640]{1,0:T(8,128)(2,1)S(1)}, bf16[128,640]{1,0:T(8,128)(2,1)S(1)}, u32[]{:S(2)}, u32[]{:S(2)}) collective-permute-start(bf16[128,640]{1,0:T(8,128)(2,1)S(1)} %shard_map.150.refs_2_.refs_3_), channel_id=1, source_target_pairs={{0,1},{1,0},{2,3},{3,2},{4,5},{5,4},{6,7},{7,6},{8,9},{9,8},{10,11... | collective-permute-start | bytes 491528 | tf_op jit(solution)/shard_map/ppermute | solution.py:528
  47.2 7.4 %collective-permute-start.11 = (bf16[128,640]{1,0:T(8,128)(2,1)S(1)}, bf16[128,640]{1,0:T(8,128)(2,1)S(1)}, u32[]{:S(2)}, u32[]{:S(2)}) collective-permute-start(bf16[128,640]{1,0:T(8,128)(2,1)S(1)} %get-tuple-element.50.refs_0_), channel_id=1, source_target_pairs={{0,2},{2,4},{4,6},{6,8},{8,10},{10,12},{12,14},{14,0},{1,3},{3,5},... | collective-permute-start | bytes 491528 | tf_op jit(solution)/shard_map/ppermute | solution.py:433
  47.3 7.4 %collective-permute-start.12 = (bf16[128,640]{1,0:T(8,128)(2,1)S(1)}, bf16[128,640]{1,0:T(8,128)(2,1)S(1)}, u32[]{:S(2)}, u32[]{:S(2)}) collective-permute-start(bf16[128,640]{1,0:T(8,128)(2,1)S(1)} %get-tuple-element.51.refs_1_), channel_id=1, source_target_pairs={{2,0},{4,2},{6,4},{8,6},{10,8},{12,10},{14,12},{0,14},{3,1},{5,3},... | collective-permute-start | bytes 491528 | tf_op jit(solution)/shard_map/ppermute | solution.py:434
  51.2 5.9 %collective-permute-start.16 = (bf16[144,640]{1,0:T(8,128)(2,1)S(1)}, bf16[144,640]{1,0:T(8,128)(2,1)S(1)}, u32[]{:S(2)}, u32[]{:S(2)}) collective-permute-start(bf16[144,640]{1,0:T(8,128)(2,1)S(1)} %shard_map.155), channel_id=1, source_target_pairs={{2,0},{4,2},{6,4},{8,6},{10,8},{12,10},{14,12},{0,14},{3,1},{5,3},... | collective-permute-start | bytes 552968 | tf_op jit(solution)/shard_map/ppermute | solution.py:434
  51.3 6.8 %collective-permute-start.15 = (bf16[144,640]{1,0:T(8,128)(2,1)S(1)}, bf16[144,640]{1,0:T(8,128)(2,1)S(1)}, u32[]{:S(2)}, u32[]{:S(2)}) collective-permute-start(bf16[144,640]{1,0:T(8,128)(2,1)S(1)} %shard_map.155), channel_id=1, source_target_pairs={{0,2},{2,4},{4,6},{6,8},{8,10},{10,12},{12,14},{14,0},{1,3},{3,5},... | collective-permute-start | bytes 552968 | tf_op jit(solution)/shard_map/ppermute | solution.py:433
  54.7 5.8 %collective-permute-start.14 = (bf16[144,640]{1,0:T(8,128)(2,1)S(1)}, bf16[144,640]{1,0:T(8,128)(2,1)S(1)}, u32[]{:S(2)}, u32[]{:S(2)}) collective-permute-start(bf16[144,640]{1,0:T(8,128)(2,1)S(1)} %get-tuple-element.55), channel_id=1, source_target_pairs={{2,0},{4,2},{6,4},{8,6},{10,8},{12,10},{14,12},{0,14},{3,1},{5,3},... | collective-permute-start | bytes 552968 | tf_op jit(solution)/shard_map/ppermute | solution.py:434
  57.1 6.8 %collective-permute-start.13 = (bf16[144,640]{1,0:T(8,128)(2,1)S(1)}, bf16[144,640]{1,0:T(8,128)(2,1)S(1)}, u32[]{:S(2)}, u32[]{:S(2)}) collective-permute-start(bf16[144,640]{1,0:T(8,128)(2,1)S(1)} %get-tuple-element.54.refs_4_), channel_id=1, source_target_pairs={{0,2},{2,4},{4,6},{6,8},{8,10},{10,12},{12,14},{14,0},{1,3},{3,5},... | collective-permute-start | bytes 552968 | tf_op jit(solution)/shard_map/ppermute | solution.py:433
  64.0 6.8 %collective-permute-start.19 = (bf16[144,640]{1,0:T(8,128)(2,1)S(1)}, bf16[144,640]{1,0:T(8,128)(2,1)S(1)}, u32[]{:S(2)}, u32[]{:S(2)}) collective-permute-start(bf16[144,640]{1,0:T(8,128)(2,1)S(1)} %get-tuple-element.59.refs_0_.refs_3_), channel_id=1, source_target_pairs={{0,2},{2,4},{4,6},{6,8},{8,10},{10,12},{12,14},{14,0},{1,3},{3,5},... | collective-permute-start | bytes 552968 | tf_op jit(solution)/shard_map/ppermute | solution.py:433
  64.1 7.2 %collective-permute-start.18 = (f32[8,128]{1,0:T(8,128)S(1)}, f32[8,128]{1,0:T(8,128)S(1)}, u32[]{:S(2)}, u32[]{:S(2)}) collective-permute-start(f32[8,128]{1,0:T(8,128)S(1)} %get-tuple-element.58), channel_id=1, source_target_pairs={{0,10},{2,12},{4,14},{6,0},{8,2},{10,4},{12,6},{14,8},{1,11},{3,13... | collective-permute-start | bytes 12296 | tf_op jit(solution)/shard_map/ppermute | solution.py:438
  65.2 6.6 %collective-permute-start.17 = (f32[8,128]{1,0:T(8,128)S(1)}, f32[8,128]{1,0:T(8,128)S(1)}, u32[]{:S(2)}, u32[]{:S(2)}) collective-permute-start(f32[8,128]{1,0:T(8,128)S(1)} %get-tuple-element.57.refs_2_.refs_0_), channel_id=1, source_target_pairs={{0,6},{2,8},{4,10},{6,12},{8,14},{10,0},{12,2},{14,4},{1,7},{3,9},... | collective-permute-start | bytes 12296 | tf_op jit(solution)/shard_map/ppermute | solution.py:438
  75.7 6.9 %collective-permute-start.20 = (bf16[128,640]{1,0:T(8,128)(2,1)S(1)}, bf16[128,640]{1,0:T(8,128)(2,1)S(1)}, u32[]{:S(2)}, u32[]{:S(2)}) collective-permute-start(bf16[128,640]{1,0:T(8,128)(2,1)S(1)} %shard_map.163.refs_3_), channel_id=1, source_target_pairs={{0,1},{1,0},{2,3},{3,2},{4,5},{5,4},{6,7},{7,6},{8,9},{9,8},{10,11... | collective-permute-start | bytes 491528 | tf_op jit(solution)/shard_map/ppermute | solution.py:528

commit v7 on v5

--- a/solution.py
+++ b/solution.py
@@ -474,7 +474,7 @@
         after=(first,),
         limit=2,
     )
-    passing = trim(HEAD, ring1, (prep, opposite))
+    passing = [*trim(HEAD, ring1[:1], (prep,)), *trim(HEAD, ring1[1:], (prep, opposite))]
     ring2 = [up(passing[0]), down(passing[1])]
     keys = lambda blocks, after=(): call(
         keys_body,

time: 85.5 us -> 85.6 us (level)
    pallas_call x20 -> x21, Pallas kernels: 24.2 us -> 24.2 us  [call(): pl.pallas_call(wrapped, out_shape=jax.tree.unflatten(tree, leaves), in_sp...]
where the time goes in v7:
time: 85.6 us; the launch traced here: 84.5 us
  starting transfers between devices  35.4 us (41%)
  Pallas kernels  24.2 us (28%)
  waiting for transfers between devices  23.9 us (28%)
  between operations  1.02 us (1%)
    pallas_call x21, Pallas kernels, call(): pl.pallas_call(wrapped, out_shape=jax.tree.unflatten(tree, leaves), in_sp...  24.2 us
    ppermute x7, starting transfers between devices, shards(): down = lambda x: lax.ppermute(x, 'patch', downward)  17.6 us
    ppermute x9, waiting for transfers between devices, shards(): up = lambda x: lax.ppermute(x, 'patch', upward)  13.5 us
    ppermute x3, starting transfers between devices, shards(): lax.ppermute(x, 'patch', [(i, (i + far) % PATCHES) for i in range(PATCHES)])  7.48 us
    ppermute x2, starting transfers between devices, shards(): exchange = lambda x: lax.ppermute(x, 'cfg', [(0, 1), (1, 0)])  5.29 us
    ppermute x9, starting transfers between devices, shards(): up = lambda x: lax.ppermute(x, 'patch', upward)  4.97 us
    ppermute x2, waiting for transfers between devices, shards(): exchange = lambda x: lax.ppermute(x, 'cfg', [(0, 1), (1, 0)])  4.9 us
    ppermute x3, waiting for transfers between devices, shards(): lax.ppermute(x, 'patch', [(i, (i + far) % PATCHES) for i in range(PATCHES)])  4.4 us
  transfers between devices with their start and end apart: 21, of which 11 were waited for; matrix products, arithmetic and copies ran while one was open for 0% of the time, Pallas kernels for 20%

profile of v7, /device:TPU:2, one launch (start us, length us, event | category | flops | bytes accessed | tf_op | source)
XLA Modules:
  0.0 84.5 jit_solution(4872017480097164447)
XLA Ops:
  0.6 0.1 add_convert_fusion.refs_3_.refs_0_
  0.7 1.6 %shard_map.140 = (bf16[272,640]{1,0:T(8,128)(2,1)S(1)}, f32[1,128,640]{2,1,0:T(8,128)S(1)}, f32[8,128]{1,0:T(8,128)S(1)}) custom-call(f32[1,128,640]{2,1,0:T(8,128)} %refs_0_.2, bf16[128,640]{1,0:T(8,128)(2,1)} %bitcast.6, bf16[128,640]{1,0:T(8,128)(2,1)} %bitcast.7, f32[3]{0:T(128)S(1)} %add_convert_fusion.refs_3_.refs_0_), custom_call_target="tpu_custom_call" | custom-call | tf_op jit(solution)/shard_map/pallas_call | solution.py:92
  2.4 5.9 %collective-permute-start.1 = (bf16[272,640]{1,0:T(8,128)(2,1)S(1)}, bf16[272,640]{1,0:T(8,128)(2,1)S(1)}, u32[]{:S(2)}, u32[]{:S(2)}) collective-permute-start(bf16[272,640]{1,0:T(8,128)(2,1)S(1)} %get-tuple-element.31.refs_10_.refs_5_), channel_id=1, source_target_pairs={{2,0},{4,2},{6,4},{8,6},{10,8},{12,10},{14,12},{0,14},{3,1},{5,3},... | collective-permute-start | bytes 1044488 | tf_op jit(solution)/shard_map/ppermute | solution.py:434
  8.3 3.4 %collective-permute-start.3 = (f32[8,128]{1,0:T(8,128)S(1)}, f32[8,128]{1,0:T(8,128)S(1)}, u32[]{:S(2)}, u32[]{:S(2)}) collective-permute-start(f32[8,128]{1,0:T(8,128)S(1)} %get-tuple-element.36), channel_id=1, source_target_pairs={{0,8},{2,10},{4,12},{6,14},{8,0},{10,2},{12,4},{14,6},{1,9},{3,11}... | collective-permute-start | bytes 12296 | tf_op jit(solution)/shard_map/ppermute | solution.py:438
  11.7 4.1 %shard_map.141 = (f32[8,640]{1,0:T(8,128)S(1)}, bf16[3,3,640,640]{3,2,1,0:T(8,128)(2,1)S(1)}, bf16[640,640]{1,0:T(8,128)(2,1)S(1)}, bf16[640,1280]{1,0:T(8,128)(2,1)S(1)}, bf16[640,640]{1,0:T(8,128)(2,1)S(1)}) custom-call(bf16[3,3,640,640]{3,2,1,0:T(8,128)(2,1)} %refs_0_.3, bf16[640,640]{1,0:T(8,128)(2,1)} %refs_1_.1, bf16[640,1280]{1,0:T(8,128)(2,1)} %refs_2_.1, ...), custom_call_target="tpu_custom_call" | custom-call | tf_op jit(solution)/shard_map/pallas_call | solution.py:92
  15.8 3.6 %collective-permute-done.3.refs_2_.refs_12_ = f32[8,128]{1,0:T(8,128)S(1)} collective-permute-done((f32[8,128]{1,0:T(8,128)S(1)}, f32[8,128]{1,0:T(8,128)S(1)}, u32[]{:S(2)}, u32[]{:S(2)}) %collective-permute-start.3) | collective-permute-done | bytes 4128 | tf_op jit(solution)/shard_map/ppermute | solution.py:438
  19.4 0.0 collective-permute-done.1.refs_2_.refs_0_.refs_1_.refs_7_
  19.4 0.2 collective-permute-start.4
  19.7 2.0 %collective-permute-start.2 = (bf16[144,640]{1,0:T(8,128)(2,1)S(1)}, bf16[144,640]{1,0:T(8,128)(2,1)S(1)}, u32[]{:S(2)}, u32[]{:S(2)}) collective-permute-start(bf16[144,640]{1,0:T(8,128)(2,1)S(1)} %shard_map.142.refs_4_), channel_id=1, source_target_pairs={{0,2},{2,4},{4,6},{6,8},{8,10},{10,12},{12,14},{14,0},{1,3},{3,5},... | collective-permute-start | bytes 552968 | tf_op jit(solution)/shard_map/ppermute | solution.py:433
  21.6 1.6 %shard_map.143.refs_3_.refs_1_ = f32[128,640]{1,0:T(8,128)S(1)} custom-call(f32[3]{0:T(128)S(1)} %add_convert_fusion.refs_3_.refs_0_, bf16[272,640]{1,0:T(8,128)(2,1)S(1)} %collective-permute-done.refs_0_.refs_1_.refs_6_, bf16[272,640]{1,0:T(8,128)(2,1)S(1)} %collective-permute-done.1.refs_2_.refs_0_.refs_1_.refs_7_, ...), custom_call_target="tpu_custom_call" | custom-call | tf_op jit(solution)/shard_map/pallas_call | solution.py:92
  23.3 0.7 shard_map.145.refs_2_
  24.0 1.1 %collective-permute-done.4.refs_1_ = bf16[144,640]{1,0:T(8,128)(2,1)S(1)} collective-permute-done((bf16[144,640]{1,0:T(8,128)(2,1)S(1)}, bf16[144,640]{1,0:T(8,128)(2,1)S(1)}, u32[]{:S(2)}, u32[]{:S(2)}) %collective-permute-start.4) | collective-permute-done | bytes 184352 | tf_op jit(solution)/shard_map/ppermute | solution.py:434
  25.1 1.5 %collective-permute-done.2.refs_0_ = bf16[144,640]{1,0:T(8,128)(2,1)S(1)} collective-permute-done((bf16[144,640]{1,0:T(8,128)(2,1)S(1)}, bf16[144,640]{1,0:T(8,128)(2,1)S(1)}, u32[]{:S(2)}, u32[]{:S(2)}) %collective-permute-start.2) | collective-permute-done | bytes 184352 | tf_op jit(solution)/shard_map/ppermute | solution.py:433
  26.5 0.8 collective-permute-start.5
  27.3 2.4 %collective-permute-start.6 = (bf16[144,640]{1,0:T(8,128)(2,1)S(1)}, bf16[144,640]{1,0:T(8,128)(2,1)S(1)}, u32[]{:S(2)}, u32[]{:S(2)}) collective-permute-start(bf16[144,640]{1,0:T(8,128)(2,1)S(1)} %get-tuple-element.39.refs_1_.refs_9_), channel_id=1, source_target_pairs={{2,0},{4,2},{6,4},{8,6},{10,8},{12,10},{14,12},{0,14},{3,1},{5,3},... | collective-permute-start | bytes 552968 | tf_op jit(solution)/shard_map/ppermute | solution.py:434
  29.8 0.7 shard_map.147.refs_2_.refs_3_
  30.4 2.8 %collective-permute-done.5.refs_0_ = bf16[144,640]{1,0:T(8,128)(2,1)S(1)} collective-permute-done((bf16[144,640]{1,0:T(8,128)(2,1)S(1)}, bf16[144,640]{1,0:T(8,128)(2,1)S(1)}, u32[]{:S(2)}, u32[]{:S(2)}) %collective-permute-start.5) | collective-permute-done | bytes 184352 | tf_op jit(solution)/shard_map/ppermute | solution.py:433
  33.3 0.1 collective-permute-start.7
  33.4 1.3 %shard_map.149 = (bf16[160,640]{1,0:T(8,128)(2,1)S(1)}, f32[128,640]{1,0:T(8,128)S(1)}, bf16[128,640]{1,0:T(8,128)(2,1)S(1)}, bf16[128,640]{1,0:T(8,128)(2,1)S(1)}) custom-call(f32[1,128,640]{2,1,0:T(8,128)S(1)} %get-tuple-element.33.refs_0_.refs_2_, f32[128,640]{1,0:T(8,128)S(1)} %shard_map.143.refs_3_.refs_1_, ...), custom_call_target="tpu_custom_call" | custom-call | tf_op jit(solution)/shard_map/pallas_call | solution.py:92
  34.7 3.3 %collective-permute-start.10 = (bf16[128,640]{1,0:T(8,128)(2,1)S(1)}, bf16[128,640]{1,0:T(8,128)(2,1)S(1)}, u32[]{:S(2)}, u32[]{:S(2)}) collective-permute-start(bf16[128,640]{1,0:T(8,128)(2,1)S(1)} %get-tuple-element.44.refs_5_), channel_id=1, source_target_pairs={{2,0},{4,2},{6,4},{8,6},{10,8},{12,10},{14,12},{0,14},{3,1},{5,3},... | collective-permute-start | bytes 491528 | tf_op jit(solution)/shard_map/ppermute | solution.py:434
  37.9 0.0 collective-permute-start.9
  37.9 0.7 shard_map.150.refs_4_
  38.6 2.6 %collective-permute-done.7.refs_6_ = bf16[144,640]{1,0:T(8,128)(2,1)S(1)} collective-permute-done((bf16[144,640]{1,0:T(8,128)(2,1)S(1)}, bf16[144,640]{1,0:T(8,128)(2,1)S(1)}, u32[]{:S(2)}, u32[]{:S(2)}) %collective-permute-start.7) | collective-permute-done | bytes 184352 | tf_op jit(solution)/shard_map/ppermute | solution.py:433
  41.2 2.8 %shard_map.151.refs_2_.refs_3_ = bf16[128,640]{1,0:T(8,128)(2,1)S(1)} custom-call(bf16[128,640]{1,0:T(8,128)(2,1)S(1)} %get-tuple-element.42.refs_0_, f32[128,640]{1,0:T(8,128)S(1)} %get-tuple-element.43.refs_1_, bf16[256,1280]{1,0:T(8,128)(2,1)S(1)} %shard_map.145.refs_2_, bf16[256,1280]{1,0:T(8,128)(2,1)S(1)} %shard_map.147.refs_2_.refs_3_, ...), custom_call_target="tpu_custom_call" | custom-call | tf_op jit(solution)/shard_map/pallas_call | solution.py:92
  44.0 3.3 %collective-permute-start.8 = (bf16[128,640]{1,0:T(8,128)(2,1)S(1)}, bf16[128,640]{1,0:T(8,128)(2,1)S(1)}, u32[]{:S(2)}, u32[]{:S(2)}) collective-permute-start(bf16[128,640]{1,0:T(8,128)(2,1)S(1)} %shard_map.151.refs_2_.refs_3_), channel_id=1, source_target_pairs={{0,1},{1,0},{2,3},{3,2},{4,5},{5,4},{6,7},{7,6},{8,9},{9,8},{10,11... | collective-permute-start | bytes 491528 | tf_op jit(solution)/shard_map/ppermute | solution.py:528
  47.3 3.2 %collective-permute-start.12 = (bf16[128,640]{1,0:T(8,128)(2,1)S(1)}, bf16[128,640]{1,0:T(8,128)(2,1)S(1)}, u32[]{:S(2)}, u32[]{:S(2)}) collective-permute-start(bf16[128,640]{1,0:T(8,128)(2,1)S(1)} %get-tuple-element.47.refs_1_), channel_id=1, source_target_pairs={{2,0},{4,2},{6,4},{8,6},{10,8},{12,10},{14,12},{0,14},{3,1},{5,3},... | collective-permute-start | bytes 491528 | tf_op jit(solution)/shard_map/ppermute | solution.py:434
  50.6 0.7 shard_map.153.refs_5_.refs_1_.refs_2_
  51.2 0.1 collective-permute-start.16
  51.3 2.0 %collective-permute-start.15 = (bf16[160,640]{1,0:T(8,128)(2,1)S(1)}, bf16[160,640]{1,0:T(8,128)(2,1)S(1)}, u32[]{:S(2)}, u32[]{:S(2)}) collective-permute-start(bf16[160,640]{1,0:T(8,128)(2,1)S(1)} %shard_map.156), channel_id=1, source_target_pairs={{0,2},{2,4},{4,6},{6,8},{8,10},{10,12},{12,14},{14,0},{1,3},{3,5},... | collective-permute-start | bytes 614408 | tf_op jit(solution)/shard_map/ppermute | solution.py:433
  53.4 1.2 %shard_map.154 = (f32[1,128,640]{2,1,0:T(8,128)S(1)}, f32[8,128]{1,0:T(8,128)S(1)}) custom-call(f32[3]{0:T(128)S(1)} %add_convert_fusion.refs_3_.refs_0_, f32[8,640]{1,0:T(8,128)S(1)} %get-tuple-element.32.refs_1_.refs_2_.refs_5_, f32[1,128,640]{2,1,0:T(8,128)S(1)} %get-tuple-element.33.refs_0_.refs_2_, bf16[128,640]{1,0:T(8,128)(2,1)S(1)} %shard_map.151.refs_2_.refs_3_, ...), custom_call_target="tpu_custom_call" | custom-call | tf_op jit(solution)/shard_map/pallas_call | solution.py:92
  54.5 0.1 collective-permute-done.11.refs_1_.refs_0_
  54.7 2.5 %collective-permute-start.14 = (bf16[144,640]{1,0:T(8,128)(2,1)S(1)}, bf16[144,640]{1,0:T(8,128)(2,1)S(1)}, u32[]{:S(2)}, u32[]{:S(2)}) collective-permute-start(bf16[144,640]{1,0:T(8,128)(2,1)S(1)} %get-tuple-element.51), channel_id=1, source_target_pairs={{2,0},{4,2},{6,4},{8,6},{10,8},{12,10},{14,12},{0,14},{3,1},{5,3},... | collective-permute-start | bytes 552968 | tf_op jit(solution)/shard_map/ppermute | solution.py:434
  57.2 1.2 %collective-permute-done.15.refs_1_ = bf16[160,640]{1,0:T(8,128)(2,1)S(1)} collective-permute-done((bf16[160,640]{1,0:T(8,128)(2,1)S(1)}, bf16[160,640]{1,0:T(8,128)(2,1)S(1)}, u32[]{:S(2)}, u32[]{:S(2)}) %collective-permute-start.15) | collective-permute-done | bytes 204832 | tf_op jit(solution)/shard_map/ppermute | solution.py:433
  58.4 1.6 %shard_map.157.refs_3_.refs_4_ = f32[128,640]{1,0:T(8,128)S(1)} custom-call(f32[3]{0:T(128)S(1)} %add_convert_fusion.refs_3_.refs_0_, bf16[160,640]{1,0:T(8,128)(2,1)S(1)} %collective-permute-done.15.refs_1_, bf16[160,640]{1,0:T(8,128)(2,1)S(1)} %collective-permute-done.16.refs_2_, bf16[3,3,640,640]{3,2,1,0:T(8,128)(2,1)S(1)} %get-tuple-element.34.refs_3_.refs_6_, ...), custom_call_target="tpu_custom_call" | custom-call | tf_op jit(solution)/shard_map/pallas_call | solution.py:92
  60.0 0.7 shard_map.158.refs_3_
  60.7 3.3 %collective-permute-done.13.refs_1_.refs_0_ = bf16[144,640]{1,0:T(8,128)(2,1)S(1)} collective-permute-done((bf16[144,640]{1,0:T(8,128)(2,1)S(1)}, bf16[144,640]{1,0:T(8,128)(2,1)S(1)}, u32[]{:S(2)}, u32[]{:S(2)}) %collective-permute-start.13) | collective-permute-done | bytes 184352 | tf_op jit(solution)/shard_map/ppermute | solution.py:433
  64.1 0.1 collective-permute-start.19
  64.1 1.3 %collective-permute-start.18 = (f32[8,128]{1,0:T(8,128)S(1)}, f32[8,128]{1,0:T(8,128)S(1)}, u32[]{:S(2)}, u32[]{:S(2)}) collective-permute-start(f32[8,128]{1,0:T(8,128)S(1)} %get-tuple-element.54), channel_id=1, source_target_pairs={{0,10},{2,12},{4,14},{6,0},{8,2},{10,4},{12,6},{14,8},{1,11},{3,13... | collective-permute-start | bytes 12296 | tf_op jit(solution)/shard_map/ppermute | solution.py:438
  65.5 2.8 %collective-permute-start.17 = (f32[8,128]{1,0:T(8,128)S(1)}, f32[8,128]{1,0:T(8,128)S(1)}, u32[]{:S(2)}, u32[]{:S(2)}) collective-permute-start(f32[8,128]{1,0:T(8,128)S(1)} %get-tuple-element.53.refs_2_.refs_0_), channel_id=1, source_target_pairs={{0,6},{2,8},{4,10},{6,12},{8,14},{10,0},{12,2},{14,4},{1,7},{3,9},... | collective-permute-start | bytes 12296 | tf_op jit(solution)/shard_map/ppermute | solution.py:438
  68.3 0.7 shard_map.161.refs_2_.refs_4_
  69.0 1.9 %collective-permute-done.19.refs_0_ = bf16[144,640]{1,0:T(8,128)(2,1)S(1)} collective-permute-done((bf16[144,640]{1,0:T(8,128)(2,1)S(1)}, bf16[144,640]{1,0:T(8,128)(2,1)S(1)}, u32[]{:S(2)}, u32[]{:S(2)}) %collective-permute-start.19) | collective-permute-done | bytes 184352 | tf_op jit(solution)/shard_map/ppermute | solution.py:433
  70.9 0.4 shard_map.162.refs_8_.refs_6_
  71.3 0.8 collective-permute-done.17.refs_1_
  72.1 1.3 %shard_map.163 = (bf16[128,640]{1,0:T(8,128)(2,1)S(1)}, f32[128,640]{1,0:T(8,128)S(1)}, bf16[128,640]{1,0:T(8,128)(2,1)S(1)}) custom-call(f32[8,128]{1,0:T(8,128)S(1)} %get-tuple-element.53.refs_2_.refs_0_, f32[8,128]{1,0:T(8,128)S(1)} %collective-permute-done.17.refs_1_, f32[8,128]{1,0:T(8,128)S(1)} %collective-permute-done.18.refs_2_, ...), custom_call_target="tpu_custom_call" | custom-call | tf_op jit(solution)/shard_map/pallas_call | solution.py:92
  73.4 2.6 %shard_map.164.refs_3_ = bf16[128,640]{1,0:T(8,128)(2,1)S(1)} custom-call(bf16[128,640]{1,0:T(8,128)(2,1)S(1)} %get-tuple-element.57.refs_0_, f32[128,640]{1,0:T(8,128)S(1)} %get-tuple-element.58.refs_1_, bf16[256,1280]{1,0:T(8,128)(2,1)S(1)} %shard_map.153.refs_5_.refs_1_.refs_2_, bf16[256,1280]{1,0:T(8,128)(2,1)S(1)} %shard_map.158.refs_3_, ...), custom_call_target="tpu_custom_call" | custom-call | tf_op jit(solution)/shard_map/pallas_call | solution.py:92
  75.9 2.0 %collective-permute-start.20 = (bf16[128,640]{1,0:T(8,128)(2,1)S(1)}, bf16[128,640]{1,0:T(8,128)(2,1)S(1)}, u32[]{:S(2)}, u32[]{:S(2)}) collective-permute-start(bf16[128,640]{1,0:T(8,128)(2,1)S(1)} %shard_map.164.refs_3_), channel_id=1, source_target_pairs={{0,1},{1,0},{2,3},{3,2},{4,5},{5,4},{6,7},{7,6},{8,9},{9,8},{10,11... | collective-permute-start | bytes 491528 | tf_op jit(solution)/shard_map/ppermute | solution.py:528
  78.0 4.9 %collective-permute-done.20.refs_4_ = bf16[128,640]{1,0:T(8,128)(2,1)S(1)} collective-permute-done((bf16[128,640]{1,0:T(8,128)(2,1)S(1)}, bf16[128,640]{1,0:T(8,128)(2,1)S(1)}, u32[]{:S(2)}, u32[]{:S(2)}) %collective-permute-start.20) | collective-permute-done | bytes 163872 | tf_op jit(solution)/shard_map/ppermute | solution.py:528
  82.9 1.5 %shard_map.165 = (f32[1,128,640]{2,1,0:T(8,128)}, f32[1,128,640]{2,1,0:T(8,128)}) custom-call(f32[3]{0:T(128)S(1)} %add_convert_fusion.refs_3_.refs_0_, f32[8,640]{1,0:T(8,128)S(1)} %get-tuple-element.32.refs_1_.refs_2_.refs_5_, f32[1,128,640]{2,1,0:T(8,128)S(1)} %get-tuple-element.48.refs_3_.refs_2_, bf16[128,640]{1,0:T(8,128)(2,1)S(1)} %shard_map.164.refs_3_, ...), custom_call_target="tpu_custom_call" | custom-call | tf_op jit(solution)/shard_map/pallas_call | solution.py:92
  (21 shorter events, 0.1 us)
Async XLA Ops:
  2.4 17.1 %collective-permute-start.1 = (bf16[272,640]{1,0:T(8,128)(2,1)S(1)}, bf16[272,640]{1,0:T(8,128)(2,1)S(1)}, u32[]{:S(2)}, u32[]{:S(2)}) collective-permute-start(bf16[272,640]{1,0:T(8,128)(2,1)S(1)} %get-tuple-element.31.refs_10_.refs_5_), channel_id=1, source_target_pairs={{2,0},{4,2},{6,4},{8,6},{10,8},{12,10},{14,12},{0,14},{3,1},{5,3},... | collective-permute-start | bytes 1044488 | tf_op jit(solution)/shard_map/ppermute | solution.py:434
  8.3 11.4 %collective-permute-start = (bf16[272,640]{1,0:T(8,128)(2,1)S(1)}, bf16[272,640]{1,0:T(8,128)(2,1)S(1)}, u32[]{:S(2)}, u32[]{:S(2)}) collective-permute-start(bf16[272,640]{1,0:T(8,128)(2,1)S(1)} %get-tuple-element.31.refs_10_.refs_5_), channel_id=1, source_target_pairs={{0,2},{2,4},{4,6},{6,8},{8,10},{10,12},{12,14},{14,0},{1,3},{3,5},... | collective-permute-start | bytes 1044488 | tf_op jit(solution)/shard_map/ppermute | solution.py:433
  8.3 11.1 %collective-permute-start.3 = (f32[8,128]{1,0:T(8,128)S(1)}, f32[8,128]{1,0:T(8,128)S(1)}, u32[]{:S(2)}, u32[]{:S(2)}) collective-permute-start(f32[8,128]{1,0:T(8,128)S(1)} %get-tuple-element.36), channel_id=1, source_target_pairs={{0,8},{2,10},{4,12},{6,14},{8,0},{10,2},{12,4},{14,6},{1,9},{3,11}... | collective-permute-start | bytes 12296 | tf_op jit(solution)/shard_map/ppermute | solution.py:438
  19.4 5.6 %collective-permute-start.4 = (bf16[144,640]{1,0:T(8,128)(2,1)S(1)}, bf16[144,640]{1,0:T(8,128)(2,1)S(1)}, u32[]{:S(2)}, u32[]{:S(2)}) collective-permute-start(bf16[144,640]{1,0:T(8,128)(2,1)S(1)} %shard_map.144), channel_id=1, source_target_pairs={{2,0},{4,2},{6,4},{8,6},{10,8},{12,10},{14,12},{0,14},{3,1},{5,3},... | collective-permute-start | bytes 552968 | tf_op jit(solution)/shard_map/ppermute | solution.py:434
  19.7 6.8 %collective-permute-start.2 = (bf16[144,640]{1,0:T(8,128)(2,1)S(1)}, bf16[144,640]{1,0:T(8,128)(2,1)S(1)}, u32[]{:S(2)}, u32[]{:S(2)}) collective-permute-start(bf16[144,640]{1,0:T(8,128)(2,1)S(1)} %shard_map.142.refs_4_), channel_id=1, source_target_pairs={{0,2},{2,4},{4,6},{6,8},{8,10},{10,12},{12,14},{14,0},{1,3},{3,5},... | collective-permute-start | bytes 552968 | tf_op jit(solution)/shard_map/ppermute | solution.py:433
  26.5 6.7 %collective-permute-start.5 = (bf16[144,640]{1,0:T(8,128)(2,1)S(1)}, bf16[144,640]{1,0:T(8,128)(2,1)S(1)}, u32[]{:S(2)}, u32[]{:S(2)}) collective-permute-start(bf16[144,640]{1,0:T(8,128)(2,1)S(1)} %get-tuple-element.38.refs_0_.refs_3_.refs_8_), channel_id=1, source_target_pairs={{0,2},{2,4},{4,6},{6,8},{8,10},{10,12},{12,14},{14,0},{1,3},{3,5},... | collective-permute-start | bytes 552968 | tf_op jit(solution)/shard_map/ppermute | solution.py:433
  27.3 5.9 %collective-permute-start.6 = (bf16[144,640]{1,0:T(8,128)(2,1)S(1)}, bf16[144,640]{1,0:T(8,128)(2,1)S(1)}, u32[]{:S(2)}, u32[]{:S(2)}) collective-permute-start(bf16[144,640]{1,0:T(8,128)(2,1)S(1)} %get-tuple-element.39.refs_1_.refs_9_), channel_id=1, source_target_pairs={{2,0},{4,2},{6,4},{8,6},{10,8},{12,10},{14,12},{0,14},{3,1},{5,3},... | collective-permute-start | bytes 552968 | tf_op jit(solution)/shard_map/ppermute | solution.py:434
  33.3 7.9 %collective-permute-start.7 = (bf16[144,640]{1,0:T(8,128)(2,1)S(1)}, bf16[144,640]{1,0:T(8,128)(2,1)S(1)}, u32[]{:S(2)}, u32[]{:S(2)}) collective-permute-start(bf16[144,640]{1,0:T(8,128)(2,1)S(1)} %get-tuple-element.40.refs_10_.refs_0_.refs_3_), channel_id=1, source_target_pairs={{0,2},{2,4},{4,6},{6,8},{8,10},{10,12},{12,14},{14,0},{1,3},{3,5},... | collective-permute-start | bytes 552968 | tf_op jit(solution)/shard_map/ppermute | solution.py:433
  34.7 12.6 %collective-permute-start.10 = (bf16[128,640]{1,0:T(8,128)(2,1)S(1)}, bf16[128,640]{1,0:T(8,128)(2,1)S(1)}, u32[]{:S(2)}, u32[]{:S(2)}) collective-permute-start(bf16[128,640]{1,0:T(8,128)(2,1)S(1)} %get-tuple-element.44.refs_5_), channel_id=1, source_target_pairs={{2,0},{4,2},{6,4},{8,6},{10,8},{12,10},{14,12},{0,14},{3,1},{5,3},... | collective-permute-start | bytes 491528 | tf_op jit(solution)/shard_map/ppermute | solution.py:434
  37.9 9.4 %collective-permute-start.9 = (bf16[128,640]{1,0:T(8,128)(2,1)S(1)}, bf16[128,640]{1,0:T(8,128)(2,1)S(1)}, u32[]{:S(2)}, u32[]{:S(2)}) collective-permute-start(bf16[128,640]{1,0:T(8,128)(2,1)S(1)} %get-tuple-element.44.refs_5_), channel_id=1, source_target_pairs={{0,2},{2,4},{4,6},{6,8},{8,10},{10,12},{12,14},{14,0},{1,3},{3,5},... | collective-permute-start | bytes 491528 | tf_op jit(solution)/shard_map/ppermute | solution.py:433
  44.0 9.3 %collective-permute-start.8 = (bf16[128,640]{1,0:T(8,128)(2,1)S(1)}, bf16[128,640]{1,0:T(8,128)(2,1)S(1)}, u32[]{:S(2)}, u32[]{:S(2)}) collective-permute-start(bf16[128,640]{1,0:T(8,128)(2,1)S(1)} %shard_map.151.refs_2_.refs_3_), channel_id=1, source_target_pairs={{0,1},{1,0},{2,3},{3,2},{4,5},{5,4},{6,7},{7,6},{8,9},{9,8},{10,11... | collective-permute-start | bytes 491528 | tf_op jit(solution)/shard_map/ppermute | solution.py:528
  47.3 7.4 %collective-permute-start.11 = (bf16[128,640]{1,0:T(8,128)(2,1)S(1)}, bf16[128,640]{1,0:T(8,128)(2,1)S(1)}, u32[]{:S(2)}, u32[]{:S(2)}) collective-permute-start(bf16[128,640]{1,0:T(8,128)(2,1)S(1)} %get-tuple-element.46.refs_0_), channel_id=1, source_target_pairs={{0,2},{2,4},{4,6},{6,8},{8,10},{10,12},{12,14},{14,0},{1,3},{3,5},... | collective-permute-start | bytes 491528 | tf_op jit(solution)/shard_map/ppermute | solution.py:433
  47.3 7.4 %collective-permute-start.12 = (bf16[128,640]{1,0:T(8,128)(2,1)S(1)}, bf16[128,640]{1,0:T(8,128)(2,1)S(1)}, u32[]{:S(2)}, u32[]{:S(2)}) collective-permute-start(bf16[128,640]{1,0:T(8,128)(2,1)S(1)} %get-tuple-element.47.refs_1_), channel_id=1, source_target_pairs={{2,0},{4,2},{6,4},{8,6},{10,8},{12,10},{14,12},{0,14},{3,1},{5,3},... | collective-permute-start | bytes 491528 | tf_op jit(solution)/shard_map/ppermute | solution.py:434
  51.2 6.0 %collective-permute-start.16 = (bf16[160,640]{1,0:T(8,128)(2,1)S(1)}, bf16[160,640]{1,0:T(8,128)(2,1)S(1)}, u32[]{:S(2)}, u32[]{:S(2)}) collective-permute-start(bf16[160,640]{1,0:T(8,128)(2,1)S(1)} %shard_map.156), channel_id=1, source_target_pairs={{2,0},{4,2},{6,4},{8,6},{10,8},{12,10},{14,12},{0,14},{3,1},{5,3},... | collective-permute-start | bytes 614408 | tf_op jit(solution)/shard_map/ppermute | solution.py:434
  51.3 7.0 %collective-permute-start.15 = (bf16[160,640]{1,0:T(8,128)(2,1)S(1)}, bf16[160,640]{1,0:T(8,128)(2,1)S(1)}, u32[]{:S(2)}, u32[]{:S(2)}) collective-permute-start(bf16[160,640]{1,0:T(8,128)(2,1)S(1)} %shard_map.156), channel_id=1, source_target_pairs={{0,2},{2,4},{4,6},{6,8},{8,10},{10,12},{12,14},{14,0},{1,3},{3,5},... | collective-permute-start | bytes 614408 | tf_op jit(solution)/shard_map/ppermute | solution.py:433
  54.7 6.0 %collective-permute-start.14 = (bf16[144,640]{1,0:T(8,128)(2,1)S(1)}, bf16[144,640]{1,0:T(8,128)(2,1)S(1)}, u32[]{:S(2)}, u32[]{:S(2)}) collective-permute-start(bf16[144,640]{1,0:T(8,128)(2,1)S(1)} %get-tuple-element.51), channel_id=1, source_target_pairs={{2,0},{4,2},{6,4},{8,6},{10,8},{12,10},{14,12},{0,14},{3,1},{5,3},... | collective-permute-start | bytes 552968 | tf_op jit(solution)/shard_map/ppermute | solution.py:434
  57.2 6.8 %collective-permute-start.13 = (bf16[144,640]{1,0:T(8,128)(2,1)S(1)}, bf16[144,640]{1,0:T(8,128)(2,1)S(1)}, u32[]{:S(2)}, u32[]{:S(2)}) collective-permute-start(bf16[144,640]{1,0:T(8,128)(2,1)S(1)} %get-tuple-element.50.refs_4_), channel_id=1, source_target_pairs={{0,2},{2,4},{4,6},{6,8},{8,10},{10,12},{12,14},{14,0},{1,3},{3,5},... | collective-permute-start | bytes 552968 | tf_op jit(solution)/shard_map/ppermute | solution.py:433
  64.1 6.8 %collective-permute-start.19 = (bf16[144,640]{1,0:T(8,128)(2,1)S(1)}, bf16[144,640]{1,0:T(8,128)(2,1)S(1)}, u32[]{:S(2)}, u32[]{:S(2)}) collective-permute-start(bf16[144,640]{1,0:T(8,128)(2,1)S(1)} %get-tuple-element.55.refs_0_.refs_3_), channel_id=1, source_target_pairs={{0,2},{2,4},{4,6},{6,8},{8,10},{10,12},{12,14},{14,0},{1,3},{3,5},... | collective-permute-start | bytes 552968 | tf_op jit(solution)/shard_map/ppermute | solution.py:433
  64.1 7.2 %collective-permute-start.18 = (f32[8,128]{1,0:T(8,128)S(1)}, f32[8,128]{1,0:T(8,128)S(1)}, u32[]{:S(2)}, u32[]{:S(2)}) collective-permute-start(f32[8,128]{1,0:T(8,128)S(1)} %get-tuple-element.54), channel_id=1, source_target_pairs={{0,10},{2,12},{4,14},{6,0},{8,2},{10,4},{12,6},{14,8},{1,11},{3,13... | collective-permute-start | bytes 12296 | tf_op jit(solution)/shard_map/ppermute | solution.py:438
  65.5 6.6 %collective-permute-start.17 = (f32[8,128]{1,0:T(8,128)S(1)}, f32[8,128]{1,0:T(8,128)S(1)}, u32[]{:S(2)}, u32[]{:S(2)}) collective-permute-start(f32[8,128]{1,0:T(8,128)S(1)} %get-tuple-element.53.refs_2_.refs_0_), channel_id=1, source_target_pairs={{0,6},{2,8},{4,10},{6,12},{8,14},{10,0},{12,2},{14,4},{1,7},{3,9},... | collective-permute-start | bytes 12296 | tf_op jit(solution)/shard_map/ppermute | solution.py:438
  75.9 6.9 %collective-permute-start.20 = (bf16[128,640]{1,0:T(8,128)(2,1)S(1)}, bf16[128,640]{1,0:T(8,128)(2,1)S(1)}, u32[]{:S(2)}, u32[]{:S(2)}) collective-permute-start(bf16[128,640]{1,0:T(8,128)(2,1)S(1)} %shard_map.164.refs_3_), channel_id=1, source_target_pairs={{0,1},{1,0},{2,3},{3,2},{4,5},{5,4},{6,7},{7,6},{8,9},{9,8},{10,11... | collective-permute-start | bytes 491528 | tf_op jit(solution)/shard_map/ppermute | solution.py:528
